TPU v7x, 32 devices: a whole 2x2x4 slice. The times are simulated.
32 devices in a mesh: blk: 8 (over y, x, core), head: 4 (over z).
Axes of the slice: x: 2, y: 2, z: 4, core: 2. Of those that a mesh axis runs over, the one named last changes fastest.
Arguments:
- layer_input: bfloat16 [2, 8, 2, 256, 2048], P(None, 'blk', None, 'head'), may hold values from -6 to 6
- block_order: int32 [8], replicated, may hold values from 0 to 7, each once
- first_gain: bfloat16 [2048], P(('blk', 'head')), may hold values from 0.5 to 1.5
- first_shift: bfloat16 [2048], P(('blk', 'head')), may hold values from -1.5 to 1.5
- query_weight: bfloat16 [2048, 2048], P('blk', 'head'), may hold values from -0.125 to 0.125
- key_weight: bfloat16 [2048, 2048], P('blk', 'head'), may hold values from -0.125 to 0.125
- value_weight: bfloat16 [2048, 2048], P('blk', 'head'), may hold values from -0.125 to 0.125
- query_bias: bfloat16 [32, 64], P('head', 'blk'), may hold values from -2.5 to 2.5
- key_bias: bfloat16 [32, 16], P('head', 'blk'), may hold values from -2.5 to 2.5
- value_bias: bfloat16 [32, 64], P('head', 'blk'), may hold values from -2.5 to 2.5
- out_weight: bfloat16 [2048, 2048], P('head', 'blk'), may hold values from -1 to 1
- second_gain: bfloat16 [2048], P(('blk', 'head')), may hold values from 0.5 to 1.5
- second_shift: bfloat16 [2048], P(('blk', 'head')), may hold values from -1.5 to 1.5
- gate_weight: bfloat16 [2048, 5632], P('blk', 'head'), may hold values from -0.125 to 0.125
- up_weight: bfloat16 [2048, 5632], P('blk', 'head'), may hold values from -0.125 to 0.125
- down_weight: bfloat16 [5632, 2048], P('head', 'blk'), may hold values from -0.3125 to 0.3125
- out_grad: bfloat16 [2, 8, 2, 256, 2048], P(None, 'blk', None, 'head'), may hold values from -6 to 6
Outputs:
- layer_output: float32 [2, 8, 2, 256, 2048], P(None, 'blk', None, 'head')
- input_grad: float32 [2, 8, 2, 256, 2048], P(None, 'blk', None, 'head')
- first_gain_grad: float32 [2048], P(('blk', 'head'))
- first_shift_grad: float32 [2048], P(('blk', 'head'))
- query_weight_grad: float32 [2048, 2048], P('blk', 'head')
- key_weight_grad: float32 [2048, 2048], P('blk', 'head')
- value_weight_grad: float32 [2048, 2048], P('blk', 'head')
- query_bias_grad: float32 [32, 64], P('head', 'blk')
- key_bias_grad: float32 [32, 16], P('head', 'blk')
- value_bias_grad: float32 [32, 64], P('head', 'blk')
- out_weight_grad: float32 [2048, 2048], P('head', 'blk')
- second_gain_grad: float32 [2048], P(('blk', 'head'))
- second_shift_grad: float32 [2048], P(('blk', 'head'))
- gate_weight_grad: float32 [2048, 5632], P('blk', 'head')
- up_weight_grad: float32 [2048, 5632], P('blk', 'head')
- down_weight_grad: float32 [5632, 2048], P('head', 'blk')
Inputs may be any that keep to these rules, and one draw needn't show every extreme that they name: A permutation: device b of blk holds blocks block_order[b] and 15 - block_order[b] of every sequence.
All inputs are finite; a program needn't handle non-finite values.
Results may differ from a plain program's by a relative error of at most 0.033.
Values may be sent and summed in bfloat16 or wider, within the bound.
No kernel may reach another device: no remote copies, remote signals or barrier semaphores. Data moves between devices by JAX's collectives and lax.ppermute only.
A program may use at most 192 MiB of HBM per device.

v0:
```python
import math

import jax
import jax.numpy as jnp
from jax import lax
from jax.sharding import PartitionSpec as P

HD = 64
ROT = 16


epsilon = 1e-05
masked_value = -1e30
rotary_base = 10000.0


def shifted(value, axis, steps):
    count = lax.axis_size(axis)
    pairs = [(source, (source + steps) % count) for source in range(count)]
    return lax.ppermute(value, axis, pairs)


def normalize(value, gain, shift):
    center = value - jnp.mean(value, axis=-1, keepdims=True)
    inverse = lax.rsqrt(jnp.mean(center * center, axis=-1, keepdims=True) + epsilon)
    return center * inverse * gain + shift


def norm_back(value, gain, upstream):
    center = value - jnp.mean(value, axis=-1, keepdims=True)
    inverse = lax.rsqrt(jnp.mean(center * center, axis=-1, keepdims=True) + epsilon)
    normed = center * inverse
    scaled = upstream * gain
    back = inverse * (
        scaled
        - jnp.mean(scaled, axis=-1, keepdims=True)
        - normed * jnp.mean(scaled * normed, axis=-1, keepdims=True)
    )
    return (back, jnp.sum(upstream * normed, axis=0), jnp.sum(upstream, axis=0))


def rotary_tables(positions):
    frequency = jnp.exp(
        jnp.arange(ROT // 2, dtype=jnp.float32) * (-2.0 * math.log(rotary_base) / ROT)
    )
    phase_angle = positions.astype(jnp.float32)[:, None] * frequency[None, :]
    return (jnp.cos(phase_angle), jnp.sin(phase_angle))


def rotate(value, cosine, sine):
    half = ROT // 2
    first = value[..., :half]
    second = value[..., half:ROT]
    cosine = cosine[:, None, :]
    sine = sine[:, None, :]
    return jnp.concatenate(
        [first * cosine - second * sine, second * cosine + first * sine, value[..., ROT:]], axis=-1
    )


def to_seq(value, head_size, seqs):
    columns = value.shape[-1]
    value = value.reshape(head_size, seqs, -1, columns)
    return jnp.swapaxes(value, 0, 1).reshape(seqs, -1, columns)


def from_seq(value, head_size):
    seqs = value.shape[0]
    columns = value.shape[-1]
    value = value.reshape(seqs, head_size, -1, columns)
    return jnp.swapaxes(value, 0, 1).reshape(-1, columns)


def scored(query_heads, key_heads, query_pos, key_pos):
    factor = query_heads.shape[-1] ** (-0.5)
    raw_scores = (
        jnp.einsum("sqhd,skhd->shqk", query_heads, key_heads, preferred_element_type=jnp.float32)
        * factor
    )
    allowed = key_pos[None, :] <= query_pos[:, None]
    return (jnp.where(allowed, raw_scores, masked_value), allowed)


def pair_grads(
    query_heads, key_heads, value_heads, grad_heads, log_total, delta, query_pos, key_pos
):
    factor = query_heads.shape[-1] ** (-0.5)
    scores, allowed = scored(query_heads, key_heads, query_pos, key_pos)
    weights_now = jnp.where(allowed, jnp.exp(scores - log_total[..., None]), 0.0)
    grad_weights = jnp.einsum(
        "sqhd,skhd->shqk", grad_heads, value_heads, preferred_element_type=jnp.float32
    )
    grad_scores = (weights_now * (grad_weights - delta[..., None])).astype(jnp.bfloat16)
    query_part = (
        jnp.einsum("shqk,skhd->sqhd", grad_scores, key_heads, preferred_element_type=jnp.float32)
        * factor
    )
    key_part = (
        jnp.einsum("shqk,sqhd->skhd", grad_scores, query_heads, preferred_element_type=jnp.float32)
        * factor
    )
    value_part = jnp.einsum(
        "shqk,sqhd->skhd",
        weights_now.astype(jnp.bfloat16),
        grad_heads,
        preferred_element_type=jnp.float32,
    )
    return (query_part, key_part, value_part)


def rotate_state(moving_data, moving_sums):
    data_next = shifted((moving_data[0], moving_data[1]), "blk", 1)
    sums_next = (
        shifted(moving_sums[0].astype(jnp.bfloat16), "blk", 1).astype(jnp.float32),
        shifted(moving_sums[1].astype(jnp.bfloat16), "blk", 1).astype(jnp.float32),
    )
    return (data_next, sums_next)


def local(
    layer_input,
    block_order,
    first_gain,
    first_shift,
    query_weight,
    key_weight,
    value_weight,
    query_bias,
    key_bias,
    value_bias,
    out_weight,
    second_gain,
    second_shift,
    gate_weight,
    up_weight,
    down_weight,
    out_grad,
):
    seqs = layer_input.shape[0]
    part_rows = layer_input.shape[3]
    width = layer_input.shape[4]
    cycle_size = lax.axis_size("blk")
    head_size = lax.axis_size("head")
    cycle_index = lax.axis_index("blk")
    block_len = part_rows * head_size
    local_heads = query_bias.shape[0]
    local_width = local_heads * HD
    f32 = jnp.float32
    bf16 = jnp.bfloat16
    gains = (
        lax.all_gather(first_gain, ("blk", "head"), axis=0, tiled=True),
        lax.all_gather(first_shift, ("blk", "head"), axis=0, tiled=True),
        lax.all_gather(second_gain, ("blk", "head"), axis=0, tiled=True),
        lax.all_gather(second_shift, ("blk", "head"), axis=0, tiled=True),
    )
    gain_one, shift_one, gain_two, shift_two = [member.astype(f32) for member in gains]
    (
        full_query,
        full_key,
        full_value,
        full_out,
        full_gate,
        full_up,
        full_down,
        bias_query,
        bias_key,
        bias_value,
    ) = (
        lax.all_gather(query_weight, "blk", axis=0, tiled=True),
        lax.all_gather(key_weight, "blk", axis=0, tiled=True),
        lax.all_gather(value_weight, "blk", axis=0, tiled=True),
        lax.all_gather(out_weight, "blk", axis=1, tiled=True),
        lax.all_gather(gate_weight, "blk", axis=0, tiled=True),
        lax.all_gather(up_weight, "blk", axis=0, tiled=True),
        lax.all_gather(down_weight, "blk", axis=1, tiled=True),
        lax.all_gather(query_bias, "blk", axis=1, tiled=True),
        lax.all_gather(key_bias, "blk", axis=1, tiled=True),
        lax.all_gather(value_bias, "blk", axis=1, tiled=True),
    )
    padded_key_bias = jnp.pad(bias_key, ((0, 0), (0, HD - ROT)))

    def positions(owner):
        first_id = lax.dynamic_index_in_dim(block_order, owner, 0, keepdims=False)
        halves = jnp.arange(2, dtype=jnp.int32)[None, :, None]
        starts = jnp.where(halves == 0, first_id, 2 * cycle_size - 1 - first_id) * block_len
        offsets = jnp.arange(head_size, dtype=jnp.int32)[:, None, None] * part_rows
        inner = jnp.arange(part_rows, dtype=jnp.int32)[None, None, :]
        return (starts + offsets + inner).reshape(-1)

    own_pos = positions(cycle_index)
    cosine, sine = rotary_tables(own_pos)
    four_shape = (seqs, 2 * block_len, local_heads, HD)
    flat_shape = (seqs, 2 * block_len, local_width)
    rows_in = layer_input.reshape(-1, width).astype(f32)
    row_count = rows_in.shape[0]
    normed_one = normalize(rows_in, gain_one, shift_one).astype(bf16)
    rows_one, grad_rows_two = (
        lax.all_gather(normed_one[None], "head", axis=0, tiled=True),
        lax.all_gather(out_grad.reshape(1, row_count, width), "head", axis=0, tiled=True),
    )
    rows_one = rows_one.reshape(-1, width)
    grad_rows_two = grad_rows_two.reshape(-1, width)

    def project(weight, bias):
        result = jnp.dot(rows_one, weight, preferred_element_type=f32) + bias.reshape(-1).astype(
            f32
        )
        return to_seq(result, head_size, seqs).reshape(four_shape)

    query_heads = rotate(project(full_query, bias_query), cosine, sine).astype(bf16)
    key_heads = rotate(project(full_key, padded_key_bias), cosine, sine).astype(bf16)
    value_heads = project(full_value, bias_value).astype(bf16)
    stat_shape = (seqs, local_heads, 2 * block_len)
    initial = (jnp.full(stat_shape, masked_value, f32), jnp.zeros(stat_shape, f32))
    state = initial
    pieces = lax.all_gather(key_heads.reshape((1,) + flat_shape), "blk", axis=0, tiled=True)

    def totals_visit(carry, member):
        key_block, owner = member
        scores, allowed = scored(
            query_heads, key_block.reshape(four_shape), own_pos, positions(owner)
        )
        peak = jnp.maximum(carry[0], jnp.max(scores, axis=-1))
        weights_now = jnp.where(allowed, jnp.exp(scores - peak[..., None]), 0.0)
        total = carry[1] * jnp.exp(carry[0] - peak) + jnp.sum(weights_now, axis=-1)
        return ((peak, total), None)

    owners = jnp.arange(pieces.shape[0], dtype=jnp.int32)
    state, unused = lax.scan(totals_visit, state, (pieces, owners))
    running_max, total = state
    log_total = running_max + jnp.log(total)
    state = (jnp.zeros(four_shape, f32), jnp.zeros(four_shape, f32))
    pieces = (
        lax.all_gather(key_heads.reshape((1,) + flat_shape), "blk", axis=0, tiled=True),
        lax.all_gather(value_heads.reshape((1,) + flat_shape), "blk", axis=0, tiled=True),
    )

    def attend_visit(carry, member):
        key_block, value_block, owner = member
        scores, allowed = scored(
            query_heads, key_block.reshape(four_shape), own_pos, positions(owner)
        )
        weights_now = jnp.where(allowed, jnp.exp(scores - log_total[..., None]), 0.0)
        values_here = value_block.reshape(four_shape)
        rounded = jnp.einsum(
            "shqk,skhd->sqhd", weights_now.astype(bf16), values_here, preferred_element_type=f32
        )
        exact = jnp.einsum(
            "shqk,skhd->sqhd", weights_now, values_here.astype(f32), preferred_element_type=f32
        )
        return ((carry[0] + rounded, carry[1] + exact), None)

    owners = jnp.arange(pieces[0].shape[0], dtype=jnp.int32)
    state, unused = lax.scan(attend_visit, state, (pieces[0], pieces[1], owners))
    attended, attended_exact = state
    out_rows = from_seq(attended.astype(bf16).reshape(flat_shape), head_size)
    middle = rows_in + lax.psum_scatter(
        jnp.dot(out_rows, full_out, preferred_element_type=f32).astype(jnp.bfloat16),
        "head",
        scatter_dimension=0,
        tiled=True,
    ).astype(jnp.float32)
    normed_two = normalize(middle, gain_two, shift_two).astype(bf16)
    rows_two = lax.all_gather(normed_two[None], "head", axis=0, tiled=True).reshape(-1, width)
    gate = jnp.dot(rows_two, full_gate, preferred_element_type=f32)
    up_value = jnp.dot(rows_two, full_up, preferred_element_type=f32)
    sigmoid_gate = jax.nn.sigmoid(gate)
    silu_gate = gate * sigmoid_gate
    hidden = (silu_gate * up_value).astype(bf16)
    result = middle + lax.psum_scatter(
        jnp.dot(hidden, full_down, preferred_element_type=f32).astype(jnp.bfloat16),
        "head",
        scatter_dimension=0,
        tiled=True,
    ).astype(jnp.float32)
    layer_output = result.reshape(layer_input.shape)
    grad_out = out_grad.reshape(row_count, width).astype(f32)
    grad_hidden = jnp.dot(grad_rows_two, full_down.T, preferred_element_type=f32)
    down_grad = jnp.dot(hidden.T, grad_rows_two, preferred_element_type=f32)
    grad_up = (grad_hidden * silu_gate).astype(bf16)
    grad_gate = (
        grad_hidden * up_value * sigmoid_gate * (1.0 + gate * (1.0 - sigmoid_gate))
    ).astype(bf16)
    gate_grad = jnp.dot(rows_two.T, grad_gate, preferred_element_type=f32)
    up_grad = jnp.dot(rows_two.T, grad_up, preferred_element_type=f32)
    part = jnp.dot(grad_gate, full_gate.T, preferred_element_type=f32)
    grad_normed_two = lax.psum_scatter(
        (part + jnp.dot(grad_up, full_up.T, preferred_element_type=f32)).astype(jnp.bfloat16),
        "head",
        scatter_dimension=0,
        tiled=True,
    ).astype(jnp.float32)
    back_two, gain_two_grad, shift_two_grad = norm_back(middle, gain_two, grad_normed_two)
    grad_middle = grad_out + back_two
    grad_rows_one = lax.all_gather(
        grad_middle.astype(bf16)[None], "head", axis=0, tiled=True
    ).reshape(-1, width)
    out_grad_weight = jnp.dot(out_rows.T, grad_rows_one, preferred_element_type=f32)
    grad_attended = jnp.dot(grad_rows_one, full_out.T, preferred_element_type=f32).astype(bf16)
    grad_heads = to_seq(grad_attended, head_size, seqs).reshape(four_shape)
    delta = jnp.swapaxes(jnp.sum(grad_heads.astype(f32) * attended_exact, axis=-1), 1, 2)

    def turn_keys(turn_index, carry):
        moving_data, moving_sums, query_acc = carry
        key_now, value_now = moving_data
        key_acc, value_acc = moving_sums
        owner = (cycle_index - turn_index) % cycle_size
        query_part, key_part, value_part = pair_grads(
            query_heads,
            key_now.reshape(four_shape),
            value_now.reshape(four_shape),
            grad_heads,
            log_total,
            delta,
            own_pos,
            positions(owner),
        )
        moving_data, moving_sums = rotate_state(
            (key_now, value_now),
            (key_acc + key_part.reshape(flat_shape), value_acc + value_part.reshape(flat_shape)),
        )
        return (moving_data, moving_sums, query_acc + query_part)

    start_state = (
        (key_heads.reshape(flat_shape), value_heads.reshape(flat_shape)),
        (jnp.zeros(flat_shape, f32), jnp.zeros(flat_shape, f32)),
        jnp.zeros(four_shape, f32),
    )
    moved_data, moved_sums, query_grad = lax.fori_loop(0, cycle_size, turn_keys, start_state)
    key_grad = moved_sums[0].reshape(four_shape)
    value_grad = moved_sums[1].reshape(four_shape)
    query_rows = from_seq(
        rotate(query_grad, cosine, -sine).astype(bf16).reshape(flat_shape), head_size
    )
    key_rows = from_seq(rotate(key_grad, cosine, -sine).astype(bf16).reshape(flat_shape), head_size)
    value_rows = from_seq(value_grad.astype(bf16).reshape(flat_shape), head_size)
    query_bias_part = jnp.sum(query_rows, axis=0, dtype=f32).reshape(local_heads, HD)
    key_bias_part = jnp.sum(key_rows, axis=0, dtype=f32).reshape(local_heads, HD)[:, :ROT]
    value_bias_part = jnp.sum(value_rows, axis=0, dtype=f32).reshape(local_heads, HD)
    query_grad_weight = jnp.dot(rows_one.T, query_rows, preferred_element_type=f32)
    key_grad_weight = jnp.dot(rows_one.T, key_rows, preferred_element_type=f32)
    value_grad_weight = jnp.dot(rows_one.T, value_rows, preferred_element_type=f32)
    part = jnp.dot(query_rows, full_query.T, preferred_element_type=f32)
    part = part + jnp.dot(key_rows, full_key.T, preferred_element_type=f32)
    grad_normed_one = lax.psum_scatter(
        (part + jnp.dot(value_rows, full_value.T, preferred_element_type=f32)).astype(jnp.bfloat16),
        "head",
        scatter_dimension=0,
        tiled=True,
    ).astype(jnp.float32)
    back_one, gain_one_grad, shift_one_grad = norm_back(rows_in, gain_one, grad_normed_one)
    input_grad = (grad_middle + back_one).reshape(layer_input.shape)
    summed = (
        lax.psum_scatter(
            query_grad_weight.astype(jnp.bfloat16), "blk", scatter_dimension=0, tiled=True
        ).astype(jnp.float32),
        lax.psum_scatter(
            key_grad_weight.astype(jnp.bfloat16), "blk", scatter_dimension=0, tiled=True
        ).astype(jnp.float32),
        lax.psum_scatter(
            value_grad_weight.astype(jnp.bfloat16), "blk", scatter_dimension=0, tiled=True
        ).astype(jnp.float32),
        lax.psum_scatter(
            out_grad_weight.astype(jnp.bfloat16), "blk", scatter_dimension=1, tiled=True
        ).astype(jnp.float32),
        lax.psum_scatter(
            gate_grad.astype(jnp.bfloat16), "blk", scatter_dimension=0, tiled=True
        ).astype(jnp.float32),
        lax.psum_scatter(
            up_grad.astype(jnp.bfloat16), "blk", scatter_dimension=0, tiled=True
        ).astype(jnp.float32),
        lax.psum_scatter(
            down_grad.astype(jnp.bfloat16), "blk", scatter_dimension=1, tiled=True
        ).astype(jnp.float32),
        lax.psum_scatter(
            query_bias_part.astype(jnp.bfloat16), "blk", scatter_dimension=1, tiled=True
        ).astype(jnp.float32),
        lax.psum_scatter(
            key_bias_part.astype(jnp.bfloat16), "blk", scatter_dimension=1, tiled=True
        ).astype(jnp.float32),
        lax.psum_scatter(
            value_bias_part.astype(jnp.bfloat16), "blk", scatter_dimension=1, tiled=True
        ).astype(jnp.float32),
    )
    norm_summed = (
        lax.psum_scatter(gain_one_grad, ("blk", "head"), scatter_dimension=0, tiled=True),
        lax.psum_scatter(shift_one_grad, ("blk", "head"), scatter_dimension=0, tiled=True),
        lax.psum_scatter(gain_two_grad, ("blk", "head"), scatter_dimension=0, tiled=True),
        lax.psum_scatter(shift_two_grad, ("blk", "head"), scatter_dimension=0, tiled=True),
    )
    return (
        layer_output,
        input_grad,
        norm_summed[0],
        norm_summed[1],
        summed[0],
        summed[1],
        summed[2],
        summed[7],
        summed[8],
        summed[9],
        summed[3],
        norm_summed[2],
        norm_summed[3],
        summed[4],
        summed[5],
        summed[6],
    )


def solution(mesh):
    return jax.shard_map(
        local,
        mesh=mesh,
        in_specs=(
            P(None, "blk", None, "head", None),
            P(),
            P(("blk", "head")),
            P(("blk", "head")),
            P("blk", "head"),
            P("blk", "head"),
            P("blk", "head"),
            P("head", "blk"),
            P("head", "blk"),
            P("head", "blk"),
            P("head", "blk"),
            P(("blk", "head")),
            P(("blk", "head")),
            P("blk", "head"),
            P("blk", "head"),
            P("head", "blk"),
            P(None, "blk", None, "head", None),
        ),
        out_specs=(
            P(None, "blk", None, "head", None),
            P(None, "blk", None, "head", None),
            P(("blk", "head")),
            P(("blk", "head")),
            P("blk", "head"),
            P("blk", "head"),
            P("blk", "head"),
            P("head", "blk"),
            P("head", "blk"),
            P("head", "blk"),
            P("head", "blk"),
            P(("blk", "head")),
            P(("blk", "head")),
            P("blk", "head"),
            P("blk", "head"),
            P("head", "blk"),
        ),
        check_vma=False,
    )
```

profile of v0, /device:TPU:0, one launch (start us, length us, event | category | flops | bytes accessed | tf_op | source)
XLA Modules:
  0.0 2329.9 jit_solution(2785217351933102324)
XLA Ops:
  11.4 42.3 %all-reduce.13 = (bf16[2048]{0:T(1024)(128)(2,1)}, bf16[2048]{0:T(1024)(128)(2,1)}, bf16[2048]{0:T(1024)(128)(2,1)S(1)}, bf16[2048]{0:T(1024)(128)(2,1)S(1)}) all-reduce(bf16[2048]{0:T(1024)(128)(2,1)S(1)} %dynamic-update-slice.3, bf16[2048]{0:T(1024)(128)(2,1)S(1)} %dynamic-update-slice.2, ...), channel_id=1, replica_groups=mesh['blk'=8,'head'=4] {'blk','head'}, use_global_device_ids=true, to_apply=%add.4 | all-reduce | flops 8192 | bytes 32768
  71.5 66.8 %all-gather.17.cloned.1.call-done = bf16[4,256,2048]{2,1,0:T(8,128)(2,1)} async-done(((bf16[1,256,2048]{2,1,0:T(8,128)(2,1)}), bf16[4,256,2048]{2,1,0:T(8,128)(2,1)}) %all-gather.17.cloned.1.call-update) | async-done | bytes 4194320 | tf_op jit(solution)/shard_map/all_gather | solution.py:198
  183.9 12.5 all-gather.27.cloned.1.call-done
  209.8 42.7 %all-gather.25.cloned.1.call-done = bf16[8,2,512,512]{3,2,1,0:T(8,128)(2,1)} async-done(((bf16[1,2,512,512]{3,2,1,0:T(8,128)(2,1)}), bf16[8,2,512,512]{3,2,1,0:T(8,128)(2,1)}) %all-gather.25.cloned.1.call-update) | async-done | bytes 8388624 | tf_op jit(solution)/shard_map/all_gather | solution.py:234
  252.5 12.4 copy.170
  264.9 173.9 %while.50 = (s32[]{:T(128)}, f32[2,8,512]{2,1,0:T(8,128)S(1)}, f32[2,8,512]{2,1,0:T(8,128)S(1)}, s32[8]{0:T(128)S(1)}, s32[8]{0:T(128)S(1)}, /*index=5*/bf16[8,2...) while((s32[]{:T(128)}, f32[2,8,512]{2,1,0:T(8,128)S(1)}, ...), condition=%wide.region_5.6_spmd.clone, body=%wide.region_2.5_spmd.clone.sunk | while | flops 570729472 | bytes 38977888 | solution.py:229
  438.8 293.5 %while.51 = (s32[]{:T(128)}, f32[2,512,8,64]{1,3,2,0:T(8,128)}, f32[2,512,8,64]{1,3,2,0:T(8,128)}, bf16[8,2,512,512]{3,2,1,0:T(8,128)(2,1)}, s32[8]{0:T(128)S(1)...) while((s32[]{:T(128)}, f32[2,512,8,64]{1,3,2,0:T(8,128)}, ...), condition=%wide.region_7.8_spmd.clone, body=%wide.region_6.7_spmd.clone.sunk | while | flops 1650721792 | bytes 70074736 | solution.py:254
  753.4 76.2 %reduce-scatter.14.cloned.1.call-done = bf16[256,2048]{1,0:T(8,128)(2,1)} async-done(((bf16[1024,2048]{1,0:T(8,128)(2,1)}), bf16[256,2048]{1,0:T(8,128)(2,1)}) %reduce-scatter.14.cloned.1.call-update) | async-done | bytes 1048592 | tf_op jit(solution)/shard_map/reduce_scatter | solution.py:257
  835.5 40.0 %all-gather.31.cloned.1.call-done = bf16[2048,1408]{1,0:T(8,128)(2,1)} async-done(((bf16[256,1408]{1,0:T(8,128)(2,1)}), bf16[2048,1408]{1,0:T(8,128)(2,1)}) %all-gather.31.cloned.1.call-update) | async-done | bytes 5767184 | tf_op jit(solution)/shard_map/all_gather | solution.py:173
  875.5 82.9 %all-gather.39.cloned.1.call-done = bf16[1024,2048]{1,0:T(8,128)(2,1)} async-done(((bf16[256,2048]{1,0:T(8,128)(2,1)}), bf16[1024,2048]{1,0:T(8,128)(2,1)}) %all-gather.39.cloned.1.call-update) | async-done | bytes 4194320 | tf_op jit(solution)/shard_map/all_gather | solution.py:264
  970.0 32.3 %all-gather.33.cloned.1.call-done = bf16[2048,1408]{1,0:T(8,128)(2,1)} async-done(((bf16[256,1408]{1,0:T(8,128)(2,1)}), bf16[2048,1408]{1,0:T(8,128)(2,1)}) %all-gather.33.cloned.1.call-update) | async-done | bytes 5767184 | tf_op jit(solution)/shard_map/all_gather | solution.py:174
  1014.0 70.6 %all-gather.37.cloned.1.call-done = bf16[4,256,2048]{2,1,0:T(8,128)(2,1)} async-done(((bf16[1,256,2048]{2,1,0:T(8,128)(2,1)}), bf16[4,256,2048]{2,1,0:T(8,128)(2,1)}) %all-gather.37.cloned.1.call-update) | async-done | bytes 4194320 | tf_op jit(solution)/shard_map/all_gather | solution.py:199
  1084.6 44.9 %all-gather.35.cloned.1.call-done = bf16[1408,2048]{1,0:T(8,128)(2,1)} async-done(((bf16[1408,256]{1,0:T(8,128)(2,1)}), bf16[1408,2048]{1,0:T(8,128)(2,1)}) %all-gather.35.cloned.1.call-update) | async-done | bytes 5767184 | tf_op jit(solution)/shard_map/all_gather | solution.py:175
  1129.6 15.6 multiply_convert_fusion.1
  1164.8 76.5 %reduce-scatter.18.cloned.1.call-done = bf16[256,2048]{1,0:T(8,128)(2,1)} async-done(((bf16[1024,2048]{1,0:T(8,128)(2,1)}), bf16[256,2048]{1,0:T(8,128)(2,1)}) %reduce-scatter.18.cloned.1.call-update) | async-done | bytes 1048592 | tf_op jit(solution)/shard_map/reduce_scatter | solution.py:287
  1282.6 45.4 %all-gather.41.cloned.1.call-done = bf16[1024,2048]{1,0:T(8,128)(2,1)} async-done(((bf16[256,2048]{1,0:T(8,128)(2,1)}), bf16[1024,2048]{1,0:T(8,128)(2,1)}) %all-gather.41.cloned.1.call-update) | async-done | bytes 4194320 | tf_op jit(solution)/shard_map/all_gather | solution.py:295
  1345.5 670.3 %while.52 = (s32[]{:T(128)}, bf16[2,512,512]{1,2,0:T(8,128)(2,1)S(1)}, bf16[2,512,512]{1,2,0:T(8,128)(2,1)}, f32[2,512,512]{1,2,0:T(8,128)}, f32[2,512,512]{1,2,...) while((s32[]{:T(128)}, ...), condition=%wide.region_17.18_spmd.clone, body=%wide.region_16.17_spmd.clone.sunk | while | flops 2741240832 | bytes 180208352 | solution.py:329
  1420.3 26.8 %collective-permute-done.1 = bf16[2,512,512]{1,2,0:T(8,128)(2,1)} collective-permute-done((bf16[2,512,512]{1,2,0:T(8,128)(2,1)}, bf16[2,512,512]{1,2,0:T(8,128)(2,1)}, u32[]{:S(2)}, u32[]{:S(2)}) %collective-permute-start.1) | collective-permute-done | bytes 1048608 | tf_op jit(solution)/shard_map/while/body/eval_jaxpr/ppermute | solution.py:20
  1501.4 17.2 collective-permute-done.3
  1521.5 16.0 collective-permute-done
  2114.7 43.3 %reduce-scatter.26.cloned.1.call-done = bf16[256,512]{1,0:T(8,128)(2,1)} async-done(((bf16[2048,512]{1,0:T(8,128)(2,1)}), bf16[256,512]{1,0:T(8,128)(2,1)}) %reduce-scatter.26.cloned.1.call-update) | async-done | bytes 262160 | tf_op jit(solution)/shard_map/reduce_scatter | solution.py:360
  2159.8 77.4 %reduce-scatter.20.cloned.1.call-done = bf16[256,2048]{1,0:T(8,128)(2,1)} async-done(((bf16[1024,2048]{1,0:T(8,128)(2,1)}), bf16[256,2048]{1,0:T(8,128)(2,1)}) %reduce-scatter.20.cloned.1.call-update) | async-done | bytes 1048592 | tf_op jit(solution)/shard_map/reduce_scatter | solution.py:345
  2239.5 46.1 %all-reduce.12 = (f32[2048]{0:T(1024)S(1)}, f32[2048]{0:T(1024)S(1)}, f32[2048]{0:T(1024)S(1)}, f32[2048]{0:T(1024)S(1)}) all-reduce(f32[2048]{0:T(1024)S(1)} %get-tuple-element.727, f32[2048]{0:T(1024)S(1)} %get-tuple-element.732, f32[2048]{0:T(1024)S(1)} %copy-done.31, ...), channel_id=8, replica_groups=mesh['blk'=8,'head'=4] {'blk','head'}, use_global_device_ids=true, to_apply=%region_22.23.clone | all-reduce | flops 8192 | bytes 65536
  2287.9 29.7 %reduce-scatter.16.cloned.1.call-done = bf16[256,2048]{1,0:T(8,128)(2,1)} async-done(((bf16[1024,2048]{1,0:T(8,128)(2,1)}), bf16[256,2048]{1,0:T(8,128)(2,1)}) %reduce-scatter.16.cloned.1.call-update) | async-done | bytes 1048592 | tf_op jit(solution)/shard_map/reduce_scatter | solution.py:270
  (817 shorter events, 1345.9 us)
Async XLA Ops:
  7.2 64.3 %all-gather.23.cloned.1.call-start = ((), (), s32[]{:S(2)}) async-start(), calls=%async_computation.14 | async-start | bytes 2359296 | tf_op jit(solution)/shard_map/all_gather | solution.py:170
  7.9 130.4 %all-gather.17.cloned.1.call-start = ((), (), s32[]{:S(2)}) async-start(), calls=%async_computation.11 | async-start | bytes 5242880 | tf_op jit(solution)/shard_map/all_gather | solution.py:198
  57.2 109.5 %all-gather.19.cloned.1.call-start = ((), (), s32[]{:S(2)}) async-start(), calls=%async_computation.12 | async-start | bytes 2359296 | tf_op jit(solution)/shard_map/all_gather | solution.py:171
  57.9 138.4 %all-gather.27.cloned.1.call-start = ((), (), s32[]{:S(2)}) async-start(), calls=%async_computation.16 | async-start | bytes 2359296 | tf_op jit(solution)/shard_map/all_gather | solution.py:169
  58.5 194.0 %all-gather.25.cloned.1.call-start = ((), (), s32[]{:S(2)}) async-start(), calls=%async_computation.15 | async-start | bytes 9437184 | tf_op jit(solution)/shard_map/all_gather | solution.py:234
  152.8 286.0 %all-gather.21.cloned.1.call-start = ((), (), s32[]{:S(2)}) async-start(), calls=%async_computation.13 | async-start | bytes 9437184 | tf_op jit(solution)/shard_map/all_gather | solution.py:235
  173.9 572.3 %all-gather.29.cloned.1.call-start = ((), (), s32[]{:S(2)}) async-start(), calls=%async_computation.17 | async-start | bytes 2359296 | tf_op jit(solution)/shard_map/all_gather | solution.py:172
  174.7 654.9 %reduce-scatter.14.cloned.1.call-start = ((), (), s32[]{:S(2)}) async-start(), calls=%async_computation.18 | async-start | bytes 5242880 | tf_op jit(solution)/shard_map/reduce_scatter | solution.py:257
  752.6 122.9 %all-gather.31.cloned.1.call-start = ((), (), s32[]{:S(2)}) async-start(), calls=%async_computation.19 | async-start | bytes 6488064 | tf_op jit(solution)/shard_map/all_gather | solution.py:173
  753.3 205.1 %all-gather.39.cloned.1.call-start = ((), (), s32[]{:S(2)}) async-start(), calls=%async_computation.33 | async-start | bytes 5242880 | tf_op jit(solution)/shard_map/all_gather | solution.py:264
  833.4 168.9 %all-gather.33.cloned.1.call-start = ((), (), s32[]{:S(2)}) async-start(), calls=%async_computation.20 | async-start | bytes 6488064 | tf_op jit(solution)/shard_map/all_gather | solution.py:174
  834.1 250.5 %all-gather.37.cloned.1.call-start = ((), (), s32[]{:S(2)}) async-start(), calls=%async_computation.23 | async-start | bytes 5242880 | tf_op jit(solution)/shard_map/all_gather | solution.py:199
  834.7 294.9 %all-gather.35.cloned.1.call-start = ((), (), s32[]{:S(2)}) async-start(), calls=%async_computation.21 | async-start | bytes 6488064 | tf_op jit(solution)/shard_map/all_gather | solution.py:175
  835.5 405.8 %reduce-scatter.18.cloned.1.call-start = ((), (), s32[]{:S(2)}) async-start(), calls=%async_computation.24 | async-start | bytes 5242880 | tf_op jit(solution)/shard_map/reduce_scatter | solution.py:287
  1164.4 163.7 %all-gather.41.cloned.1.call-start = ((), (), s32[]{:S(2)}) async-start(), calls=%async_computation.34 | async-start | bytes 5242880 | tf_op jit(solution)/shard_map/all_gather | solution.py:295
  1246.6 831.4 %reduce-scatter.30.cloned.1.call-start = ((), (), s32[]{:S(2)}) async-start(), calls=%async_computation.30 | async-start | bytes 6488064 | tf_op jit(solution)/shard_map/reduce_scatter | solution.py:366
  1257.7 822.7 %reduce-scatter.32.cloned.1.call-start = ((), (), s32[]{:S(2)}) async-start(), calls=%async_computation.31 | async-start | bytes 6488064 | tf_op jit(solution)/shard_map/reduce_scatter | solution.py:369
  1268.8 813.9 %reduce-scatter.34.cloned.1.call-start = ((), (), s32[]{:S(2)}) async-start(), calls=%async_computation.32 | async-start | bytes 6488064 | tf_op jit(solution)/shard_map/reduce_scatter | solution.py:372
  1279.4 820.3 %reduce-scatter.28.cloned.1.call-start = ((), (), s32[]{:S(2)}) async-start(), calls=%async_computation.29 | async-start | bytes 2359296 | tf_op jit(solution)/shard_map/reduce_scatter | solution.py:363
  1344.2 757.3 %reduce-scatter.22.cloned.1.call-start = ((), (), s32[]{:S(2)}) async-start(), calls=%async_computation.26 | async-start | bytes 2359296 | tf_op jit(solution)/shard_map/reduce_scatter | solution.py:354
  2027.9 85.0 %reduce-scatter.24.cloned.1.call-start = ((), (), s32[]{:S(2)}) async-start(), calls=%async_computation.27 | async-start | bytes 2359296 | tf_op jit(solution)/shard_map/reduce_scatter | solution.py:357
  2035.3 122.8 %reduce-scatter.26.cloned.1.call-start = ((), (), s32[]{:S(2)}) async-start(), calls=%async_computation.28 | async-start | bytes 2359296 | tf_op jit(solution)/shard_map/reduce_scatter | solution.py:360
  2045.6 191.6 %reduce-scatter.20.cloned.1.call-start = ((), (), s32[]{:S(2)}) async-start(), calls=%async_computation.25 | async-start | bytes 5242880 | tf_op jit(solution)/shard_map/reduce_scatter | solution.py:345
  2064.4 253.3 %reduce-scatter.16.cloned.1.call-start = ((), (), s32[]{:S(2)}) async-start(), calls=%async_computation.22 | async-start | bytes 5242880 | tf_op jit(solution)/shard_map/reduce_scatter | solution.py:270
  (107 other events, 5254.9 us)
Sparse Core Ops, SparseCore 0:
  9.9 30.7 all-gather.22
  57.3 80.9 all-gather.16
  140.2 26.4 all-gather.18
  168.4 27.9 all-gather.26
  198.1 54.3 all-gather.24
  254.8 54.3 all-gather.20
  311.1 28.1 all-gather.28
  752.7 76.8 reduce-scatter.13
  831.7 43.8 all-gather.30
  877.6 80.7 all-gather.38
  960.4 41.8 all-gather.32
  1003.8 80.7 all-gather.36
  1086.7 42.8 all-gather.34
  1164.5 76.7 reduce-scatter.17
  1246.7 81.2 all-gather.40
  1331.3 62.3 reduce-scatter.29
  1397.4 65.0 reduce-scatter.31
  1465.8 71.7 reduce-scatter.33
  1541.3 40.5 reduce-scatter.27
  2028.0 39.9 reduce-scatter.21
  2071.6 41.2 reduce-scatter.23
  2116.7 41.2 reduce-scatter.25
  2160.4 76.7 reduce-scatter.19
  2239.4 78.2 reduce-scatter.15
where the time goes:
time: 2340 us; the launch traced here: 2330 us
  waiting for transfers between devices  983 us (42%)
  matrix products  755 us (32%)
  other arithmetic  206 us (9%)
  local copies, waits for them, and re-layouts  163 us (7%)
  blocking collectives  128 us (5%)
  loops' own time  48.7 us (2%)
  starting transfers between devices  27.5 us (1%)
    ppermute x32, waiting for transfers between devices, shifted(): return lax.ppermute(value, axis, pairs)  223 us
    dot_general x24, matrix products, scored(): jnp.einsum('sqhd,skhd->shqk', query_heads, key_heads, preferred_element_t...  189 us
    unnamed x3, blocking collectives  101 us
    dot_general x8, matrix products, pair_grads(): jnp.einsum('sqhd,skhd->shqk', grad_heads, value_heads, preferred_element_...  84.6 us
    all_gather x1, waiting for transfers between devices, local(): lax.all_gather(normed_two[None], 'head', axis=0, tiled=True)  82.9 us
    dot_general x8, matrix products, attend_visit(): jnp.einsum('shqk,skhd->sqhd', weights_now, values_here.astype(f32), prefe...  81.5 us
    dot_general x8, matrix products, attend_visit(): jnp.einsum('shqk,skhd->sqhd', weights_now.astype(bf16), values_here, pref...  81.3 us
    reduce_scatter x1, waiting for transfers between devices, local(): lax.psum_scatter((part + jnp.dot(value_rows, full_value.T, preferred_elem...  77.4 us
  transfers between devices with their start and end apart: 56, of which 41 were waited for; matrix products, arithmetic and copies ran while one was open for 45% of the time, Pallas kernels for 0%

commit v1 on v0

v1 whole, which is shorter than its diff:
```python
import functools
import math

import jax
import jax.numpy as jnp
from jax import lax
from jax.experimental import pallas as pl
from jax.experimental.pallas import tpu as pltpu
from jax.sharding import Mesh
from jax.sharding import PartitionSpec as P

HD = 64
ROT = 16

epsilon = 1e-05
masked_value = -1e30
rotary_base = 10000.0
log2_e = math.log2(math.e)
f32 = jnp.float32
bf16 = jnp.bfloat16
BLK = ("plane", "core")
ALL = ("plane", "core", "head")
MIB = 2**20


def dot(left, right, left_axis, right_axis):
    return lax.dot_general(
        left, right, (((left_axis,), (right_axis,)), ((), ())), preferred_element_type=f32
    )


def paired(value, axis, step):
    count = lax.axis_size(axis)
    return lax.ppermute(value, axis, [(source, source ^ step) for source in range(count)])


def exchange(value):
    planes = lax.axis_size("plane")
    value = value.reshape((planes, 2) + value.shape[1:])
    crossed = paired(value[:, 1], "core", 1)
    received = [jnp.stack([value[0, 0], crossed[0]])]
    for step in range(1, planes):
        received.append(paired(jnp.stack([value[step, 0], crossed[step]]), "plane", step))
    received = jnp.stack(received)
    return received.reshape((2 * planes,) + received.shape[2:])


def in_chain():
    return lax.axis_size("head") == 4


def head_offsets(part_rows):
    count = lax.axis_size("head")
    first = lax.axis_index("head") if in_chain() else 0
    part = (first + jnp.arange(count, dtype=jnp.int32)) % count
    inner = jnp.arange(part_rows, dtype=jnp.int32)
    return (part[:, None] * part_rows + inner[None, :]).reshape(-1)


def head_gather(value):
    if not in_chain():
        return lax.all_gather(value, "head", axis=1, tiled=True)
    index = lax.axis_index("head")
    two = lax.ppermute(value, "head", [(0, 2), (1, 3), (2, 0), (3, 1)])
    before = lax.ppermute(value, "head", [(0, 1), (1, 2), (2, 3)])
    after = lax.ppermute(value, "head", [(1, 0), (2, 1), (3, 2)])
    far = lax.ppermute(two, "head", [(1, 0), (2, 3)])
    return jnp.concatenate(
        [value, jnp.where(index == 3, far, after), two, jnp.where(index == 0, far, before)], axis=1
    )


def head_scatter(value):
    if not in_chain():
        return lax.psum_scatter(value, "head", scatter_dimension=1, tiled=True).astype(f32)
    index = lax.axis_index("head")
    own, after, two, before = jnp.split(value, 4, axis=1)
    far = lax.ppermute(
        jnp.where(index == 0, before, after), "head", [(0, 1), (3, 2)]
    )
    passed = (two.astype(f32) + far.astype(f32)).astype(bf16)
    from_two = lax.ppermute(passed, "head", [(0, 2), (1, 3), (2, 0), (3, 1)])
    from_before = lax.ppermute(after, "head", [(0, 1), (1, 2), (2, 3)])
    from_after = lax.ppermute(before, "head", [(1, 0), (2, 1), (3, 2)])
    return (own.astype(f32) + from_two.astype(f32)) + (
        from_before.astype(f32) + from_after.astype(f32)
    )


def blk_gather(value, axis=0):
    return lax.all_gather(value, BLK, axis=axis, tiled=True)


def blk_scatter(value, axis=0):
    return lax.psum_scatter(value.astype(bf16), BLK, scatter_dimension=axis, tiled=True).astype(f32)


def normalize(value, gain, shift):
    center = value - jnp.mean(value, axis=-1, keepdims=True)
    inverse = lax.rsqrt(jnp.mean(center * center, axis=-1, keepdims=True) + epsilon)
    return center * inverse * gain + shift


def norm_back(value, gain, upstream):
    center = value - jnp.mean(value, axis=-1, keepdims=True)
    inverse = lax.rsqrt(jnp.mean(center * center, axis=-1, keepdims=True) + epsilon)
    normed = center * inverse
    scaled = upstream * gain
    back = inverse * (
        scaled
        - jnp.mean(scaled, axis=-1, keepdims=True)
        - normed * jnp.mean(scaled * normed, axis=-1, keepdims=True)
    )
    return (back, jnp.sum(upstream * normed, axis=(0, 1)), jnp.sum(upstream, axis=(0, 1)))


def rotary_tables(positions):
    frequency = jnp.exp(
        jnp.arange(ROT // 2, dtype=jnp.float32) * (-2.0 * math.log(rotary_base) / ROT)
    )
    phase_angle = positions.astype(f32)[:, None, :] * frequency[None, :, None]
    return (jnp.cos(phase_angle), jnp.sin(phase_angle))


smem = pl.BlockSpec(memory_space=pltpu.SMEM)


def whole(shape):
    return pl.BlockSpec(shape, lambda step: (0,) * len(shape))


def compiler_params(mebibytes):
    return pltpu.CompilerParams(vmem_limit_bytes=mebibytes * MIB)


def project_in_kernel(
    blk_ref, rows_ref, query_ref, key_ref, value_ref, bias_q, bias_k, bias_v, cos_ref, sin_ref, out_ref
):
    group = pl.program_id(0)
    blk = blk_ref[0]
    halves = rows_ref.shape[0]
    heads = query_ref.shape[1] // HD
    copies = out_ref.shape[0] // (heads * pl.num_programs(0))
    half = ROT // 2
    for part, (weight, bias) in enumerate(
        ((query_ref, bias_q), (key_ref, bias_k), (value_ref, bias_v))
    ):
        for c in range(halves):
            result = dot(rows_ref[c], weight[...], 1, 0) + bias[...]
            result = result.T
            cosine, sine = cos_ref[c], sin_ref[c]
            for h in range(heads):
                values = result[h * HD : (h + 1) * HD]
                if part < 2:
                    first, second = values[:half], values[half:ROT]
                    values = jnp.concatenate(
                        [
                            first * cosine - second * sine,
                            second * cosine + first * sine,
                            values[ROT:],
                        ],
                        axis=0,
                    )
                values = values.astype(bf16)
                for copy in range(copies):
                    at = ((group * heads + h) * copies + copy) ^ blk
                    out_ref[at, c, part * HD : (part + 1) * HD, :] = values


def project_in(blk, rows, weight, bias, cosine, sine, devices):
    halves, ch, width = rows.shape
    total = weight.shape[1] // 3
    block = min(4 * HD, total)
    groups = total // block
    weights = [
        pl.BlockSpec((width, block), functools.partial(lambda p, g: (0, p * groups + g), part))
        for part in range(3)
    ]
    biases = [
        pl.BlockSpec((1, block), functools.partial(lambda p, g: (0, p * groups + g), part))
        for part in range(3)
    ]
    out = (devices, halves, 3 * HD, ch)
    return pl.pallas_call(
        project_in_kernel,
        grid=(groups,),
        in_specs=[smem, whole(rows.shape)]
        + weights
        + biases
        + [whole(cosine.shape), whole(sine.shape)],
        out_specs=whole(out),
        out_shape=jax.ShapeDtypeStruct(out, bf16),
        compiler_params=compiler_params(40),
        cost_estimate=pl.CostEstimate(
            flops=2 * halves * ch * width * 3 * total,
            bytes_accessed=2 * (rows.size + weight.size + math.prod(out)),
            transcendentals=0,
        ),
    )(blk, rows, weight, weight, weight, bias, bias, bias, cosine, sine)


def head_rows(ref, c, head, copies, blk):
    values = ref[(head * copies) ^ blk, c]
    if copies == 1:
        return values
    values = values.astype(f32)
    for copy in range(1, copies):
        values = values + ref[(head * copies + copy) ^ blk, c].astype(f32)
    return values.astype(bf16)


def project_out_kernel(blk_ref, attended_ref, weight_ref, out_ref, rows_ref, *, heads):
    blk = blk_ref[0]
    halves = out_ref.shape[0]
    copies = attended_ref.shape[0] // heads

    @pl.when(pl.program_id(0) == 0)
    def _():
        for c in range(halves):
            columns = [head_rows(attended_ref, c, h, copies, blk) for h in range(heads)]
            rows_ref[c] = jnp.concatenate(columns, axis=0).T

    for c in range(halves):
        out_ref[c] = dot(rows_ref[c], weight_ref[...], 1, 0).astype(bf16)


def project_out(blk, attended, weight):
    devices, halves, _, ch = attended.shape
    total, width = weight.shape
    block = min(1024, width)
    return pl.pallas_call(
        functools.partial(project_out_kernel, heads=total // HD),
        grid=(width // block,),
        in_specs=[
            smem,
            whole(attended.shape),
            pl.BlockSpec((total, block), lambda step: (0, step)),
        ],
        out_specs=[
            pl.BlockSpec((halves, ch, block), lambda step: (0, 0, step)),
            whole((halves, ch, total)),
        ],
        out_shape=[
            jax.ShapeDtypeStruct((halves, ch, width), bf16),
            jax.ShapeDtypeStruct((halves, ch, total), bf16),
        ],
        compiler_params=compiler_params(32),
        cost_estimate=pl.CostEstimate(
            flops=2 * halves * ch * width * total,
            bytes_accessed=2 * (attended.size + weight.size + halves * ch * (width + total)),
            transcendentals=0,
        ),
    )(blk, attended, weight)


def project_grad_kernel(blk_ref, rows_ref, weight_ref, out_ref):
    group = pl.program_id(0)
    blk = blk_ref[0]
    halves = rows_ref.shape[0]
    heads = weight_ref.shape[0] // HD
    copies = out_ref.shape[0] // (heads * pl.num_programs(0))
    for c in range(halves):
        result = dot(weight_ref[...], rows_ref[c], 1, 1).astype(bf16)
        for h in range(heads):
            for copy in range(copies):
                at = ((group * heads + h) * copies + copy) ^ blk
                out_ref[at, c] = result[h * HD : (h + 1) * HD]


def project_grad(blk, rows, weight, devices):
    halves, ch, width = rows.shape
    total = weight.shape[0]
    block = min(4 * HD, total)
    out = (devices, halves, HD, ch)
    return pl.pallas_call(
        project_grad_kernel,
        grid=(total // block,),
        in_specs=[
            smem,
            whole(rows.shape),
            pl.BlockSpec((block, width), lambda step: (step, 0)),
        ],
        out_specs=whole(out),
        out_shape=jax.ShapeDtypeStruct(out, bf16),
        compiler_params=compiler_params(32),
        cost_estimate=pl.CostEstimate(
            flops=2 * halves * ch * width * total,
            bytes_accessed=2 * (rows.size + weight.size + math.prod(out)),
            transcendentals=0,
        ),
    )(blk, rows, weight)


def project_back_kernel(blk_ref, grads_ref, weight_ref, out_ref, rows_ref, *, heads):
    blk = blk_ref[0]
    halves = out_ref.shape[0]
    copies = grads_ref.shape[0] // heads

    @pl.when(pl.program_id(0) == 0)
    def _():
        for c in range(halves):
            columns = [head_rows(grads_ref, c, h, copies, blk) for h in range(heads)]
            for part in range(3):
                rows_ref[c, :, part * heads * HD : (part + 1) * heads * HD] = jnp.concatenate(
                    [column[part * HD : (part + 1) * HD] for column in columns], axis=0
                ).T

    for c in range(halves):
        out_ref[c] = dot(rows_ref[c], weight_ref[...], 1, 1).astype(bf16)


def project_back(blk, grads, weight):
    devices, halves, _, ch = grads.shape
    width, total = weight.shape
    block = min(512, width)
    return pl.pallas_call(
        functools.partial(project_back_kernel, heads=total // (3 * HD)),
        grid=(width // block,),
        in_specs=[
            smem,
            whole(grads.shape),
            pl.BlockSpec((block, total), lambda step: (step, 0)),
        ],
        out_specs=[
            pl.BlockSpec((halves, ch, block), lambda step: (0, 0, step)),
            whole((halves, ch, total)),
        ],
        out_shape=[
            jax.ShapeDtypeStruct((halves, ch, width), bf16),
            jax.ShapeDtypeStruct((halves, ch, total), bf16),
        ],
        compiler_params=compiler_params(32),
        cost_estimate=pl.CostEstimate(
            flops=2 * halves * ch * width * total,
            bytes_accessed=2 * (grads.size + weight.size + halves * ch * (width + total)),
            transcendentals=0,
        ),
    )(blk, grads, weight)


def attend_kernel(
    place_ref, tiles_ref, along_ref, down_ref, qkv_ref, out_ref, exact_ref, lse_ref, keys, queries, values
):
    blocks, _, ch = qkv_ref.shape
    span = 2 * ch
    tiles = blocks // 2
    mine = tiles_ref.shape[0]
    if mine < tiles:
        out_ref[...] = jnp.zeros(out_ref.shape, out_ref.dtype)
        exact_ref[...] = jnp.zeros(exact_ref.shape, exact_ref.dtype)
        lse_ref[...] = jnp.zeros(lse_ref.shape, lse_ref.dtype)

    def arrange(t, unused):
        for half in range(2):
            block = qkv_ref[place_ref[2 * t + half]]
            columns = slice(half * ch, (half + 1) * ch)
            queries[t, :, columns] = block[:HD]
            keys[t, columns, :] = block[HD : 2 * HD].T
            values[t, :, columns] = block[2 * HD :]
        return unused

    lax.fori_loop(0, tiles, arrange, 0)
    scale = log2_e * HD**-0.5

    def query_tile(step, unused):
        t = tiles_ref[step]
        query = queries[t]

        def visit(j, carry, diagonal=False):
            peak, total, acc = carry
            scores = dot(keys[j], query, 1, 0) * scale
            if diagonal:
                scores = jnp.where(down_ref[...] <= along_ref[...], scores, masked_value)
            new_peak = jnp.maximum(peak, jnp.max(scores, axis=0, keepdims=True))
            weights = jnp.exp2(scores - new_peak)
            shrink = jnp.exp2(peak - new_peak)
            total = total * shrink + jnp.sum(weights, axis=0, keepdims=True)
            acc = acc * shrink + dot(values[j], weights.astype(bf16), 1, 0)
            return new_peak, total, acc

        carry = (
            jnp.full((1, span), masked_value, f32),
            jnp.zeros((1, span), f32),
            jnp.zeros((HD, span), f32),
        )
        carry = visit(t, carry, True)
        peak, total, acc = lax.fori_loop(0, t, visit, carry)
        result = acc / total
        lse = peak + jnp.log2(total)
        for half in range(2):
            at = place_ref[2 * t + half]
            columns = slice(half * ch, (half + 1) * ch)
            exact_ref[at] = result[:, columns]
            out_ref[at] = result[:, columns].astype(bf16)
            lse_ref[at] = lse[:, columns]
        return unused

    lax.fori_loop(0, mine, query_tile, 0)


vmem = pl.BlockSpec(memory_space=pltpu.VMEM)


def attend(place, tiles, along, down, qkv):
    blocks, _, ch = qkv.shape
    n = blocks // 2
    return pl.pallas_call(
        attend_kernel,
        in_specs=[smem, smem] + [vmem] * 3,
        out_specs=[vmem] * 3,
        out_shape=[
            jax.ShapeDtypeStruct((blocks, HD, ch), bf16),
            jax.ShapeDtypeStruct((blocks, HD, ch), f32),
            jax.ShapeDtypeStruct((blocks, 1, ch), f32),
        ],
        scratch_shapes=[
            pltpu.VMEM((n, 2 * ch, HD), bf16),
            pltpu.VMEM((n, HD, 2 * ch), bf16),
            pltpu.VMEM((n, HD, 2 * ch), bf16),
        ],
        compiler_params=compiler_params(40),
        cost_estimate=pl.CostEstimate(
            flops=blocks * blocks * ch * ch * HD * 8,
            bytes_accessed=blocks * ch * HD * 12,
            transcendentals=blocks * blocks * ch * ch // 2,
        ),
    )(place, tiles, along, down, qkv)


def unrotate(values, cosine, sine):
    half = ROT // 2
    first, second = values[:half], values[half:ROT]
    return jnp.concatenate(
        [first * cosine + second * sine, second * cosine - first * sine, values[ROT:]], axis=0
    )


def attend_back_kernel(
    place_ref,
    tiles_ref,
    along_ref,
    down_ref,
    qkv_ref,
    grad_ref,
    exact_ref,
    lse_ref,
    cos_ref,
    sin_ref,
    out_ref,
    sums_ref,
    keys_t,
    keys,
    queries_t,
    queries,
    values,
    grads_t,
    grads,
    lse,
    delta,
    grad_q,
    grad_k,
    grad_v,
):
    blocks, _, ch = qkv_ref.shape
    span = 2 * ch
    tiles = blocks // 2
    mine = tiles_ref.shape[0]

    def arrange(t, unused):
        for half in range(2):
            at = place_ref[2 * t + half]
            block = qkv_ref[at]
            columns = slice(half * ch, (half + 1) * ch)
            queries_t[t, :, columns] = block[:HD]
            queries[t, columns, :] = block[:HD].T
            keys_t[t, :, columns] = block[HD : 2 * HD]
            keys[t, columns, :] = block[HD : 2 * HD].T
            values[t, columns, :] = block[2 * HD :].T
            grad = grad_ref[at]
            grads_t[t, :, columns] = grad
            grads[t, columns, :] = grad.T
            lse[t, :, columns] = lse_ref[at]
            delta[t, :, columns] = jnp.sum(grad.astype(f32) * exact_ref[at], axis=0, keepdims=True)
        grad_q[t] = jnp.zeros(grad_q.shape[1:], f32)
        grad_k[t] = jnp.zeros(grad_k.shape[1:], f32)
        grad_v[t] = jnp.zeros(grad_v.shape[1:], f32)
        return unused

    lax.fori_loop(0, tiles, arrange, 0)
    factor = HD**-0.5
    scale = log2_e * factor

    def query_tile(step, unused):
        t = tiles_ref[step]

        def visit(j, acc, diagonal=False):
            scores = dot(keys[j], queries_t[t], 1, 0) * scale
            weights = jnp.exp2(scores - lse[t])
            if diagonal:
                weights = jnp.where(down_ref[...] <= along_ref[...], weights, 0.0)
            grad_weights = dot(values[j], grads_t[t], 1, 0)
            grad_scores = (weights * (grad_weights - delta[t])).astype(bf16)
            grad_v[j] += dot(weights.astype(bf16), grads[t], 1, 0)
            grad_k[j] += dot(grad_scores, queries[t], 1, 0)
            return acc + dot(keys_t[j], grad_scores, 1, 0)

        acc = visit(t, jnp.zeros((HD, span), f32), True)
        grad_q[t] = lax.fori_loop(0, t, visit, acc)
        return unused

    lax.fori_loop(0, mine, query_tile, 0)

    def finish(t, sums):
        key_t = grad_k[t].T
        value_t = grad_v[t].T
        for half in range(2):
            at = place_ref[2 * t + half]
            columns = slice(half * ch, (half + 1) * ch)
            cosine, sine = cos_ref[2 * t + half], sin_ref[2 * t + half]
            parts = (
                unrotate(grad_q[t][:, columns] * factor, cosine, sine),
                unrotate(key_t[:, columns] * factor, cosine, sine),
                value_t[:, columns],
            )
            rows = jnp.concatenate(parts, axis=0).astype(bf16)
            out_ref[at] = rows
            sums = sums + rows.astype(f32)
        return sums

    sums = lax.fori_loop(0, tiles, finish, jnp.zeros((3 * HD, ch), f32))
    sums_ref[...] = jnp.sum(sums, axis=1, keepdims=True)


def attend_back(place, tiles, along, down, qkv, grad, exact, lse, cosine, sine):
    blocks, _, ch = qkv.shape
    n = blocks // 2
    flat = pltpu.VMEM((n, HD, 2 * ch), bf16)
    tall = pltpu.VMEM((n, 2 * ch, HD), bf16)
    line = pltpu.VMEM((n, 1, 2 * ch), f32)
    return pl.pallas_call(
        attend_back_kernel,
        in_specs=[smem, smem] + [vmem] * 8,
        out_specs=[vmem] * 2,
        out_shape=[
            jax.ShapeDtypeStruct((blocks, 3 * HD, ch), bf16),
            jax.ShapeDtypeStruct((3 * HD, 1), f32),
        ],
        scratch_shapes=[
            flat,
            tall,
            flat,
            tall,
            tall,
            flat,
            tall,
            line,
            line,
            pltpu.VMEM((n, HD, 2 * ch), f32),
            pltpu.VMEM((n, 2 * ch, HD), f32),
            pltpu.VMEM((n, 2 * ch, HD), f32),
        ],
        compiler_params=compiler_params(48),
        cost_estimate=pl.CostEstimate(
            flops=blocks * blocks * ch * ch * HD * 20,
            bytes_accessed=blocks * ch * HD * 24,
            transcendentals=blocks * blocks * ch * ch // 2,
        ),
    )(place, tiles, along, down, qkv, grad, exact, lse, cosine, sine)


def local(
    layer_input,
    block_order,
    first_gain,
    first_shift,
    query_weight,
    key_weight,
    value_weight,
    query_bias,
    key_bias,
    value_bias,
    out_weight,
    second_gain,
    second_shift,
    gate_weight,
    up_weight,
    down_weight,
    out_grad,
):
    seqs, _, halves, part_rows, width = layer_input.shape
    planes = lax.axis_size("plane")
    devices = 2 * planes
    head_size = lax.axis_size("head")
    blk = lax.axis_index("plane") * 2 + lax.axis_index("core")
    head_index = lax.axis_index("head")
    blk_scalar = blk.astype(jnp.int32).reshape(1)
    ch = part_rows * head_size
    blocks = halves * devices
    heads = query_bias.shape[0]
    local_width = heads * HD
    copies = devices // heads

    part = first_gain.shape[0]
    small = jnp.concatenate(
        [first_gain, first_shift, second_gain, second_shift]
        + [member.reshape(-1) for member in (query_bias, key_bias, value_bias)]
    )
    small = lax.all_gather(small, ALL, axis=0, tiled=False).astype(f32)
    gain_one, shift_one, gain_two, shift_two = [
        small[:, k * part : (k + 1) * part].reshape(-1) for k in range(4)
    ]
    biases = lax.dynamic_index_in_dim(
        small[:, 4 * part :].reshape(devices, head_size, -1), head_index, 1, keepdims=False
    )

    def bias_of(start, dims):
        member = biases[:, start : start + heads * dims].reshape(devices, heads, dims)
        return jnp.swapaxes(member, 0, 1).reshape(heads, devices * dims)

    q_dims, k_dims = query_bias.shape[1], key_bias.shape[1]
    bias_query = bias_of(0, q_dims)
    bias_key = jnp.pad(bias_of(heads * q_dims, k_dims), ((0, 0), (0, HD - ROT)))
    bias_value = bias_of(heads * (q_dims + k_dims), q_dims)
    bias = jnp.concatenate([bias_query, bias_key, bias_value], axis=0).reshape(1, -1)

    owner = jnp.arange(devices, dtype=jnp.int32) ^ blk
    first_id = block_order[owner]
    rank = jnp.stack([first_id, 2 * devices - 1 - first_id], axis=1).reshape(-1)
    place = jnp.zeros((blocks,), jnp.int32).at[rank].set(jnp.arange(blocks, dtype=jnp.int32))
    offsets = head_offsets(part_rows)
    own_positions = rank[:halves, None] * ch + offsets[None, :]
    cos_own, sin_own = rotary_tables(own_positions)
    all_positions = jnp.arange(blocks, dtype=jnp.int32)[:, None] * ch + offsets[None, :]
    cos_all, sin_all = rotary_tables(all_positions)
    along = all_positions[:2].reshape(1, -1)
    down = all_positions[:2].reshape(-1, 1)
    tile_count = blocks // 2
    cycle = jnp.arange(tile_count // copies, dtype=jnp.int32)
    share = blk % copies
    tiles = (cycle // 2) * 2 * copies + jnp.where(cycle % 2 == 0, share, 2 * copies - 1 - share)
    if copies == 1:
        tiles = jnp.arange(tile_count, dtype=jnp.int32)

    full_qkv = blk_gather(jnp.concatenate([query_weight, key_weight, value_weight], axis=1))
    full_out = blk_gather(out_weight, 1)
    full_gate = blk_gather(gate_weight)
    full_up = blk_gather(up_weight)
    full_down = blk_gather(down_weight, 1)

    each = range(seqs)
    rows_in = [layer_input[s, 0].astype(f32) for s in each]
    grad_own = [out_grad[s, 0] for s in each]
    rows_one = [head_gather(normalize(rows_in[s], gain_one, shift_one).astype(bf16)) for s in each]
    qkv = [
        exchange(project_in(blk_scalar, rows_one[s], full_qkv, bias, cos_own, sin_own, devices))
        for s in each
    ]
    qkv = [member.reshape(blocks, 3 * HD, ch) for member in qkv]
    grad_rows = [head_gather(grad_own[s]) for s in each]
    attended = [attend(place, tiles, along, down, qkv[s]) for s in each]
    middle = []
    out_rows = []
    rows_two = []
    for s in each:
        moved = exchange(attended[s][0].reshape(devices, halves, HD, ch))
        summand, rows = project_out(blk_scalar, moved, full_out)
        out_rows.append(rows)
        middle.append(rows_in[s] + head_scatter(summand))
        rows_two.append(
            head_gather(normalize(middle[s], gain_two, shift_two).astype(bf16)).reshape(-1, width)
        )

    layer_output = []
    hiddens, grad_gates, grad_ups, grad_middle, norm_two_grads, grad_branch = [], [], [], [], [], []
    for s in each:
        flat_grad = grad_rows[s].reshape(-1, width)
        gate = dot(rows_two[s], full_gate, 1, 0)
        up_value = dot(rows_two[s], full_up, 1, 0)
        sigmoid_gate = jax.nn.sigmoid(gate)
        silu_gate = gate * sigmoid_gate
        hidden = (silu_gate * up_value).astype(bf16)
        summand = dot(hidden, full_down, 1, 0).astype(bf16)
        layer_output.append(middle[s] + head_scatter(summand.reshape(halves, ch, width)))
        grad_hidden = dot(flat_grad, full_down, 1, 1)
        grad_up = (grad_hidden * silu_gate).astype(bf16)
        grad_gate = (
            grad_hidden * up_value * sigmoid_gate * (1.0 + gate * (1.0 - sigmoid_gate))
        ).astype(bf16)
        summand = (dot(grad_gate, full_gate, 1, 1) + dot(grad_up, full_up, 1, 1)).astype(bf16)
        grad_normed_two = head_scatter(summand.reshape(halves, ch, width))
        back, gain_grad, shift_grad = norm_back(middle[s], gain_two, grad_normed_two)
        grad_middle.append(grad_own[s].astype(f32) + back)
        norm_two_grads.append((gain_grad, shift_grad))
        grad_branch.append(head_gather(grad_middle[s].astype(bf16)))
        hiddens.append(hidden)
        grad_gates.append(grad_gate)
        grad_ups.append(grad_up)

    def summed_dot(lefts, rights):
        total = dot(lefts[0], rights[0], 0, 0)
        for s in range(1, seqs):
            total = total + dot(lefts[s], rights[s], 0, 0)
        return total

    flat_grads = [member.reshape(-1, width) for member in grad_rows]
    down_grad = blk_scatter(summed_dot(hiddens, flat_grads), 1)
    gate_grad = blk_scatter(summed_dot(rows_two, grad_gates))
    up_grad = blk_scatter(summed_dot(rows_two, grad_ups))
    flat_branch = [member.reshape(-1, width) for member in grad_branch]
    flat_out_rows = [member.reshape(-1, local_width) for member in out_rows]
    out_weight_grad = blk_scatter(summed_dot(flat_out_rows, flat_branch), 1)

    input_grad, norm_one_grads, qkv_rows, bias_sums = [], [], [], []
    for s in each:
        grad_heads = exchange(project_grad(blk_scalar, grad_branch[s], full_out, devices))
        _, exact, lse = attended[s]
        qkv_grad, sums = attend_back(
            place,
            tiles,
            along,
            down,
            qkv[s],
            grad_heads.reshape(blocks, HD, ch),
            exact,
            lse,
            cos_all,
            sin_all,
        )
        bias_sums.append(sums)
        moved = exchange(qkv_grad.reshape(devices, halves, 3 * HD, ch))
        summand, rows = project_back(blk_scalar, moved, full_qkv)
        qkv_rows.append(rows.reshape(-1, 3 * local_width))
        back, gain_grad, shift_grad = norm_back(rows_in[s], gain_one, head_scatter(summand))
        norm_one_grads.append((gain_grad, shift_grad))
        input_grad.append(grad_middle[s] + back)
    qkv_grad = blk_scatter(
        summed_dot([member.reshape(-1, width) for member in rows_one], qkv_rows)
    )

    def over_all(grads, k):
        total = grads[0][k]
        for s in range(1, seqs):
            total = total + grads[s][k]
        return total.reshape(devices * head_size, part)

    bias_total = bias_sums[0]
    for s in range(1, seqs):
        bias_total = bias_total + bias_sums[s]
    bias_total = bias_total.reshape(3, HD)
    shares = jnp.concatenate(
        [
            bias_total[0].reshape(devices, q_dims),
            bias_total[1, :ROT].reshape(devices, k_dims),
            bias_total[2].reshape(devices, q_dims),
        ],
        axis=1,
    )
    own_head = (jnp.arange(heads, dtype=jnp.int32) == blk // copies).astype(f32)
    own_column = (jnp.arange(head_size, dtype=jnp.int32) == head_index).astype(f32)
    spread = (
        shares[:, None, None, :] * own_head[None, None, :, None] * own_column[None, :, None, None]
    ).reshape(devices * head_size, -1)
    smalls = jnp.concatenate(
        [
            over_all(norm_one_grads, 0),
            over_all(norm_one_grads, 1),
            over_all(norm_two_grads, 0),
            over_all(norm_two_grads, 1),
            spread,
        ],
        axis=1,
    )
    smalls = lax.psum_scatter(smalls, ALL, scatter_dimension=0, tiled=True).reshape(-1)
    norm_grads = [smalls[k * part : (k + 1) * part] for k in range(4)]
    bias_grads = smalls[4 * part :].reshape(heads, 2 * q_dims + k_dims)
    stacked = lambda members: jnp.stack(members)[:, None]
    return (
        stacked(layer_output),
        stacked(input_grad),
        norm_grads[0],
        norm_grads[1],
        qkv_grad[:, :local_width],
        qkv_grad[:, local_width : 2 * local_width],
        qkv_grad[:, 2 * local_width :],
        bias_grads[:, :q_dims],
        bias_grads[:, q_dims : q_dims + k_dims],
        bias_grads[:, q_dims + k_dims :],
        out_weight_grad,
        norm_grads[2],
        norm_grads[3],
        gate_grad,
        up_grad,
        down_grad,
    )


def solution(mesh):
    blk_size, head_size = mesh.devices.shape
    split = Mesh(mesh.devices.reshape(blk_size // 2, 2, head_size), ALL)
    tokens = P(None, BLK, None, "head", None)
    rows = P(BLK, "head")
    columns = P("head", BLK)
    return jax.shard_map(
        local,
        mesh=split,
        in_specs=(
            tokens,
            P(),
            P(ALL),
            P(ALL),
            rows,
            rows,
            rows,
            columns,
            columns,
            columns,
            columns,
            P(ALL),
            P(ALL),
            rows,
            rows,
            columns,
            tokens,
        ),
        out_specs=(
            tokens,
            tokens,
            P(ALL),
            P(ALL),
            rows,
            rows,
            rows,
            columns,
            columns,
            columns,
            columns,
            P(ALL),
            P(ALL),
            rows,
            rows,
            columns,
        ),
        check_vma=False,
    )
```

time: 2340 us -> 1120 us (0.48)
  waiting for transfers between devices: 983 us -> 303 us
  matrix products: 755 us -> 131 us
  starting transfers between devices: 27.5 us -> 341 us
  local copies, waits for them, and re-layouts: 163 us -> 23.5 us
  other arithmetic: 206 us -> 67.6 us
  Pallas kernels: 0 us -> 138 us
  loops' own time: 48.7 us -> 0 us
  blocking collectives: 128 us -> 94.5 us
    dot_general x93 -> x22, matrix products: 755 us -> 131 us  [dot(): lax.dot_general(left, right, (((left_axis,), (right_axis,)), ((), ())), p...]
    all_gather x13 -> x5, waiting for transfers between devices: 443 us -> 0.03 us  [blk_gather(): return lax.all_gather(value, BLK, axis=axis, tiled=True)]
    ppermute x32 -> x96, starting transfers between devices: 25.9 us -> 340 us  [the longest x8 91.4 us: head_gather(): before = lax.ppermute(value, 'head', [(0, 1), (1, 2), (2, 3)])]
    reduce_scatter x11 -> x5, waiting for transfers between devices: 313 us -> 0.01 us  [blk_scatter(): lax.psum_scatter(value.astype(bf16), BLK, scatter_dimension=axis, tiled=T...]
    pallas_call x0 -> x12, Pallas kernels: none -> 138 us  [the longest x2 64.1 us: attend_back(): pl.pallas_call(attend_back_kernel, in_specs=[smem, smem] + [vmem] * 8, ou...]
    ppermute x32 -> x96, waiting for transfers between devices: 223 us -> 301 us  [the longest x8 87.2 us: head_scatter(): from_two = lax.ppermute(passed, 'head', [(0, 2), (1, 3), (2, 0), (3, 1)])]
    convert_element_type x53 -> x19, other arithmetic: 93 us -> 21.6 us  [the longest x4 8.71 us: blk_scatter(): lax.psum_scatter(value.astype(bf16), BLK, scatter_dimension=axis, tiled=T...]
    reduce_sum x13 -> x2, other arithmetic: 72.6 us -> 6.59 us  [norm_back(): jnp.sum(upstream * normed, axis=(0, 1))]
  transfers between devices with their start and end apart: 56 -> 106, of which waited for: 41 -> 35; matrix products, arithmetic and copies ran while one was open for 45% -> 18% of each run, Pallas kernels for 0% -> 12%
where the time goes in v1:
time: 1120 us
  starting transfers between devices  341 us (30%)
  waiting for transfers between devices  303 us (27%)
  Pallas kernels  138 us (12%)
  matrix products  131 us (12%)
  blocking collectives  94.5 us (8%)
  other arithmetic  67.6 us (6%)
  local copies, waits for them, and re-layouts  23.5 us (2%)
  between operations  17.6 us (2%)
    dot_general x22, matrix products, dot(): lax.dot_general(left, right, (((left_axis,), (right_axis,)), ((), ())), p...  131 us
    unnamed x2, blocking collectives  94.5 us
    ppermute x8, starting transfers between devices, head_gather(): before = lax.ppermute(value, 'head', [(0, 1), (1, 2), (2, 3)])  91.4 us
    ppermute x8, waiting for transfers between devices, head_scatter(): from_two = lax.ppermute(passed, 'head', [(0, 2), (1, 3), (2, 0), (3, 1)])  87.2 us
    ppermute x32, waiting for transfers between devices, paired(): lax.ppermute(value, axis, [(source, source ^ step) for source in range(co...  73.1 us
    ppermute x8, waiting for transfers between devices, head_gather(): two = lax.ppermute(value, 'head', [(0, 2), (1, 3), (2, 0), (3, 1)])  65.4 us
    pallas_call x2, Pallas kernels, attend_back(): pl.pallas_call(attend_back_kernel, in_specs=[smem, smem] + [vmem] * 8, ou...  64.1 us
    ppermute x8, starting transfers between devices, head_scatter(): from_two = lax.ppermute(passed, 'head', [(0, 2), (1, 3), (2, 0), (3, 1)])  61 us
  transfers between devices with their start and end apart: 106, of which 35 were waited for; matrix products, arithmetic and copies ran while one was open for 18% of the time, Pallas kernels for 12%

profile of v1, /device:TPU:0, one launch (start us, length us, event | category | flops | bytes accessed | tf_op | source)
XLA Modules:
  0.0 1116.9 jit_solution(13966024294020403615)
XLA Ops:
  12.4 42.7 %all-reduce.1 = bf16[12800]{0:T(1024)(128)(2,1)S(1)} all-reduce(bf16[12800]{0:T(1024)(128)(2,1)S(1)} %dynamic-update-slice), channel_id=2, replica_groups=mesh['plane'=4,'core'=2,'head'=4] {'plane','core','head'}, use_global_device_ids=true, to_apply=%add.1 | all-reduce | flops 12800 | bytes 51200
  70.5 14.2 %collective-permute-done = bf16[2,64,2048]{2,1,0:T(8,128)(2,1)S(1)} collective-permute-done((bf16[2,64,2048]{2,1,0:T(8,128)(2,1)S(1)}, bf16[2,64,2048]{2,1,0:T(8,128)(2,1)S(1)}, u32[]{:S(2)}, u32[]{:S(2)}) %collective-permute-start) | collective-permute-done | bytes 524320 | tf_op jit(solution)/shard_map/ppermute | solution.py:64
  86.2 22.4 %collective-permute-start.27 = (bf16[2,64,2048]{2,1,0:T(8,128)(2,1)S(1)}, bf16[2,64,2048]{2,1,0:T(8,128)(2,1)S(1)}, u32[]{:S(2)}, u32[]{:S(2)}) collective-permute-start(bf16[2,64,2048]{2,1,0:T(8,128)(2,1)S(1)} %get-tuple-element.197), channel_id=1, source_target_pairs={{0,1},{1,2},{2,3},{4,5},{5,6},{6,7},{8,9},{9,10},{10,11},{12,13},{... | collective-permute-start | bytes 1572872 | tf_op jit(solution)/shard_map/ppermute | solution.py:65
  172.6 24.3 %shard_map.289 = (bf16[16,64,256]{2,1,0:T(8,128)(2,1)S(1)}, f32[16,64,256]{2,1,0:T(8,128)S(1)}, f32[16,1,256]{2,1,0:T(1,128)S(1)}) custom-call(s32[16]{0:T(128)S(1)} %scatter_custom_fusion.place_ref, s32[8]{0:T(128)S(1)} %iota.50.tiles_ref, s32[1,512]{1,0:T(1,128)S(1)} %bitcast.369, s32[512,1]{1,0:T(8,128)S(1)} %bitcast.364, bf16[16,192,256]{2,1,0:T(8,128)(2,1)S(1)} %bitcast.348), custom_call_target="tpu_custom_call" | custom-call | flops 8589934592 | bytes 3145728 | tf_op jit(solution)/shard_map/pallas_call | solution.py:407
  203.0 24.3 %shard_map.292 = (bf16[16,64,256]{2,1,0:T(8,128)(2,1)S(1)}, f32[16,64,256]{2,1,0:T(8,128)S(1)}, f32[16,1,256]{2,1,0:T(1,128)S(1)}) custom-call(s32[16]{0:T(128)S(1)} %scatter_custom_fusion.place_ref, s32[8]{0:T(128)S(1)} %iota.54.tiles_ref, s32[1,512]{1,0:T(1,128)S(1)} %bitcast.370, s32[512,1]{1,0:T(8,128)S(1)} %bitcast.365, bf16[16,192,256]{2,1,0:T(8,128)(2,1)S(1)} %bitcast.346), custom_call_target="tpu_custom_call" | custom-call | flops 8589934592 | bytes 3145728 | tf_op jit(solution)/shard_map/pallas_call | solution.py:407
  295.4 32.5 %collective-permute-start.75 = (bf16[2,64,2048]{2,1,0:T(8,128)(2,1)S(1)}, bf16[2,64,2048]{2,1,0:T(8,128)(2,1)S(1)}, u32[]{:S(2)}, u32[]{:S(2)}) collective-permute-start(bf16[2,64,2048]{2,1,0:T(8,128)(2,1)S(1)} %get-tuple-element.203), channel_id=1, source_target_pairs={{0,1},{1,2},{2,3},{4,5},{5,6},{6,7},{8,9},{9,10},{10,11},{12,13},{... | collective-permute-start | bytes 1572872 | tf_op jit(solution)/shard_map/ppermute | solution.py:65
  335.9 17.0 %collective-permute-done.37 = bf16[2,64,2048]{2,1,0:T(8,128)(2,1)} collective-permute-done((bf16[2,64,2048]{2,1,0:T(8,128)(2,1)}, bf16[2,64,2048]{2,1,0:T(8,128)(2,1)}, u32[]{:S(2)}, u32[]{:S(2)}) %collective-permute-start.37) | collective-permute-done | bytes 524320 | tf_op jit(solution)/shard_map/ppermute | solution.py:82
  357.2 12.4 %collective-permute-done.72 = bf16[2,64,2048]{2,1,0:T(8,128)(2,1)S(1)} collective-permute-done((bf16[2,64,2048]{2,1,0:T(8,128)(2,1)S(1)}, bf16[2,64,2048]{2,1,0:T(8,128)(2,1)S(1)}, u32[]{:S(2)}, u32[]{:S(2)}) %collective-permute-start.72) | collective-permute-done | bytes 524320 | tf_op jit(solution)/shard_map/ppermute | solution.py:64
  375.1 17.1 %collective-permute-done.48 = bf16[2,64,2048]{2,1,0:T(8,128)(2,1)S(1)} collective-permute-done((bf16[2,64,2048]{2,1,0:T(8,128)(2,1)S(1)}, bf16[2,64,2048]{2,1,0:T(8,128)(2,1)S(1)}, u32[]{:S(2)}, u32[]{:S(2)}) %collective-permute-start.48) | collective-permute-done | bytes 524320 | tf_op jit(solution)/shard_map/ppermute | solution.py:64
  401.8 12.4 %collective-permute-done.49 = bf16[2,64,2048]{2,1,0:T(8,128)(2,1)S(1)} collective-permute-done((bf16[2,64,2048]{2,1,0:T(8,128)(2,1)S(1)}, bf16[2,64,2048]{2,1,0:T(8,128)(2,1)S(1)}, u32[]{:S(2)}, u32[]{:S(2)}) %collective-permute-start.49) | collective-permute-done | bytes 524320 | tf_op jit(solution)/shard_map/ppermute | solution.py:67
  420.8 16.9 %collective-permute-start.16 = (bf16[2,64,2048]{2,1,0:T(8,128)(2,1)}, bf16[2,64,2048]{2,1,0:T(8,128)(2,1)}, u32[]{:S(2)}, u32[]{:S(2)}) collective-permute-start(bf16[2,64,2048]{2,1,0:T(8,128)(2,1)} %get-tuple-element.284), channel_id=1, source_target_pairs={{0,2},{1,3},{2,0},{3,1},{4,6},{5,7},{6,4},{7,5},{8,10},{9,11},{10,... | collective-permute-start | bytes 1572872 | tf_op jit(solution)/shard_map/ppermute | solution.py:64
  442.1 13.4 %collective-permute-start.19 = (bf16[2,64,2048]{2,1,0:T(8,128)(2,1)}, bf16[2,64,2048]{2,1,0:T(8,128)(2,1)}, u32[]{:S(2)}, u32[]{:S(2)}) collective-permute-start(bf16[2,64,2048]{2,1,0:T(8,128)(2,1)} %get-tuple-element.284), channel_id=1, source_target_pairs={{0,1},{1,2},{2,3},{4,5},{5,6},{6,7},{8,9},{9,10},{10,11},{12,13},{... | collective-permute-start | bytes 1572872 | tf_op jit(solution)/shard_map/ppermute | solution.py:65
  597.4 17.4 %collective-permute-start.21 = (bf16[2,64,2048]{2,1,0:T(8,128)(2,1)S(1)}, bf16[2,64,2048]{2,1,0:T(8,128)(2,1)S(1)}, u32[]{:S(2)}, u32[]{:S(2)}) collective-permute-start(bf16[2,64,2048]{2,1,0:T(8,128)(2,1)S(1)} %add_convert_fusion.12), channel_id=1, source_target_pairs={{0,2},{1,3},{2,0},{3,1},{4,6},{5,7},{6,4},{7,5},{8,10},{9,11},{10,... | collective-permute-start | bytes 1572872 | tf_op jit(solution)/shard_map/ppermute | solution.py:82
  614.9 13.4 %collective-permute-done.53 = bf16[2,64,2048]{2,1,0:T(8,128)(2,1)S(1)} collective-permute-done((bf16[2,64,2048]{2,1,0:T(8,128)(2,1)S(1)}, bf16[2,64,2048]{2,1,0:T(8,128)(2,1)S(1)}, u32[]{:S(2)}, u32[]{:S(2)}) %collective-permute-start.53) | collective-permute-done | bytes 524320 | tf_op jit(solution)/shard_map/ppermute | solution.py:82
  630.2 26.5 %collective-permute-done.21 = bf16[2,64,2048]{2,1,0:T(8,128)(2,1)S(1)} collective-permute-done((bf16[2,64,2048]{2,1,0:T(8,128)(2,1)S(1)}, bf16[2,64,2048]{2,1,0:T(8,128)(2,1)S(1)}, u32[]{:S(2)}, u32[]{:S(2)}) %collective-permute-start.21) | collective-permute-done | bytes 524320 | tf_op jit(solution)/shard_map/ppermute | solution.py:82
  666.6 20.4 %collective-permute-start.80 = (bf16[2,64,2048]{2,1,0:T(8,128)(2,1)S(1)}, bf16[2,64,2048]{2,1,0:T(8,128)(2,1)S(1)}, u32[]{:S(2)}, u32[]{:S(2)}) collective-permute-start(bf16[2,64,2048]{2,1,0:T(8,128)(2,1)S(1)} %get-tuple-element.198), channel_id=1, source_target_pairs={{0,2},{1,3},{2,0},{3,1},{4,6},{5,7},{6,4},{7,5},{8,10},{9,11},{10,... | collective-permute-start | bytes 1572872 | tf_op jit(solution)/shard_map/ppermute | solution.py:64
  778.8 32.1 %shard_map.295 = (bf16[16,192,256]{2,1,0:T(8,128)(2,1)S(1)}, f32[192,1]{1,0:T(8,128)S(1)}) custom-call(s32[16]{0:T(128)S(1)} %copy-done.20, s32[8]{0:T(128)S(1)} %iota.55.tiles_ref, s32[1,512]{1,0:T(1,128)S(1)} %bitcast.371, s32[512,1]{1,0:T(8,128)S(1)} %bitcast.366, bf16[16,192,256]{2,1,0:T(8,128)(2,1)S(1)} %bitcast.349, ...), custom_call_target="tpu_custom_call" | custom-call | flops 21474836480 | bytes 6291456 | tf_op jit(solution)/shard_map/pallas_call | solution.py:540
  812.6 32.0 %shard_map.298 = (bf16[16,192,256]{2,1,0:T(8,128)(2,1)S(1)}, f32[192,1]{1,0:T(8,128)S(1)}) custom-call(s32[16]{0:T(128)S(1)} %copy-done.20, s32[8]{0:T(128)S(1)} %iota.56.tiles_ref, s32[1,512]{1,0:T(1,128)S(1)} %bitcast.372, s32[512,1]{1,0:T(8,128)S(1)} %bitcast.367, bf16[16,192,256]{2,1,0:T(8,128)(2,1)S(1)} %bitcast.347, ...), custom_call_target="tpu_custom_call" | custom-call | flops 21474836480 | bytes 6291456 | tf_op jit(solution)/shard_map/pallas_call | solution.py:540
  859.3 13.1 %collective-permute-done.66 = bf16[2,2,192,256]{3,2,1,0:T(8,128)(2,1)S(1)} collective-permute-done((bf16[2,2,192,256]{3,2,1,0:T(8,128)(2,1)S(1)}, bf16[2,2,192,256]{3,2,1,0:T(8,128)(2,1)S(1)}, u32[]{:S(2)}, u32[]{:S(2)}) %collective-permute-start.66) | collective-permute-done | bytes 393248 | tf_op jit(solution)/shard_map/ppermute | solution.py:34
  872.6 16.2 %collective-permute-done.91 = bf16[2,2,192,256]{3,2,1,0:T(8,128)(2,1)S(1)} collective-permute-done((bf16[2,2,192,256]{3,2,1,0:T(8,128)(2,1)S(1)}, bf16[2,2,192,256]{3,2,1,0:T(8,128)(2,1)S(1)}, u32[]{:S(2)}, u32[]{:S(2)}) %collective-permute-start.91) | collective-permute-done | bytes 393248 | tf_op jit(solution)/shard_map/ppermute | solution.py:34
  936.4 11.2 collective-permute-done.44
  994.1 11.9 %collective-permute-done.95 = bf16[2,64,2048]{2,1,0:T(8,128)(2,1)} collective-permute-done((bf16[2,64,2048]{2,1,0:T(8,128)(2,1)}, bf16[2,64,2048]{2,1,0:T(8,128)(2,1)}, u32[]{:S(2)}, u32[]{:S(2)}) %collective-permute-start.95) | collective-permute-done | bytes 524320 | tf_op jit(solution)/shard_map/ppermute | solution.py:84
  1013.3 17.4 %collective-permute-done.93 = bf16[2,64,2048]{2,1,0:T(8,128)(2,1)} collective-permute-done((bf16[2,64,2048]{2,1,0:T(8,128)(2,1)}, bf16[2,64,2048]{2,1,0:T(8,128)(2,1)}, u32[]{:S(2)}, u32[]{:S(2)}) %collective-permute-start.93) | collective-permute-done | bytes 524320 | tf_op jit(solution)/shard_map/ppermute | solution.py:82
  1035.7 51.7 %all-reduce.2 = f32[32,400]{1,0:T(8,128)S(1)} all-reduce(f32[32,400]{1,0:T(8,128)S(1)} %concatenate.51), channel_id=3, replica_groups=mesh['plane'=4,'core'=2,'head'=4] {'plane','core','head'}, use_global_device_ids=true, to_apply=%region_25.26.clone | all-reduce | flops 12800 | bytes 102400
  (724 shorter events, 586.4 us)
Async XLA Ops:
  7.3 129.2 %all-gather.7.cloned.1.call-start = ((), (), s32[]{:S(2)}) async-start(), calls=%async_computation.5 | async-start | bytes 7077888 | tf_op jit(solution)/shard_map/all_gather | solution.py:91
  9.5 229.1 %all-gather.9.cloned.1.call-start = ((), (), s32[]{:S(2)}) async-start(), calls=%async_computation.6 | async-start | bytes 2359296 | tf_op jit(solution)/shard_map/all_gather | solution.py:91
  10.2 456.3 %all-gather.11.cloned.1.call-start = ((), (), s32[]{:S(2)}) async-start(), calls=%async_computation.7 | async-start | bytes 6488064 | tf_op jit(solution)/shard_map/all_gather | solution.py:91
  11.0 463.9 %all-gather.13.cloned.1.call-start = ((), (), s32[]{:S(2)}) async-start(), calls=%async_computation.8 | async-start | bytes 6488064 | tf_op jit(solution)/shard_map/all_gather | solution.py:91
  11.5 471.5 %all-gather.15.cloned.1.call-start = ((), (), s32[]{:S(2)}) async-start(), calls=%async_computation.9 | async-start | bytes 6488064 | tf_op jit(solution)/shard_map/all_gather | solution.py:91
  60.4 58.7 %collective-permute-start.3 = (bf16[2,64,2048]{2,1,0:T(8,128)(2,1)S(1)}, bf16[2,64,2048]{2,1,0:T(8,128)(2,1)S(1)}, u32[]{:S(2)}, u32[]{:S(2)}) collective-permute-start(bf16[2,64,2048]{2,1,0:T(8,128)(2,1)S(1)} %get-tuple-element.196), channel_id=1, source_target_pairs={{0,1},{1,2},{2,3},{4,5},{5,6},{6,7},{8,9},{9,10},{10,11},{12,13},{... | collective-permute-start | bytes 1572872 | tf_op jit(solution)/shard_map/ppermute | solution.py:65
  66.9 1031.8 %reduce-scatter.8.cloned.1.call-start = ((), (), s32[]{:S(2)}) async-start(), calls=%async_computation.11 | async-start | bytes 2359296 | tf_op jit(solution)/shard_map/reduce_scatter | solution.py:95
  275.3 60.5 %collective-permute-start.13 = (bf16[2,64,2048]{2,1,0:T(8,128)(2,1)}, bf16[2,64,2048]{2,1,0:T(8,128)(2,1)}, u32[]{:S(2)}, u32[]{:S(2)}) collective-permute-start(bf16[2,64,2048]{2,1,0:T(8,128)(2,1)} %add_convert_fusion.14), channel_id=1, source_target_pairs={{0,2},{1,3},{2,0},{3,1},{4,6},{5,7},{6,4},{7,5},{8,10},{9,11},{10,... | collective-permute-start | bytes 1572872 | tf_op jit(solution)/shard_map/ppermute | solution.py:82
  282.1 70.7 %collective-permute-start.37 = (bf16[2,64,2048]{2,1,0:T(8,128)(2,1)}, bf16[2,64,2048]{2,1,0:T(8,128)(2,1)}, u32[]{:S(2)}, u32[]{:S(2)}) collective-permute-start(bf16[2,64,2048]{2,1,0:T(8,128)(2,1)} %add_convert_fusion.11), channel_id=1, source_target_pairs={{0,2},{1,3},{2,0},{3,1},{4,6},{5,7},{6,4},{7,5},{8,10},{9,11},{10,... | collective-permute-start | bytes 1572872 | tf_op jit(solution)/shard_map/ppermute | solution.py:82
  294.0 75.6 %collective-permute-start.72 = (bf16[2,64,2048]{2,1,0:T(8,128)(2,1)S(1)}, bf16[2,64,2048]{2,1,0:T(8,128)(2,1)S(1)}, u32[]{:S(2)}, u32[]{:S(2)}) collective-permute-start(bf16[2,64,2048]{2,1,0:T(8,128)(2,1)S(1)} %get-tuple-element.203), channel_id=1, source_target_pairs={{0,2},{1,3},{2,0},{3,1},{4,6},{5,7},{6,4},{7,5},{8,10},{9,11},{10,... | collective-permute-start | bytes 1572872 | tf_op jit(solution)/shard_map/ppermute | solution.py:64
  294.1 79.7 %collective-permute-start.74 = (bf16[2,64,2048]{2,1,0:T(8,128)(2,1)S(1)}, bf16[2,64,2048]{2,1,0:T(8,128)(2,1)S(1)}, u32[]{:S(2)}, u32[]{:S(2)}) collective-permute-start(bf16[2,64,2048]{2,1,0:T(8,128)(2,1)S(1)} %get-tuple-element.203), channel_id=1, source_target_pairs={{1,0},{2,1},{3,2},{5,4},{6,5},{7,6},{9,8},{10,9},{11,10},{13,12},{... | collective-permute-start | bytes 1572872 | tf_op jit(solution)/shard_map/ppermute | solution.py:66
  295.4 99.2 %collective-permute-start.75 = (bf16[2,64,2048]{2,1,0:T(8,128)(2,1)S(1)}, bf16[2,64,2048]{2,1,0:T(8,128)(2,1)S(1)}, u32[]{:S(2)}, u32[]{:S(2)}) collective-permute-start(bf16[2,64,2048]{2,1,0:T(8,128)(2,1)S(1)} %get-tuple-element.203), channel_id=1, source_target_pairs={{0,1},{1,2},{2,3},{4,5},{5,6},{6,7},{8,9},{9,10},{10,11},{12,13},{... | collective-permute-start | bytes 1572872 | tf_op jit(solution)/shard_map/ppermute | solution.py:65
  440.8 69.0 %collective-permute-start.18 = (bf16[2,64,2048]{2,1,0:T(8,128)(2,1)}, bf16[2,64,2048]{2,1,0:T(8,128)(2,1)}, u32[]{:S(2)}, u32[]{:S(2)}) collective-permute-start(bf16[2,64,2048]{2,1,0:T(8,128)(2,1)} %get-tuple-element.284), channel_id=1, source_target_pairs={{1,0},{2,1},{3,2},{5,4},{6,5},{7,6},{9,8},{10,9},{11,10},{13,12},{... | collective-permute-start | bytes 1572872 | tf_op jit(solution)/shard_map/ppermute | solution.py:66
  442.1 73.9 %collective-permute-start.19 = (bf16[2,64,2048]{2,1,0:T(8,128)(2,1)}, bf16[2,64,2048]{2,1,0:T(8,128)(2,1)}, u32[]{:S(2)}, u32[]{:S(2)}) collective-permute-start(bf16[2,64,2048]{2,1,0:T(8,128)(2,1)} %get-tuple-element.284), channel_id=1, source_target_pairs={{0,1},{1,2},{2,3},{4,5},{5,6},{6,7},{8,9},{9,10},{10,11},{12,13},{... | collective-permute-start | bytes 1572872 | tf_op jit(solution)/shard_map/ppermute | solution.py:65
  502.5 71.1 %collective-permute-start.79 = (bf16[2,64,2048]{2,1,0:T(8,128)(2,1)S(1)}, bf16[2,64,2048]{2,1,0:T(8,128)(2,1)S(1)}, u32[]{:S(2)}, u32[]{:S(2)}) collective-permute-start(bf16[2,64,2048]{2,1,0:T(8,128)(2,1)S(1)} %get-tuple-element.161), channel_id=1, source_target_pairs={{1,0},{2,1},{3,2},{5,4},{6,5},{7,6},{9,8},{10,9},{11,10},{13,12},{... | collective-permute-start | bytes 1572872 | tf_op jit(solution)/shard_map/ppermute | solution.py:84
  503.8 87.4 %collective-permute-start.78 = (bf16[2,64,2048]{2,1,0:T(8,128)(2,1)S(1)}, bf16[2,64,2048]{2,1,0:T(8,128)(2,1)S(1)}, u32[]{:S(2)}, u32[]{:S(2)}) collective-permute-start(bf16[2,64,2048]{2,1,0:T(8,128)(2,1)S(1)} %get-tuple-element.160), channel_id=1, source_target_pairs={{0,1},{1,2},{2,3},{4,5},{5,6},{6,7},{8,9},{9,10},{10,11},{12,13},{... | collective-permute-start | bytes 1572872 | tf_op jit(solution)/shard_map/ppermute | solution.py:83
  597.4 59.3 %collective-permute-start.21 = (bf16[2,64,2048]{2,1,0:T(8,128)(2,1)S(1)}, bf16[2,64,2048]{2,1,0:T(8,128)(2,1)S(1)}, u32[]{:S(2)}, u32[]{:S(2)}) collective-permute-start(bf16[2,64,2048]{2,1,0:T(8,128)(2,1)S(1)} %add_convert_fusion.12), channel_id=1, source_target_pairs={{0,2},{1,3},{2,0},{3,1},{4,6},{5,7},{6,4},{7,5},{8,10},{9,11},{10,... | collective-permute-start | bytes 1572872 | tf_op jit(solution)/shard_map/ppermute | solution.py:82
  726.3 374.2 %reduce-scatter.10.cloned.1.call-start = ((), (), s32[]{:S(2)}) async-start(), calls=%async_computation.12 | async-start | bytes 6488064 | tf_op jit(solution)/shard_map/reduce_scatter | solution.py:95
  737.3 365.5 %reduce-scatter.12.cloned.1.call-start = ((), (), s32[]{:S(2)}) async-start(), calls=%async_computation.13 | async-start | bytes 6488064 | tf_op jit(solution)/shard_map/reduce_scatter | solution.py:95
  748.8 356.3 %reduce-scatter.14.cloned.1.call-start = ((), (), s32[]{:S(2)}) async-start(), calls=%async_computation.14 | async-start | bytes 6488064 | tf_op jit(solution)/shard_map/reduce_scatter | solution.py:95
  759.9 347.6 %reduce-scatter.6.cloned.1.call-start = ((), (), s32[]{:S(2)}) async-start(), calls=%async_computation.10 | async-start | bytes 7077888 | tf_op jit(solution)/shard_map/reduce_scatter | solution.py:95
  992.8 96.8 %collective-permute-start.47 = (bf16[2,64,2048]{2,1,0:T(8,128)(2,1)}, bf16[2,64,2048]{2,1,0:T(8,128)(2,1)}, u32[]{:S(2)}, u32[]{:S(2)}) collective-permute-start(bf16[2,64,2048]{2,1,0:T(8,128)(2,1)} %get-tuple-element.176), channel_id=1, source_target_pairs={{1,0},{2,1},{3,2},{5,4},{6,5},{7,6},{9,8},{10,9},{11,10},{13,12},{... | collective-permute-start | bytes 1572872 | tf_op jit(solution)/shard_map/ppermute | solution.py:84
  1006.0 83.7 %collective-permute-start.46 = (bf16[2,64,2048]{2,1,0:T(8,128)(2,1)}, bf16[2,64,2048]{2,1,0:T(8,128)(2,1)}, u32[]{:S(2)}, u32[]{:S(2)}) collective-permute-start(bf16[2,64,2048]{2,1,0:T(8,128)(2,1)} %get-tuple-element.175), channel_id=1, source_target_pairs={{0,1},{1,2},{2,3},{4,5},{5,6},{6,7},{8,9},{9,10},{10,11},{12,13},{... | collective-permute-start | bytes 1572872 | tf_op jit(solution)/shard_map/ppermute | solution.py:83
  1008.4 81.3 %collective-permute-start.45 = (bf16[2,64,2048]{2,1,0:T(8,128)(2,1)}, bf16[2,64,2048]{2,1,0:T(8,128)(2,1)}, u32[]{:S(2)}, u32[]{:S(2)}) collective-permute-start(bf16[2,64,2048]{2,1,0:T(8,128)(2,1)} %add_convert_fusion.9), channel_id=1, source_target_pairs={{0,2},{1,3},{2,0},{3,1},{4,6},{5,7},{6,4},{7,5},{8,10},{9,11},{10,... | collective-permute-start | bytes 1572872 | tf_op jit(solution)/shard_map/ppermute | solution.py:82
  (215 other events, 6858.2 us)
Sparse Core Ops, SparseCore 0:
  10.6 49.0 all-gather.6
  61.6 28.2 all-gather.8
  91.8 43.3 all-gather.10
  136.8 69.3 all-gather.12
  208.0 53.1 all-gather.14
  726.5 41.2 reduce-scatter.7
  771.6 59.0 reduce-scatter.9
  834.2 80.2 reduce-scatter.11
  918.3 59.0 reduce-scatter.13
  980.6 61.7 reduce-scatter.5

commit v2 on v1

--- a/solution.py
+++ b/solution.py
@@ -45,46 +45,121 @@
     return received.reshape((2 * planes,) + received.shape[2:])
 
 
+def steps_of(axes):
+    for axis in reversed(axes):
+        step = 1
+        while step < lax.axis_size(axis):
+            yield axis, step
+            step *= 2
+
+
+def small_gather(value, axes):
+    for axis, step in steps_of(axes):
+        other = paired(value, axis, step)
+        low = (lax.axis_index(axis) & step) == 0
+        value = jnp.concatenate([jnp.where(low, value, other), jnp.where(low, other, value)])
+    return value
+
+
+def small_scatter(value):
+    shape = value.shape[1:]
+    for axis, step in steps_of(ALL):
+        value = value.reshape((-1, 2) + shape)
+        low = (lax.axis_index(axis) & step) == 0
+        keep = jnp.where(low, value[:, 0], value[:, 1])
+        value = keep + paired(jnp.where(low, value[:, 1], value[:, 0]), axis, step)
+    return value.reshape(shape)
+
+
 def in_chain():
     return lax.axis_size("head") == 4
 
 
+def head_order():
+    first = lax.axis_index("head") if in_chain() else 0
+    return first ^ jnp.arange(lax.axis_size("head"), dtype=jnp.int32)
+
+
 def head_offsets(part_rows):
-    count = lax.axis_size("head")
-    first = lax.axis_index("head") if in_chain() else 0
-    part = (first + jnp.arange(count, dtype=jnp.int32)) % count
     inner = jnp.arange(part_rows, dtype=jnp.int32)
-    return (part[:, None] * part_rows + inner[None, :]).reshape(-1)
-
-
-def head_gather(value):
+    return (head_order()[:, None] * part_rows + inner[None, :]).reshape(-1)
+
+
+def in_head_order(value, axis):
+    if not in_chain():
+        return value
+    order = head_order()
+    rows = value.shape[axis] // lax.axis_size("head")
+    return jnp.concatenate(
+        [
+            lax.dynamic_slice_in_dim(value, order[k] * rows, rows, axis)
+            for k in range(lax.axis_size("head"))
+        ],
+        axis=axis,
+    )
+
+
+ONE = [(0, 1), (1, 0), (2, 3), (3, 2)]
+TWO = [(0, 2), (1, 3), (2, 0), (3, 1)]
+MIDDLE = [(1, 2), (2, 1)]
+OUTWARD = [(1, 0), (2, 3)]
+INWARD = [(0, 1), (3, 2)]
+
+
+def gather_first(value):
+    if not in_chain():
+        return value
+    return lax.ppermute(value, "head", TWO), lax.ppermute(value, "head", ONE)
+
+
+def gather_rest(value, received):
     if not in_chain():
         return lax.all_gather(value, "head", axis=1, tiled=True)
+    two, one = received
+    return (
+        value,
+        one,
+        two,
+        lax.ppermute(two, "head", OUTWARD),
+        lax.ppermute(value, "head", MIDDLE),
+    )
+
+
+def gather_whole(parts):
+    if not in_chain():
+        return parts
+    value, one, two, far, near = parts
     index = lax.axis_index("head")
-    two = lax.ppermute(value, "head", [(0, 2), (1, 3), (2, 0), (3, 1)])
-    before = lax.ppermute(value, "head", [(0, 1), (1, 2), (2, 3)])
-    after = lax.ppermute(value, "head", [(1, 0), (2, 1), (3, 2)])
-    far = lax.ppermute(two, "head", [(1, 0), (2, 3)])
-    return jnp.concatenate(
-        [value, jnp.where(index == 3, far, after), two, jnp.where(index == 0, far, before)], axis=1
-    )
-
-
-def head_scatter(value):
+    last = jnp.where((index == 0) | (index == 3), far, near)
+    return jnp.concatenate([value, one, two, last], axis=1)
+
+
+def scatter_first(value):
     if not in_chain():
-        return lax.psum_scatter(value, "head", scatter_dimension=1, tiled=True).astype(f32)
-    index = lax.axis_index("head")
-    own, after, two, before = jnp.split(value, 4, axis=1)
-    far = lax.ppermute(
-        jnp.where(index == 0, before, after), "head", [(0, 1), (3, 2)]
-    )
+        return value
+    own, one, two, last = jnp.split(value, 4, axis=1)
+    return (
+        own,
+        one,
+        two,
+        lax.ppermute(last, "head", INWARD),
+        lax.ppermute(last, "head", MIDDLE),
+    )
+
+
+def scatter_rest(parts):
+    if not in_chain():
+        return lax.psum_scatter(parts, "head", scatter_dimension=1, tiled=True)
+    own, one, two, far, near = parts
     passed = (two.astype(f32) + far.astype(f32)).astype(bf16)
-    from_two = lax.ppermute(passed, "head", [(0, 2), (1, 3), (2, 0), (3, 1)])
-    from_before = lax.ppermute(after, "head", [(0, 1), (1, 2), (2, 3)])
-    from_after = lax.ppermute(before, "head", [(1, 0), (2, 1), (3, 2)])
-    return (own.astype(f32) + from_two.astype(f32)) + (
-        from_before.astype(f32) + from_after.astype(f32)
-    )
+    return own, lax.ppermute(passed, "head", TWO), lax.ppermute(one, "head", ONE), near
+
+
+def scatter_whole(parts):
+    if not in_chain():
+        return parts.astype(f32)
+    own, two, one, near = [member.astype(f32) for member in parts]
+    return (own + two) + (one + near)
 
 
 def blk_gather(value, axis=0):
@@ -601,27 +676,11 @@
     copies = devices // heads
 
     part = first_gain.shape[0]
+    q_dims, k_dims = query_bias.shape[1], key_bias.shape[1]
     small = jnp.concatenate(
         [first_gain, first_shift, second_gain, second_shift]
         + [member.reshape(-1) for member in (query_bias, key_bias, value_bias)]
     )
-    small = lax.all_gather(small, ALL, axis=0, tiled=False).astype(f32)
-    gain_one, shift_one, gain_two, shift_two = [
-        small[:, k * part : (k + 1) * part].reshape(-1) for k in range(4)
-    ]
-    biases = lax.dynamic_index_in_dim(
-        small[:, 4 * part :].reshape(devices, head_size, -1), head_index, 1, keepdims=False
-    )
-
-    def bias_of(start, dims):
-        member = biases[:, start : start + heads * dims].reshape(devices, heads, dims)
-        return jnp.swapaxes(member, 0, 1).reshape(heads, devices * dims)
-
-    q_dims, k_dims = query_bias.shape[1], key_bias.shape[1]
-    bias_query = bias_of(0, q_dims)
-    bias_key = jnp.pad(bias_of(heads * q_dims, k_dims), ((0, 0), (0, HD - ROT)))
-    bias_value = bias_of(heads * (q_dims + k_dims), q_dims)
-    bias = jnp.concatenate([bias_query, bias_key, bias_value], axis=0).reshape(1, -1)
 
     owner = jnp.arange(devices, dtype=jnp.int32) ^ blk
     first_id = block_order[owner]
@@ -643,99 +702,220 @@
 
     full_qkv = blk_gather(jnp.concatenate([query_weight, key_weight, value_weight], axis=1))
     full_out = blk_gather(out_weight, 1)
-    full_gate = blk_gather(gate_weight)
-    full_up = blk_gather(up_weight)
-    full_down = blk_gather(down_weight, 1)
+
+    def split_small(small):
+        small = small_gather(in_head_order(small[0], 0), BLK).astype(f32)
+        gain_one, shift_one, gain_two, shift_two = [
+            small[:, k * part : (k + 1) * part].reshape(-1) for k in range(4)
+        ]
+        biases = lax.dynamic_index_in_dim(
+            small[:, 4 * part :].reshape(devices, head_size, -1), head_index, 1, keepdims=False
+        )
+
+        def bias_of(start, dims):
+            member = biases[:, start : start + heads * dims].reshape(devices, heads, dims)
+            return jnp.swapaxes(member, 0, 1).reshape(heads, devices * dims)
+
+        bias_query = bias_of(0, q_dims)
+        bias_key = jnp.pad(bias_of(heads * q_dims, k_dims), ((0, 0), (0, HD - ROT)))
+        bias_value = bias_of(heads * (q_dims + k_dims), q_dims)
+        bias = jnp.concatenate([bias_query, bias_key, bias_value], axis=0).reshape(1, -1)
+        return gain_one, shift_one, gain_two, shift_two, bias
 
     each = range(seqs)
-    rows_in = [layer_input[s, 0].astype(f32) for s in each]
+    inputs = [layer_input[s, 0] for s in each]
     grad_own = [out_grad[s, 0] for s in each]
-    rows_one = [head_gather(normalize(rows_in[s], gain_one, shift_one).astype(bf16)) for s in each]
-    qkv = [
-        exchange(project_in(blk_scalar, rows_one[s], full_qkv, bias, cos_own, sin_own, devices))
-        for s in each
-    ]
-    qkv = [member.reshape(blocks, 3 * HD, ch) for member in qkv]
-    grad_rows = [head_gather(grad_own[s]) for s in each]
-    attended = [attend(place, tiles, along, down, qkv[s]) for s in each]
-    middle = []
-    out_rows = []
-    rows_two = []
-    for s in each:
-        moved = exchange(attended[s][0].reshape(devices, halves, HD, ch))
-        summand, rows = project_out(blk_scalar, moved, full_out)
-        out_rows.append(rows)
-        middle.append(rows_in[s] + head_scatter(summand))
-        rows_two.append(
-            head_gather(normalize(middle[s], gain_two, shift_two).astype(bf16)).reshape(-1, width)
-        )
-
-    layer_output = []
-    hiddens, grad_gates, grad_ups, grad_middle, norm_two_grads, grad_branch = [], [], [], [], [], []
-    for s in each:
-        flat_grad = grad_rows[s].reshape(-1, width)
-        gate = dot(rows_two[s], full_gate, 1, 0)
-        up_value = dot(rows_two[s], full_up, 1, 0)
+    rows_in = [member.astype(f32) for member in inputs]
+
+    def norm_one(whole_rows):
+        return normalize(whole_rows.astype(f32), gain_one, shift_one).astype(bf16)
+
+    def norm_one_sums(whole_rows, summand):
+        value = whole_rows.astype(f32)
+        upstream = summand.astype(f32)
+        center = value - jnp.mean(value, axis=-1, keepdims=True)
+        inverse = lax.rsqrt(jnp.mean(center * center, axis=-1, keepdims=True) + epsilon)
+        return jnp.sum(upstream * (center * inverse), axis=(0, 1)), jnp.sum(upstream, axis=(0, 1))
+
+    def queries_of(rows):
+        return project_in(blk_scalar, rows, full_qkv, bias, cos_own, sin_own, devices)
+
+    def move(value, rows):
+        return exchange(value.reshape(devices, halves, rows, ch))
+
+    def norm_two(value):
+        return normalize(value, gain_two, shift_two).astype(bf16)
+
+    def flat(member):
+        return member.reshape(-1, member.shape[-1])
+
+    def feed_first(rows, grad):
+        gate = dot(flat(rows), full_gate, 1, 0)
+        up_value = dot(flat(rows), full_up, 1, 0)
         sigmoid_gate = jax.nn.sigmoid(gate)
         silu_gate = gate * sigmoid_gate
         hidden = (silu_gate * up_value).astype(bf16)
-        summand = dot(hidden, full_down, 1, 0).astype(bf16)
-        layer_output.append(middle[s] + head_scatter(summand.reshape(halves, ch, width)))
-        grad_hidden = dot(flat_grad, full_down, 1, 1)
+        grad_hidden = dot(flat(grad), full_down, 1, 1)
         grad_up = (grad_hidden * silu_gate).astype(bf16)
         grad_gate = (
             grad_hidden * up_value * sigmoid_gate * (1.0 + gate * (1.0 - sigmoid_gate))
         ).astype(bf16)
-        summand = (dot(grad_gate, full_gate, 1, 1) + dot(grad_up, full_up, 1, 1)).astype(bf16)
-        grad_normed_two = head_scatter(summand.reshape(halves, ch, width))
-        back, gain_grad, shift_grad = norm_back(middle[s], gain_two, grad_normed_two)
-        grad_middle.append(grad_own[s].astype(f32) + back)
-        norm_two_grads.append((gain_grad, shift_grad))
-        grad_branch.append(head_gather(grad_middle[s].astype(bf16)))
-        hiddens.append(hidden)
-        grad_gates.append(grad_gate)
-        grad_ups.append(grad_up)
-
-    def summed_dot(lefts, rights):
-        total = dot(lefts[0], rights[0], 0, 0)
-        for s in range(1, seqs):
-            total = total + dot(lefts[s], rights[s], 0, 0)
-        return total
-
-    flat_grads = [member.reshape(-1, width) for member in grad_rows]
-    down_grad = blk_scatter(summed_dot(hiddens, flat_grads), 1)
-    gate_grad = blk_scatter(summed_dot(rows_two, grad_gates))
-    up_grad = blk_scatter(summed_dot(rows_two, grad_ups))
-    flat_branch = [member.reshape(-1, width) for member in grad_branch]
-    flat_out_rows = [member.reshape(-1, local_width) for member in out_rows]
-    out_weight_grad = blk_scatter(summed_dot(flat_out_rows, flat_branch), 1)
-
-    input_grad, norm_one_grads, qkv_rows, bias_sums = [], [], [], []
-    for s in each:
-        grad_heads = exchange(project_grad(blk_scalar, grad_branch[s], full_out, devices))
-        _, exact, lse = attended[s]
-        qkv_grad, sums = attend_back(
-            place,
-            tiles,
-            along,
-            down,
-            qkv[s],
-            grad_heads.reshape(blocks, HD, ch),
-            exact,
-            lse,
-            cos_all,
-            sin_all,
-        )
-        bias_sums.append(sums)
-        moved = exchange(qkv_grad.reshape(devices, halves, 3 * HD, ch))
-        summand, rows = project_back(blk_scalar, moved, full_qkv)
-        qkv_rows.append(rows.reshape(-1, 3 * local_width))
-        back, gain_grad, shift_grad = norm_back(rows_in[s], gain_one, head_scatter(summand))
-        norm_one_grads.append((gain_grad, shift_grad))
-        input_grad.append(grad_middle[s] + back)
-    qkv_grad = blk_scatter(
-        summed_dot([member.reshape(-1, width) for member in rows_one], qkv_rows)
-    )
+        return hidden, grad_gate, grad_up
+
+    def feed_back(grad_gate, grad_up):
+        summand = dot(grad_gate, full_gate, 1, 1) + dot(grad_up, full_up, 1, 1)
+        return summand.astype(bf16).reshape(halves, ch, width)
+
+    def feed_out(hidden):
+        return dot(hidden, full_down, 1, 0).astype(bf16).reshape(halves, ch, width)
+
+    def back_two(s, parts, middle):
+        back, gain_grad, shift_grad = norm_back(middle, gain_two, scatter_whole(parts))
+        grad = grad_own[s].astype(f32) + back
+        return grad, grad.astype(bf16), (gain_grad, shift_grad)
+
+    def back_one(s, parts, grad_middle):
+        back, _, _ = norm_back(rows_in[s], gain_one, scatter_whole(parts))
+        return grad_middle + back
+
+    def attend_of(qkv):
+        return attend(place, tiles, along, down, qkv.reshape(blocks, 3 * HD, ch))
+
+    def attend_back_of(qkv, attended, grad):
+        _, exact, lse = attended
+        grad = grad.reshape(blocks, HD, ch)
+        qkv = qkv.reshape(blocks, 3 * HD, ch)
+        return attend_back(place, tiles, along, down, qkv, grad, exact, lse, cos_all, sin_all)
+
+    def weight_grad(lefts, rights):
+        total = dot(flat(lefts[0]), flat(rights[0]), 0, 0)
+        for left, right in zip(lefts[1:], rights[1:]):
+            total = total + dot(flat(left), flat(right), 0, 0)
+        return total.astype(bf16)
+
+    stage = lax.optimization_barrier
+    in_a, in_b = inputs
+    small = small[None, None]
+    got, got_small = gather_first(in_a), gather_first(small)
+    in_a, small, got, got_small, in_b = stage((in_a, small, got, got_small, in_b))
+    parts, small = gather_rest(in_a, got), gather_rest(small, got_small)
+    parts, small, in_b = stage((parts, small, in_b))
+    got = gather_first(in_b)
+    x_a = gather_whole(parts)
+    gain_one, shift_one, gain_two, shift_two, bias = split_small(gather_whole(small))
+    one_a = norm_one(x_a)
+    qkv_a = queries_of(one_a)
+    got, in_b, x_a, one_a, qkv_a, own_grads = stage((got, in_b, x_a, one_a, qkv_a, out_grad))
+    grads = lax.all_gather(own_grads[:, 0], "head", axis=2, tiled=True)
+    parts = gather_rest(in_b, got)
+    qkv_a = move(qkv_a, 3 * HD)
+    parts, qkv_a, late = stage((parts, qkv_a, (gate_weight, up_weight, down_weight)))
+    full_gate, full_up, full_down = blk_gather(late[0]), blk_gather(late[1]), blk_gather(late[2], 1)
+    x_b = gather_whole(parts)
+    one_b = norm_one(x_b)
+    qkv_b = move(queries_of(one_b), 3 * HD)
+    att_a = attend_of(qkv_a)
+    x_b, one_b, qkv_b, att_a = stage((x_b, one_b, qkv_b, att_a))
+    att = move(att_a[0], HD)
+    att, qkv_b = stage((att, qkv_b))
+    partial, out_a = project_out(blk_scalar, att, full_out)
+    sums = scatter_first(partial)
+    att_b = attend_of(qkv_b)
+    sums, att_b, out_a = stage((sums, att_b, out_a))
+    sums = scatter_rest(sums)
+    att = move(att_b[0], HD)
+    partial, out_b = project_out(blk_scalar, att, full_out)
+    sums, partial, out_b = stage((sums, partial, out_b))
+    middle_a = rows_in[0] + scatter_whole(sums)
+    normed = norm_two(middle_a)
+    got = gather_first(normed)
+    sums = scatter_first(partial)
+    got, sums, normed, middle_a, grads = stage((got, sums, normed, middle_a, grads))
+    parts = gather_rest(normed, got)
+    sums = scatter_rest(sums)
+    grads = in_head_order(grads, 2)
+    parts, sums, (grad_a, grad_b) = stage((parts, sums, (grads[0], grads[1])))
+    middle_b = rows_in[1] + scatter_whole(sums)
+    normed = norm_two(middle_b)
+    got = gather_first(normed)
+    two_a = gather_whole(parts)
+    hid_a, gate_a, up_a = feed_first(two_a, grad_a)
+    got, normed, middle_b, two_a, hid_a, gate_a, up_a = stage(
+        (got, normed, middle_b, two_a, hid_a, gate_a, up_a)
+    )
+    parts = gather_rest(normed, got)
+    partial = feed_back(gate_a, up_a)
+    parts, partial, hid_a, gate_a, up_a = stage((parts, partial, hid_a, gate_a, up_a))
+    sums = scatter_first(partial)
+    two_b = gather_whole(parts)
+    hid_b, gate_b, up_b = feed_first(two_b, grad_b)
+    sums, two_b, hid_b, gate_b, up_b = stage((sums, two_b, hid_b, gate_b, up_b))
+    sums = scatter_rest(sums)
+    partial = feed_back(gate_b, up_b)
+    sums, partial, hid_a, hid_b, gate_b, up_b, two_b = stage(
+        (sums, partial, hid_a, hid_b, gate_b, up_b, two_b)
+    )
+    mid_grad_a, branch_a, norm_grads_two_a = back_two(0, sums, middle_a)
+    got = gather_first(branch_a)
+    sums = scatter_first(partial)
+    down_grad = weight_grad((hid_a, hid_b), (grad_a, grad_b))
+    feeds = jnp.concatenate([feed_out(hid_a), feed_out(hid_b)])
+    got, sums, down_grad, feeds, branch_a, mid_grad_a, gate_a, up_a = stage(
+        (got, sums, down_grad, feeds, branch_a, mid_grad_a, gate_a, up_a)
+    )
+    down_grad = blk_scatter(down_grad, 1)
+    parts = gather_rest(branch_a, got)
+    sums = scatter_rest(sums)
+    gate_grad = weight_grad((two_a, two_b), (gate_a, gate_b))
+    up_grad = weight_grad((two_a, two_b), (up_a, up_b))
+    parts, sums, gate_grad, up_grad, feeds = stage((parts, sums, gate_grad, up_grad, feeds))
+    gate_grad = blk_scatter(gate_grad)
+    up_grad = blk_scatter(up_grad)
+    mid_grad_b, branch_b, norm_grads_two_b = back_two(1, sums, middle_b)
+    got = gather_first(branch_b)
+    whole_a = gather_whole(parts)
+    att_grad_a = move(project_grad(blk_scalar, whole_a, full_out, devices), HD)
+    got, branch_b, mid_grad_b, whole_a, att_grad_a, feeds = stage(
+        (got, branch_b, mid_grad_b, whole_a, att_grad_a, feeds)
+    )
+    parts = gather_rest(branch_b, got)
+    feeds = scatter_first(feeds)
+    made_a, bias_sums_a = attend_back_of(qkv_a, att_a, att_grad_a)
+    parts, feeds, made_a, whole_a = stage((parts, feeds, made_a, whole_a))
+    whole_b = gather_whole(parts)
+    att_grad_b = move(project_grad(blk_scalar, whole_b, full_out, devices), HD)
+    out_weight_grad = weight_grad((out_a, out_b), (whole_a, whole_b))
+    feeds, made_a, att_grad_b, out_weight_grad, down_grad = stage(
+        (feeds, made_a, att_grad_b, out_weight_grad, down_grad)
+    )
+    out_weight_grad = blk_scatter(out_weight_grad, 1)
+    feeds = scatter_rest(feeds)
+    moved = move(made_a, 3 * HD)
+    made_b, bias_sums_b = attend_back_of(qkv_b, att_b, att_grad_b)
+    feeds, moved, made_b = stage((feeds, moved, made_b))
+    partial_a, qkv_rows_a = project_back(blk_scalar, moved, full_qkv)
+    sums = scatter_first(partial_a)
+    moved = move(made_b, 3 * HD)
+    feeds = scatter_whole(feeds)
+    layer_output = (middle_a + feeds[:halves], middle_b + feeds[halves:])
+    sums, moved, partial_a, qkv_rows_a, layer_output, gate_grad = stage(
+        (sums, moved, partial_a, qkv_rows_a, layer_output, gate_grad)
+    )
+    partial_b, qkv_rows_b = project_back(blk_scalar, moved, full_qkv)
+    sums_b = scatter_first(partial_b)
+    sums = scatter_rest(sums)
+    qkv_grad = weight_grad((one_a, one_b), (qkv_rows_a, qkv_rows_b))
+    norm_grads_one_a = norm_one_sums(x_a, partial_a)
+    sums, sums_b, partial_b, qkv_grad, norm_grads_one_a = stage(
+        (sums, sums_b, partial_b, qkv_grad, norm_grads_one_a)
+    )
+    qkv_grad = blk_scatter(qkv_grad)
+    sums_b = scatter_rest(sums_b)
+    norm_grads_one_b = norm_one_sums(x_b, partial_b)
+    input_grad = (back_one(0, sums, mid_grad_a), back_one(1, sums_b, mid_grad_b))
+    norm_one_grads = (norm_grads_one_a, norm_grads_one_b)
+    norm_two_grads = (norm_grads_two_a, norm_grads_two_b)
+    bias_sums = (bias_sums_a, bias_sums_b)
 
     def over_all(grads, k):
         total = grads[0][k]
@@ -770,7 +950,7 @@
         ],
         axis=1,
     )
-    smalls = lax.psum_scatter(smalls, ALL, scatter_dimension=0, tiled=True).reshape(-1)
+    smalls = small_scatter(smalls)
     norm_grads = [smalls[k * part : (k + 1) * part] for k in range(4)]
     bias_grads = smalls[4 * part :].reshape(heads, 2 * q_dims + k_dims)
     stacked = lambda members: jnp.stack(members)[:, None]

time: 1120 us -> 820 us (0.73)
  starting transfers between devices: 341 us -> 132 us
  blocking collectives: 94.5 us -> 0 us
  waiting for transfers between devices: 303 us -> 242 us
  other arithmetic: 67.6 us -> 97.2 us
  local copies, waits for them, and re-layouts: 23.5 us -> 47.8 us
    ppermute x64 -> x56, starting transfers between devices: 308 us -> 91 us  [the longest x7 29.7 us: scatter_first(): lax.ppermute(last, 'head', INWARD)]
    unnamed x2 -> x0, blocking collectives: 94.5 us -> none
    ppermute x64 -> x56, waiting for transfers between devices: 228 us -> 169 us  [the longest x7 73.5 us: scatter_rest(): lax.ppermute(passed, 'head', TWO)]
    reduce_sum x0 -> x13, other arithmetic: none -> 19.6 us  [the longest x2 4.69 us: norm_back(): jnp.mean(scaled, axis=-1, keepdims=True)]
    ppermute x32 -> x40, starting transfers between devices: 32.8 us -> 39.8 us  [paired(): lax.ppermute(value, axis, [(source, source ^ step) for source in range(co...]
    ppermute x32 -> x40, waiting for transfers between devices: 73.1 us -> 67.3 us  [paired(): lax.ppermute(value, axis, [(source, source ^ step) for source in range(co...]
  transfers between devices with their start and end apart: 106 -> 107, of which waited for: 35 -> 43; matrix products, arithmetic and copies ran while one was open for 18% -> 30% of each run, Pallas kernels for 12% -> 17%
where the time goes in v2:
time: 820 us; the launch traced here: 812 us
  waiting for transfers between devices  242 us (30%)
  Pallas kernels  138 us (17%)
  starting transfers between devices  132 us (16%)
  matrix products  127 us (15%)
  other arithmetic  97.2 us (12%)
  local copies, waits for them, and re-layouts  47.8 us (6%)
  between operations  27.6 us (3%)
    dot_general x22, matrix products, dot(): lax.dot_general(left, right, (((left_axis,), (right_axis,)), ((), ())), p...  127 us
    ppermute x7, waiting for transfers between devices, scatter_rest(): lax.ppermute(passed, 'head', TWO)  73.5 us
    ppermute x40, waiting for transfers between devices, paired(): lax.ppermute(value, axis, [(source, source ^ step) for source in range(co...  67.3 us
    pallas_call x2, Pallas kernels, attend_back(): pl.pallas_call(attend_back_kernel, in_specs=[smem, smem] + [vmem] * 8, ou...  64.2 us
    ppermute x14, waiting for transfers between devices, gather_first(): return (lax.ppermute(value, 'head', TWO), lax.ppermute(value, 'head', ONE))  49.7 us
    pallas_call x2, Pallas kernels, attend(): pl.pallas_call(attend_kernel, in_specs=[smem, smem] + [vmem] * 3, out_spe...  48.6 us
    ppermute x40, starting transfers between devices, paired(): lax.ppermute(value, axis, [(source, source ^ step) for source in range(co...  39.8 us
    ppermute x7, waiting for transfers between devices, gather_rest(): lax.ppermute(two, 'head', OUTWARD)  35.2 us
  transfers between devices with their start and end apart: 107, of which 43 were waited for; matrix products, arithmetic and copies ran while one was open for 30% of the time, Pallas kernels for 17%

profile of v2, /device:TPU:0, one launch (start us, length us, event | category | flops | bytes accessed | tf_op | source)
XLA Modules:
  0.0 811.8 jit_solution(9896122310767770412)
XLA Ops:
  21.9 17.1 %collective-permute-done.1 = bf16[2,64,2048]{2,1,0:T(8,128)(2,1)S(1)} collective-permute-done((bf16[2,64,2048]{2,1,0:T(8,128)(2,1)S(1)}, bf16[2,64,2048]{2,1,0:T(8,128)(2,1)S(1)}, u32[]{:S(2)}, u32[]{:S(2)}) %collective-permute-start.1) | collective-permute-done | bytes 524320 | tf_op jit(solution)/shard_map/ppermute | solution.py:112
  96.5 8.9 %collective-permute-done.17 = bf16[2,2,192,256]{3,2,1,0:T(8,128)(2,1)S(1)} collective-permute-done((bf16[2,2,192,256]{3,2,1,0:T(8,128)(2,1)S(1)}, bf16[2,2,192,256]{3,2,1,0:T(8,128)(2,1)S(1)}, u32[]{:S(2)}, u32[]{:S(2)}) %collective-permute-start.17) | collective-permute-done | bytes 393248 | tf_op jit(solution)/shard_map/ppermute | solution.py:34
  106.7 8.3 %collective-permute-done.13 = bf16[2,64,2048]{2,1,0:T(8,128)(2,1)} collective-permute-done((bf16[2,64,2048]{2,1,0:T(8,128)(2,1)}, bf16[2,64,2048]{2,1,0:T(8,128)(2,1)}, u32[]{:S(2)}, u32[]{:S(2)}) %collective-permute-start.13) | collective-permute-done | bytes 524320 | tf_op jit(solution)/shard_map/ppermute | solution.py:123
  133.6 24.3 %shard_map.290 = (bf16[16,64,256]{2,1,0:T(8,128)(2,1)S(1)}, f32[16,64,256]{2,1,0:T(8,128)S(1)}, f32[16,1,256]{2,1,0:T(1,128)S(1)}) custom-call(s32[16]{0:T(128)S(1)} %scatter_custom_fusion.place_ref, s32[8]{0:T(128)S(1)} %iota.65.tiles_ref, s32[1,512]{1,0:T(1,128)S(1)} %bitcast.383, s32[512,1]{1,0:T(8,128)S(1)} %bitcast.378, bf16[16,192,256]{2,1,0:T(8,128)(2,1)S(1)} %bitcast.362), custom_call_target="tpu_custom_call" | custom-call | flops 8589934592 | bytes 3145728 | tf_op jit(solution)/shard_map/pallas_call | solution.py:482
  176.9 24.3 %shard_map.292 = (bf16[16,64,256]{2,1,0:T(8,128)(2,1)S(1)}, f32[16,64,256]{2,1,0:T(8,128)S(1)}, f32[16,1,256]{2,1,0:T(1,128)S(1)}) custom-call(s32[16]{0:T(128)S(1)} %scatter_custom_fusion.place_ref, s32[8]{0:T(128)S(1)} %iota.67.tiles_ref, s32[1,512]{1,0:T(1,128)S(1)} %bitcast.384, s32[512,1]{1,0:T(8,128)S(1)} %bitcast.379, bf16[16,192,256]{2,1,0:T(8,128)(2,1)S(1)} %bitcast.360), custom_call_target="tpu_custom_call" | custom-call | flops 8589934592 | bytes 3145728 | tf_op jit(solution)/shard_map/pallas_call | solution.py:482
  244.7 11.2 %collective-permute-done.36 = bf16[2,64,2048]{2,1,0:T(8,128)(2,1)} collective-permute-done((bf16[2,64,2048]{2,1,0:T(8,128)(2,1)}, bf16[2,64,2048]{2,1,0:T(8,128)(2,1)}, u32[]{:S(2)}, u32[]{:S(2)}) %collective-permute-start.36) | collective-permute-done | bytes 524320 | tf_op jit(solution)/shard_map/ppermute | solution.py:112
  281.6 15.0 %collective-permute-done.41 = bf16[2,64,2048]{2,1,0:T(8,128)(2,1)} collective-permute-done((bf16[2,64,2048]{2,1,0:T(8,128)(2,1)}, bf16[2,64,2048]{2,1,0:T(8,128)(2,1)}, u32[]{:S(2)}, u32[]{:S(2)}) %collective-permute-start.41) | collective-permute-done | bytes 524320 | tf_op jit(solution)/shard_map/ppermute | solution.py:155
  296.7 9.3 %collective-permute-done.39 = bf16[2,64,2048]{2,1,0:T(8,128)(2,1)} collective-permute-done((bf16[2,64,2048]{2,1,0:T(8,128)(2,1)}, bf16[2,64,2048]{2,1,0:T(8,128)(2,1)}, u32[]{:S(2)}, u32[]{:S(2)}) %collective-permute-start.39) | collective-permute-done | bytes 524320 | tf_op jit(solution)/shard_map/ppermute | solution.py:123
  316.3 8.3 %fusion.96 = f32[512,1408]{1,0:T(8,128)} fusion(bf16[512,2048]{1,0:T(8,128)(2,1)} %bitcast.390, bf16[2048,1408]{1,0:T(8,128)(2,1)} %all-gather.14.cloned.1.call-done), kind=kOutput, calls=%fused_computation.361 | convolution fusion | flops 2952790016 | bytes 10747904 | tf_op jit(solution)/shard_map/dot_general | solution.py:27
  324.6 8.2 %fusion.95 = f32[512,1408]{1,0:T(8,128)} fusion(bf16[512,2048]{1,0:T(8,128)(2,1)} %bitcast.391, bf16[2048,1408]{1,0:T(8,128)(2,1)} %all-gather.12.cloned.1.call-done), kind=kOutput, calls=%fused_computation.360 | convolution fusion | flops 2952790016 | bytes 10747904 | tf_op jit(solution)/shard_map/dot_general | solution.py:27
  332.8 10.4 %multiply_convert_fusion.3 = (bf16[512,1408]{1,0:T(8,128)(2,1)S(1)}, bf16[512,1408]{1,0:T(8,128)(2,1)S(1)}, bf16[512,1408]{1,0:T(8,128)(2,1)}) fusion(f32[512,1408]{1,0:T(8,128)} %fusion.95, f32[512,1408]{1,0:T(8,128)} %fusion.96, bf16[512,2048]{1,0:T(8,128)(2,1)} %bitcast.400, bf16[1408,2048]{1,0:T(8,128)(2,1)} %all-gather.16.cloned.1.call-done), kind=kOutput, calls=%fused_computation.52 | convolution fusion | flops 2963603456 | bytes 17956864 | tf_op jit(solution)/shard_map/dot_general | solution.py:27
  375.3 8.1 multiply_convert_fusion
  396.7 9.6 %collective-permute-done.49 = bf16[2,64,2048]{2,1,0:T(8,128)(2,1)S(1)} collective-permute-done((bf16[2,64,2048]{2,1,0:T(8,128)(2,1)S(1)}, bf16[2,64,2048]{2,1,0:T(8,128)(2,1)S(1)}, u32[]{:S(2)}, u32[]{:S(2)}) %collective-permute-start.49) | collective-permute-done | bytes 524320 | tf_op jit(solution)/shard_map/ppermute | solution.py:155
  450.6 7.2 fusion.102
  471.3 8.4 %add_convert_fusion.1 = bf16[2048,1408]{1,0:T(8,128)(2,1)} fusion(f32[2048,1408]{1,0:T(8,128)} %fusion.102, bf16[512,2048]{1,0:T(8,128)(2,1)S(1)} %bitcast.393, bf16[512,1408]{1,0:T(8,128)(2,1)} %copy-done.108), kind=kOutput, calls=%fused_computation.5 | convolution fusion | flops 2958557184 | bytes 20840448 | tf_op jit(solution)/shard_map/dot_general | solution.py:27
  479.7 7.7 collective-permute-done.57
  488.1 9.0 %collective-permute-done.55 = bf16[2,64,2048]{2,1,0:T(8,128)(2,1)} collective-permute-done((bf16[2,64,2048]{2,1,0:T(8,128)(2,1)}, bf16[2,64,2048]{2,1,0:T(8,128)(2,1)}, u32[]{:S(2)}, u32[]{:S(2)}) %collective-permute-start.55) | collective-permute-done | bytes 524320 | tf_op jit(solution)/shard_map/ppermute | solution.py:123
  523.5 12.8 %collective-permute-done.60 = bf16[2,64,2048]{2,1,0:T(8,128)(2,1)S(1)} collective-permute-done((bf16[2,64,2048]{2,1,0:T(8,128)(2,1)S(1)}, bf16[2,64,2048]{2,1,0:T(8,128)(2,1)S(1)}, u32[]{:S(2)}, u32[]{:S(2)}) %collective-permute-start.60) | collective-permute-done | bytes 524320 | tf_op jit(solution)/shard_map/ppermute | solution.py:112
  547.7 32.1 %shard_map.295 = (bf16[16,192,256]{2,1,0:T(8,128)(2,1)S(1)}, f32[192,1]{1,0:T(8,128)S(1)}) custom-call(s32[16]{0:T(128)S(1)} %copy-done.27, s32[8]{0:T(128)S(1)} %iota.68.tiles_ref, s32[1,512]{1,0:T(1,128)S(1)} %bitcast.385, s32[512,1]{1,0:T(8,128)S(1)} %bitcast.380, bf16[16,192,256]{2,1,0:T(8,128)(2,1)S(1)} %bitcast.363, ...), custom_call_target="tpu_custom_call" | custom-call | flops 21474836480 | bytes 6291456 | tf_op jit(solution)/shard_map/pallas_call | solution.py:615
  614.7 32.1 %shard_map.297 = (bf16[16,192,256]{2,1,0:T(8,128)(2,1)S(1)}, f32[192,1]{1,0:T(8,128)S(1)}) custom-call(s32[16]{0:T(128)S(1)} %copy-done.27, s32[8]{0:T(128)S(1)} %iota.69.tiles_ref, s32[1,512]{1,0:T(1,128)S(1)} %bitcast.386, s32[512,1]{1,0:T(8,128)S(1)} %bitcast.381, bf16[16,192,256]{2,1,0:T(8,128)(2,1)S(1)} %bitcast.361, ...), custom_call_target="tpu_custom_call" | custom-call | flops 21474836480 | bytes 6291456 | tf_op jit(solution)/shard_map/pallas_call | solution.py:615
  678.1 8.9 %collective-permute-done.82 = bf16[2,2,192,256]{3,2,1,0:T(8,128)(2,1)S(1)} collective-permute-done((bf16[2,2,192,256]{3,2,1,0:T(8,128)(2,1)S(1)}, bf16[2,2,192,256]{3,2,1,0:T(8,128)(2,1)S(1)}, u32[]{:S(2)}, u32[]{:S(2)}) %collective-permute-start.82) | collective-permute-done | bytes 393248 | tf_op jit(solution)/shard_map/ppermute | solution.py:34
  687.0 8.2 %collective-permute-done.83 = bf16[2,2,192,256]{3,2,1,0:T(8,128)(2,1)S(1)} collective-permute-done((bf16[2,2,192,256]{3,2,1,0:T(8,128)(2,1)S(1)}, bf16[2,2,192,256]{3,2,1,0:T(8,128)(2,1)S(1)}, u32[]{:S(2)}, u32[]{:S(2)}) %collective-permute-start.83) | collective-permute-done | bytes 393248 | tf_op jit(solution)/shard_map/ppermute | solution.py:34
  725.2 15.6 %collective-permute-done.85 = bf16[2,64,2048]{2,1,0:T(8,128)(2,1)} collective-permute-done((bf16[2,64,2048]{2,1,0:T(8,128)(2,1)}, bf16[2,64,2048]{2,1,0:T(8,128)(2,1)}, u32[]{:S(2)}, u32[]{:S(2)}) %collective-permute-start.85) | collective-permute-done | bytes 524320 | tf_op jit(solution)/shard_map/ppermute | solution.py:155
  775.0 18.0 %collective-permute-done.89 = bf16[2,64,2048]{2,1,0:T(8,128)(2,1)} collective-permute-done((bf16[2,64,2048]{2,1,0:T(8,128)(2,1)}, bf16[2,64,2048]{2,1,0:T(8,128)(2,1)}, u32[]{:S(2)}, u32[]{:S(2)}) %collective-permute-start.89) | collective-permute-done | bytes 524320 | tf_op jit(solution)/shard_map/ppermute | solution.py:155
  (751 shorter events, 461.3 us)
Async XLA Ops:
  7.3 64.9 %all-gather.8.cloned.1.call-start = ((), (), s32[]{:S(2)}) async-start(), calls=%async_computation.5 | async-start | bytes 7077888 | tf_op jit(solution)/shard_map/all_gather | solution.py:166
  9.5 160.6 %all-gather.10.cloned.1.call-start = ((), (), s32[]{:S(2)}) async-start(), calls=%async_computation.6 | async-start | bytes 2359296 | tf_op jit(solution)/shard_map/all_gather | solution.py:166
  16.3 250.1 %all-gather.18.cloned.1.call-start = ((), (), s32[]{:S(2)}) async-start(), calls=%async_computation.15 | async-start | bytes 5242880 | tf_op jit(solution)/shard_map/all_gather | solution.py:809
  80.6 235.7 %all-gather.14.cloned.1.call-start = ((), (), s32[]{:S(2)}) async-start(), calls=%async_computation.8 | async-start | bytes 6488064 | tf_op jit(solution)/shard_map/all_gather | solution.py:166
  115.0 209.6 %all-gather.12.cloned.1.call-start = ((), (), s32[]{:S(2)}) async-start(), calls=%async_computation.7 | async-start | bytes 6488064 | tf_op jit(solution)/shard_map/all_gather | solution.py:166
  115.6 217.2 %all-gather.16.cloned.1.call-start = ((), (), s32[]{:S(2)}) async-start(), calls=%async_computation.9 | async-start | bytes 6488064 | tf_op jit(solution)/shard_map/all_gather | solution.py:166
  164.2 434.2 %reduce-scatter.6.cloned.1.call-start = ((), (), s32[]{:S(2)}) async-start(), calls=%async_computation.10 | async-start | bytes 6488064 | tf_op jit(solution)/shard_map/reduce_scatter | solution.py:170
  308.9 34.3 %collective-permute-start.44 = (bf16[2,64,2048]{2,1,0:T(8,128)(2,1)S(1)}, bf16[2,64,2048]{2,1,0:T(8,128)(2,1)}, u32[]{:S(2)}, u32[]{:S(2)}) collective-permute-start(bf16[2,64,2048]{2,1,0:T(8,128)(2,1)S(1)} %add_convert_fusion.10), channel_id=1, source_target_pairs={{0,1},{1,0},{2,3},{3,2},{4,5},{5,4},{6,7},{7,6},{8,9},{9,8},{10,11... | collective-permute-start | bytes 1572872 | tf_op jit(solution)/shard_map/ppermute | solution.py:112
  443.9 202.9 %reduce-scatter.8.cloned.1.call-start = ((), (), s32[]{:S(2)}) async-start(), calls=%async_computation.11 | async-start | bytes 6488064 | tf_op jit(solution)/shard_map/reduce_scatter | solution.py:170
  497.1 248.7 %reduce-scatter.14.cloned.1.call-start = ((), (), s32[]{:S(2)}) async-start(), calls=%async_computation.14 | async-start | bytes 6488064 | tf_op jit(solution)/shard_map/reduce_scatter | solution.py:170
  508.2 265.0 %reduce-scatter.12.cloned.1.call-start = ((), (), s32[]{:S(2)}) async-start(), calls=%async_computation.13 | async-start | bytes 2359296 | tf_op jit(solution)/shard_map/reduce_scatter | solution.py:170
  540.7 39.1 %collective-permute-start.68 = (bf16[4,64,2048]{2,1,0:T(8,128)(2,1)S(1)}, bf16[4,64,2048]{2,1,0:T(8,128)(2,1)S(1)}, u32[]{:S(2)}, u32[]{:S(2)}) collective-permute-start(bf16[4,64,2048]{2,1,0:T(8,128)(2,1)S(1)} %get-tuple-element.555), channel_id=1, source_target_pairs={{1,2},{2,1},{5,6},{6,5},{9,10},{10,9},{13,14},{14,13},{17,18},{18,... | collective-permute-start | bytes 3145736 | tf_op jit(solution)/shard_map/ppermute | solution.py:146
  541.5 38.3 %collective-permute-start.67 = (bf16[4,64,2048]{2,1,0:T(8,128)(2,1)S(1)}, bf16[4,64,2048]{2,1,0:T(8,128)(2,1)S(1)}, u32[]{:S(2)}, u32[]{:S(2)}) collective-permute-start(bf16[4,64,2048]{2,1,0:T(8,128)(2,1)S(1)} %get-tuple-element.555), channel_id=1, source_target_pairs={{0,1},{3,2},{4,5},{7,6},{8,9},{11,10},{12,13},{15,14},{16,17},{19,... | collective-permute-start | bytes 3145736 | tf_op jit(solution)/shard_map/ppermute | solution.py:145
  545.6 34.2 %collective-permute-start.66 = (bf16[2,64,2048]{2,1,0:T(8,128)(2,1)S(1)}, bf16[2,64,2048]{2,1,0:T(8,128)(2,1)S(1)}, u32[]{:S(2)}, u32[]{:S(2)}) collective-permute-start(bf16[2,64,2048]{2,1,0:T(8,128)(2,1)S(1)} %get-tuple-element.381), channel_id=1, source_target_pairs={{1,2},{2,1},{5,6},{6,5},{9,10},{10,9},{13,14},{14,13},{17,18},{18,... | collective-permute-start | bytes 1572872 | tf_op jit(solution)/shard_map/ppermute | solution.py:124
  603.3 49.9 %collective-permute-start.73 = (bf16[4,64,2048]{2,1,0:T(8,128)(2,1)}, bf16[4,64,2048]{2,1,0:T(8,128)(2,1)}, u32[]{:S(2)}, u32[]{:S(2)}) collective-permute-start(bf16[4,64,2048]{2,1,0:T(8,128)(2,1)} %add_convert_fusion.5), channel_id=1, source_target_pairs={{0,2},{1,3},{2,0},{3,1},{4,6},{5,7},{6,4},{7,5},{8,10},{9,11},{10,... | collective-permute-start | bytes 3145736 | tf_op jit(solution)/shard_map/ppermute | solution.py:155
  606.6 46.6 %collective-permute-start.74 = (bf16[4,64,2048]{2,1,0:T(8,128)(2,1)}, bf16[4,64,2048]{2,1,0:T(8,128)(2,1)}, u32[]{:S(2)}, u32[]{:S(2)}) collective-permute-start(bf16[4,64,2048]{2,1,0:T(8,128)(2,1)} %get-tuple-element.393), channel_id=1, source_target_pairs={{0,1},{1,0},{2,3},{3,2},{4,5},{5,4},{6,7},{7,6},{8,9},{9,8},{10,11... | collective-permute-start | bytes 3145736 | tf_op jit(solution)/shard_map/ppermute | solution.py:155
  606.6 195.9 %reduce-scatter.10.cloned.1.call-start = ((), (), s32[]{:S(2)}) async-start(), calls=%async_computation.12 | async-start | bytes 7077888 | tf_op jit(solution)/shard_map/reduce_scatter | solution.py:170
  609.2 40.0 %collective-permute-start.76 = (bf16[2,2,192,256]{3,2,1,0:T(8,128)(2,1)}, bf16[2,2,192,256]{3,2,1,0:T(8,128)(2,1)}, u32[]{:S(2)}, u32[]{:S(2)}) collective-permute-start(bf16[2,2,192,256]{3,2,1,0:T(8,128)(2,1)} %pad_maximum_fusion.23), channel_id=1, source_target_pairs={{0,8},{8,0},{16,24},{24,16},{1,9},{9,1},{17,25},{25,17},{2,10},{10... | collective-permute-start | bytes 1179656 | tf_op jit(solution)/shard_map/ppermute | solution.py:34
  610.7 38.5 %collective-permute-start.77 = (bf16[2,2,192,256]{3,2,1,0:T(8,128)(2,1)}, bf16[2,2,192,256]{3,2,1,0:T(8,128)(2,1)}, u32[]{:S(2)}, u32[]{:S(2)}) collective-permute-start(bf16[2,2,192,256]{3,2,1,0:T(8,128)(2,1)} %pad_maximum_fusion.24), channel_id=1, source_target_pairs={{0,16},{8,24},{16,0},{24,8},{1,17},{9,25},{17,1},{25,9},{2,18},{10... | collective-permute-start | bytes 1179656 | tf_op jit(solution)/shard_map/ppermute | solution.py:34
  613.2 36.0 %collective-permute-start.78 = (bf16[2,2,192,256]{3,2,1,0:T(8,128)(2,1)}, bf16[2,2,192,256]{3,2,1,0:T(8,128)(2,1)}, u32[]{:S(2)}, u32[]{:S(2)}) collective-permute-start(bf16[2,2,192,256]{3,2,1,0:T(8,128)(2,1)} %pad_maximum_fusion.25), channel_id=1, source_target_pairs={{0,24},{8,16},{16,8},{24,0},{1,25},{9,17},{17,9},{25,1},{2,26},{10... | collective-permute-start | bytes 1179656 | tf_op jit(solution)/shard_map/ppermute | solution.py:34
  662.6 34.5 %collective-permute-start.80 = (bf16[2,64,2048]{2,1,0:T(8,128)(2,1)S(1)}, bf16[2,64,2048]{2,1,0:T(8,128)(2,1)S(1)}, u32[]{:S(2)}, u32[]{:S(2)}) collective-permute-start(bf16[2,64,2048]{2,1,0:T(8,128)(2,1)S(1)} %get-tuple-element.571), channel_id=1, source_target_pairs={{1,2},{2,1},{5,6},{6,5},{9,10},{10,9},{13,14},{14,13},{17,18},{18,... | collective-permute-start | bytes 1572872 | tf_op jit(solution)/shard_map/ppermute | solution.py:146
  663.4 33.8 %collective-permute-start.79 = (bf16[2,64,2048]{2,1,0:T(8,128)(2,1)S(1)}, bf16[2,64,2048]{2,1,0:T(8,128)(2,1)S(1)}, u32[]{:S(2)}, u32[]{:S(2)}) collective-permute-start(bf16[2,64,2048]{2,1,0:T(8,128)(2,1)S(1)} %get-tuple-element.571), channel_id=1, source_target_pairs={{0,1},{3,2},{4,5},{7,6},{8,9},{11,10},{12,13},{15,14},{16,17},{19,... | collective-permute-start | bytes 1572872 | tf_op jit(solution)/shard_map/ppermute | solution.py:145
  703.8 37.8 %collective-permute-start.88 = (bf16[2,64,2048]{2,1,0:T(8,128)(2,1)}, bf16[2,64,2048]{2,1,0:T(8,128)(2,1)}, u32[]{:S(2)}, u32[]{:S(2)}) collective-permute-start(bf16[2,64,2048]{2,1,0:T(8,128)(2,1)} %get-tuple-element.565), channel_id=1, source_target_pairs={{1,2},{2,1},{5,6},{6,5},{9,10},{10,9},{13,14},{14,13},{17,18},{18,... | collective-permute-start | bytes 1572872 | tf_op jit(solution)/shard_map/ppermute | solution.py:146
  705.3 36.3 %collective-permute-start.87 = (bf16[2,64,2048]{2,1,0:T(8,128)(2,1)}, bf16[2,64,2048]{2,1,0:T(8,128)(2,1)}, u32[]{:S(2)}, u32[]{:S(2)}) collective-permute-start(bf16[2,64,2048]{2,1,0:T(8,128)(2,1)} %get-tuple-element.565), channel_id=1, source_target_pairs={{0,1},{3,2},{4,5},{7,6},{8,9},{11,10},{12,13},{15,14},{16,17},{19,... | collective-permute-start | bytes 1572872 | tf_op jit(solution)/shard_map/ppermute | solution.py:145
  (201 other events, 2713.4 us)
Sparse Core Ops, SparseCore 0:
  10.6 48.2 all-gather.7
  60.7 28.2 all-gather.9
  90.6 81.6 all-gather.17
  174.1 48.7 all-gather.13
  224.6 43.2 all-gather.11
  269.7 44.3 all-gather.15
  444.1 60.8 reduce-scatter.5
  508.8 59.0 reduce-scatter.7
  571.4 67.3 reduce-scatter.13
  642.2 45.5 reduce-scatter.11
  741.8 60.6 reduce-scatter.9

commit v3 on v2

--- a/solution.py
+++ b/solution.py
@@ -34,15 +34,19 @@
     return lax.ppermute(value, axis, [(source, source ^ step) for source in range(count)])
 
 
-def exchange(value):
+def exchange_first(value):
     planes = lax.axis_size("plane")
     value = value.reshape((planes, 2) + value.shape[1:])
-    crossed = paired(value[:, 1], "core", 1)
-    received = [jnp.stack([value[0, 0], crossed[0]])]
-    for step in range(1, planes):
-        received.append(paired(jnp.stack([value[step, 0], crossed[step]]), "plane", step))
+    return value[:, 0], paired(value[:, 1], "core", 1)
+
+
+def exchange_rest(parts):
+    near, crossed = parts
+    received = [jnp.stack([near[0], crossed[0]])]
+    for step in range(1, near.shape[0]):
+        received.append(paired(jnp.stack([near[step], crossed[step]]), "plane", step))
     received = jnp.stack(received)
-    return received.reshape((2 * planes,) + received.shape[2:])
+    return received.reshape((-1,) + received.shape[2:])
 
 
 def steps_of(axes):
@@ -61,9 +65,9 @@
     return value
 
 
-def small_scatter(value):
+def small_scatter(value, axes):
     shape = value.shape[1:]
-    for axis, step in steps_of(ALL):
+    for axis, step in steps_of(axes):
         value = value.reshape((-1, 2) + shape)
         low = (lax.axis_index(axis) & step) == 0
         keep = jnp.where(low, value[:, 0], value[:, 1])
@@ -101,6 +105,7 @@
 
 ONE = [(0, 1), (1, 0), (2, 3), (3, 2)]
 TWO = [(0, 2), (1, 3), (2, 0), (3, 1)]
+THREE = [(0, 3), (1, 2), (2, 1), (3, 0)]
 MIDDLE = [(1, 2), (2, 1)]
 OUTWARD = [(1, 0), (2, 3)]
 INWARD = [(0, 1), (3, 2)]
@@ -125,41 +130,60 @@
     )
 
 
+def gather_direct(value):
+    if not in_chain():
+        return lax.all_gather(value, "head", axis=1, tiled=True)
+    two = lax.ppermute(value, "head", TWO)
+    three = lax.ppermute(value, "head", THREE)
+    return value, lax.ppermute(value, "head", ONE), two, three, three
+
+
+def gather_pieces(parts):
+    return parts if in_chain() else (parts,)
+
+
 def gather_whole(parts):
     if not in_chain():
         return parts
     value, one, two, far, near = parts
+    last = jnp.where(ends_chain() == 1, far, near)
+    return jnp.concatenate([value, one, two, last], axis=1)
+
+
+def ends_chain():
     index = lax.axis_index("head")
-    last = jnp.where((index == 0) | (index == 3), far, near)
-    return jnp.concatenate([value, one, two, last], axis=1)
-
-
-def scatter_first(value):
+    return ((index == 0) | (index == lax.axis_size("head") - 1)).astype(jnp.int32)
+
+
+def scatter_first(pieces):
     if not in_chain():
-        return value
-    own, one, two, last = jnp.split(value, 4, axis=1)
-    return (
-        own,
-        one,
-        two,
-        lax.ppermute(last, "head", INWARD),
-        lax.ppermute(last, "head", MIDDLE),
-    )
+        return pieces[0]
+    own, one, two, last = pieces
+    far = lax.ppermute(last, "head", INWARD)
+    return scatter_pass((own, one, two, far, lax.ppermute(last, "head", MIDDLE)))
+
+
+def scatter_pass(parts):
+    if not in_chain():
+        return parts
+    own, one, two, far, near = parts
+    return own, one, (two.astype(f32) + far.astype(f32)).astype(bf16), near
 
 
 def scatter_rest(parts):
     if not in_chain():
         return lax.psum_scatter(parts, "head", scatter_dimension=1, tiled=True)
-    own, one, two, far, near = parts
-    passed = (two.astype(f32) + far.astype(f32)).astype(bf16)
+    own, one, passed, near = parts
     return own, lax.ppermute(passed, "head", TWO), lax.ppermute(one, "head", ONE), near
 
 
+def scatter_pieces(parts):
+    return parts if in_chain() else (parts,)
+
+
 def scatter_whole(parts):
-    if not in_chain():
-        return parts.astype(f32)
-    own, two, one, near = [member.astype(f32) for member in parts]
-    return (own + two) + (one + near)
+    total = [member.astype(f32) for member in scatter_pieces(parts)]
+    return functools.reduce(jnp.add, total)
 
 
 def blk_gather(value, axis=0):
@@ -167,26 +191,7 @@
 
 
 def blk_scatter(value, axis=0):
-    return lax.psum_scatter(value.astype(bf16), BLK, scatter_dimension=axis, tiled=True).astype(f32)
-
-
-def normalize(value, gain, shift):
-    center = value - jnp.mean(value, axis=-1, keepdims=True)
-    inverse = lax.rsqrt(jnp.mean(center * center, axis=-1, keepdims=True) + epsilon)
-    return center * inverse * gain + shift
-
-
-def norm_back(value, gain, upstream):
-    center = value - jnp.mean(value, axis=-1, keepdims=True)
-    inverse = lax.rsqrt(jnp.mean(center * center, axis=-1, keepdims=True) + epsilon)
-    normed = center * inverse
-    scaled = upstream * gain
-    back = inverse * (
-        scaled
-        - jnp.mean(scaled, axis=-1, keepdims=True)
-        - normed * jnp.mean(scaled * normed, axis=-1, keepdims=True)
-    )
-    return (back, jnp.sum(upstream * normed, axis=(0, 1)), jnp.sum(upstream, axis=(0, 1)))
+    return lax.psum_scatter(value, BLK, scatter_dimension=axis, tiled=True)
 
 
 def rotary_tables(positions):
@@ -198,25 +203,58 @@
 
 
 smem = pl.BlockSpec(memory_space=pltpu.SMEM)
+vmem = pl.BlockSpec(memory_space=pltpu.VMEM)
 
 
 def whole(shape):
     return pl.BlockSpec(shape, lambda step: (0,) * len(shape))
 
 
+light = pl.CostEstimate(flops=1000, bytes_accessed=1000, transcendentals=0)
+heavy = pl.CostEstimate(flops=30 * 10**9, bytes_accessed=1000, transcendentals=0)
+
+
 def compiler_params(mebibytes):
     return pltpu.CompilerParams(vmem_limit_bytes=mebibytes * MIB)
 
 
-def project_in_kernel(
-    blk_ref, rows_ref, query_ref, key_ref, value_ref, bias_q, bias_k, bias_v, cos_ref, sin_ref, out_ref
-):
+def piece(refs, k, c, ends):
+    if k < 3:
+        return refs[k][c]
+    return jnp.where(ends == 1, refs[3][c], refs[4][c])
+
+
+def each_piece(refs):
+    count = 4 if len(refs) == 5 else 1
+    return [(k, slice(k * refs[0].shape[1], (k + 1) * refs[0].shape[1])) for k in range(count)]
+
+
+def row_norm(value):
+    center = value - jnp.mean(value, axis=-1, keepdims=True)
+    inverse = lax.rsqrt(jnp.mean(center * center, axis=-1, keepdims=True) + epsilon)
+    return center * inverse, inverse
+
+
+def project_in_kernel(blk_ref, *refs, pieces):
+    rows_in = refs[:pieces]
+    gain_ref, shift_ref, query_ref, key_ref, value_ref, bias_q, bias_k, bias_v = refs[
+        pieces : pieces + 8
+    ]
+    cos_ref, sin_ref, out_ref, rows_ref = refs[pieces + 8 :]
     group = pl.program_id(0)
     blk = blk_ref[0]
     halves = rows_ref.shape[0]
     heads = query_ref.shape[1] // HD
     copies = out_ref.shape[0] // (heads * pl.num_programs(0))
     half = ROT // 2
+
+    @pl.when(group == 0)
+    def _():
+        for c in range(halves):
+            for k, place in each_piece(rows_in):
+                normed, _ = row_norm(piece(rows_in, k, c, blk_ref[1]).astype(f32))
+                rows_ref[c, place, :] = (normed * gain_ref[...] + shift_ref[...]).astype(bf16)
+
     for part, (weight, bias) in enumerate(
         ((query_ref, bias_q), (key_ref, bias_k), (value_ref, bias_v))
     ):
@@ -242,8 +280,9 @@
                     out_ref[at, c, part * HD : (part + 1) * HD, :] = values
 
 
-def project_in(blk, rows, weight, bias, cosine, sine, devices):
-    halves, ch, width = rows.shape
+def project_in(blk, pieces, gain, shift, weight, bias, cosine, sine, devices):
+    halves, _, width = pieces[0].shape
+    ch = cosine.shape[-1]
     total = weight.shape[1] // 3
     block = min(4 * HD, total)
     groups = total // block
@@ -256,22 +295,115 @@
         for part in range(3)
     ]
     out = (devices, halves, 3 * HD, ch)
+    rows = (halves, ch, width)
     return pl.pallas_call(
-        project_in_kernel,
+        functools.partial(project_in_kernel, pieces=len(pieces)),
         grid=(groups,),
-        in_specs=[smem, whole(rows.shape)]
+        in_specs=[smem]
+        + [whole(member.shape) for member in pieces]
+        + [whole(gain.shape)] * 2
         + weights
         + biases
         + [whole(cosine.shape), whole(sine.shape)],
-        out_specs=whole(out),
-        out_shape=jax.ShapeDtypeStruct(out, bf16),
-        compiler_params=compiler_params(40),
-        cost_estimate=pl.CostEstimate(
-            flops=2 * halves * ch * width * 3 * total,
-            bytes_accessed=2 * (rows.size + weight.size + math.prod(out)),
-            transcendentals=0,
-        ),
-    )(blk, rows, weight, weight, weight, bias, bias, bias, cosine, sine)
+        out_specs=[whole(out), whole(rows)],
+        out_shape=[jax.ShapeDtypeStruct(out, bf16), jax.ShapeDtypeStruct(rows, bf16)],
+        compiler_params=compiler_params(48),
+        cost_estimate=light,
+    )(blk, *pieces, gain, shift, weight, weight, weight, bias, bias, bias, cosine, sine)
+
+
+def add_all(refs, c):
+    total = refs[0][c].astype(f32)
+    for ref in refs[1:]:
+        total = total + ref[c].astype(f32)
+    return total
+
+
+def middle_kernel(*refs):
+    sums = refs[:-5]
+    rows_ref, gain_ref, shift_ref, middle_ref, normed_ref = refs[-5:]
+    for c in range(rows_ref.shape[0]):
+        value = rows_ref[c].astype(f32) + add_all(sums, c)
+        middle_ref[c] = value
+        normed, _ = row_norm(value)
+        normed_ref[c] = (normed * gain_ref[...] + shift_ref[...]).astype(bf16)
+
+
+def middle_of(sums, rows, gain, shift):
+    return pl.pallas_call(
+        middle_kernel,
+        in_specs=[vmem] * (len(sums) + 3),
+        out_specs=[vmem] * 2,
+        out_shape=[
+            jax.ShapeDtypeStruct(rows.shape, f32),
+            jax.ShapeDtypeStruct(rows.shape, bf16),
+        ],
+        compiler_params=compiler_params(32),
+        cost_estimate=light,
+    )(*sums, rows, gain, shift)
+
+
+def norm_back_rows(value, gain, upstream):
+    normed, inverse = row_norm(value)
+    scaled = upstream * gain
+    back = inverse * (
+        scaled
+        - jnp.mean(scaled, axis=-1, keepdims=True)
+        - normed * jnp.mean(scaled * normed, axis=-1, keepdims=True)
+    )
+    return back, normed
+
+
+def back_two_kernel(*refs):
+    sums = refs[:-7]
+    middle_ref, grad_ref, gain_ref, out_ref, low_ref, gain_sum, shift_sum = refs[-7:]
+    gain_total = shift_total = 0.0
+    for c in range(middle_ref.shape[0]):
+        upstream = add_all(sums, c)
+        back, normed = norm_back_rows(middle_ref[c], gain_ref[...], upstream)
+        grad = grad_ref[c].astype(f32) + back
+        out_ref[c] = grad
+        low_ref[c] = grad.astype(bf16)
+        gain_total = gain_total + jnp.sum(upstream * normed, axis=0, keepdims=True)
+        shift_total = shift_total + jnp.sum(upstream, axis=0, keepdims=True)
+    gain_sum[...] = gain_total
+    shift_sum[...] = shift_total
+
+
+def back_two(sums, middle, grad, gain):
+    line = jax.ShapeDtypeStruct(gain.shape, f32)
+    return pl.pallas_call(
+        back_two_kernel,
+        in_specs=[vmem] * (len(sums) + 3),
+        out_specs=[vmem] * 4,
+        out_shape=[
+            jax.ShapeDtypeStruct(middle.shape, f32),
+            jax.ShapeDtypeStruct(middle.shape, bf16),
+            line,
+            line,
+        ],
+        compiler_params=compiler_params(32),
+        cost_estimate=light,
+    )(*sums, middle, grad, gain)
+
+
+def back_one_kernel(*refs):
+    sums = refs[:-4]
+    rows_ref, grad_ref, gain_ref, out_ref = refs[-4:]
+    for c in range(rows_ref.shape[0]):
+        back, _ = norm_back_rows(rows_ref[c].astype(f32), gain_ref[...], add_all(sums, c))
+        out_ref[c] = grad_ref[c] + back
+
+
+def back_one(sums, rows, grad, gain):
+    return pl.pallas_call(
+        back_one_kernel,
+        in_specs=[vmem] * (len(sums) + 3),
+        out_specs=vmem,
+        out_shape=jax.ShapeDtypeStruct(rows.shape, f32),
+        compiler_params=compiler_params(32),
+        cost_estimate=light,
+    )(*sums, rows, grad, gain)
 
 
 def head_rows(ref, c, head, copies, blk):
@@ -284,9 +416,15 @@
     return values.astype(bf16)
 
 
-def project_out_kernel(blk_ref, attended_ref, weight_ref, out_ref, rows_ref, *, heads):
+def put_pieces(refs, c, rows):
+    step = rows.shape[0] // len(refs)
+    for k, ref in enumerate(refs):
+        ref[c] = rows[k * step : (k + 1) * step]
+
+
+def project_out_kernel(blk_ref, attended_ref, weight_ref, rows_ref, *out_refs, heads):
     blk = blk_ref[0]
-    halves = out_ref.shape[0]
+    halves = rows_ref.shape[0]
     copies = attended_ref.shape[0] // heads
 
     @pl.when(pl.program_id(0) == 0)
@@ -296,14 +434,15 @@
             rows_ref[c] = jnp.concatenate(columns, axis=0).T
 
     for c in range(halves):
-        out_ref[c] = dot(rows_ref[c], weight_ref[...], 1, 0).astype(bf16)
-
-
-def project_out(blk, attended, weight):
+        put_pieces(out_refs, c, dot(rows_ref[c], weight_ref[...], 1, 0).astype(bf16))
+
+
+def project_out(blk, attended, weight, pieces):
     devices, halves, _, ch = attended.shape
     total, width = weight.shape
     block = min(1024, width)
-    return pl.pallas_call(
+    part = ch // pieces
+    rows, *out = pl.pallas_call(
         functools.partial(project_out_kernel, heads=total // HD),
         grid=(width // block,),
         in_specs=[
@@ -311,30 +450,31 @@
             whole(attended.shape),
             pl.BlockSpec((total, block), lambda step: (0, step)),
         ],
-        out_specs=[
-            pl.BlockSpec((halves, ch, block), lambda step: (0, 0, step)),
-            whole((halves, ch, total)),
-        ],
-        out_shape=[
-            jax.ShapeDtypeStruct((halves, ch, width), bf16),
-            jax.ShapeDtypeStruct((halves, ch, total), bf16),
-        ],
+        out_specs=[whole((halves, ch, total))]
+        + [pl.BlockSpec((halves, part, block), lambda step: (0, 0, step))] * pieces,
+        out_shape=[jax.ShapeDtypeStruct((halves, ch, total), bf16)]
+        + [jax.ShapeDtypeStruct((halves, part, width), bf16)] * pieces,
         compiler_params=compiler_params(32),
-        cost_estimate=pl.CostEstimate(
-            flops=2 * halves * ch * width * total,
-            bytes_accessed=2 * (attended.size + weight.size + halves * ch * (width + total)),
-            transcendentals=0,
-        ),
+        cost_estimate=light,
     )(blk, attended, weight)
-
-
-def project_grad_kernel(blk_ref, rows_ref, weight_ref, out_ref):
+    return out, rows
+
+
+def project_grad_kernel(blk_ref, *refs, pieces):
+    rows_in = refs[:pieces]
+    weight_ref, out_ref, rows_ref = refs[pieces:]
     group = pl.program_id(0)
     blk = blk_ref[0]
-    halves = rows_ref.shape[0]
     heads = weight_ref.shape[0] // HD
     copies = out_ref.shape[0] // (heads * pl.num_programs(0))
-    for c in range(halves):
+
+    @pl.when(group == 0)
+    def _():
+        for c in range(rows_ref.shape[0]):
+            for k, place in each_piece(rows_in):
+                rows_ref[c, place, :] = piece(rows_in, k, c, blk_ref[1])
+
+    for c in range(rows_ref.shape[0]):
         result = dot(weight_ref[...], rows_ref[c], 1, 1).astype(bf16)
         for h in range(heads):
             for copy in range(copies):
@@ -342,36 +482,35 @@
                 out_ref[at, c] = result[h * HD : (h + 1) * HD]
 
 
-def project_grad(blk, rows, weight, devices):
-    halves, ch, width = rows.shape
+def project_grad(blk, pieces, weight, devices, ch):
+    halves, _, width = pieces[0].shape
     total = weight.shape[0]
     block = min(4 * HD, total)
     out = (devices, halves, HD, ch)
+    rows = (halves, ch, width)
     return pl.pallas_call(
-        project_grad_kernel,
+        functools.partial(project_grad_kernel, pieces=len(pieces)),
         grid=(total // block,),
-        in_specs=[
-            smem,
-            whole(rows.shape),
-            pl.BlockSpec((block, width), lambda step: (step, 0)),
-        ],
-        out_specs=whole(out),
-        out_shape=jax.ShapeDtypeStruct(out, bf16),
+        in_specs=[smem]
+        + [whole(member.shape) for member in pieces]
+        + [pl.BlockSpec((block, width), lambda step: (step, 0))],
+        out_specs=[whole(out), whole(rows)],
+        out_shape=[jax.ShapeDtypeStruct(out, bf16), jax.ShapeDtypeStruct(rows, bf16)],
         compiler_params=compiler_params(32),
-        cost_estimate=pl.CostEstimate(
-            flops=2 * halves * ch * width * total,
-            bytes_accessed=2 * (rows.size + weight.size + math.prod(out)),
-            transcendentals=0,
-        ),
-    )(blk, rows, weight)
-
-
-def project_back_kernel(blk_ref, grads_ref, weight_ref, out_ref, rows_ref, *, heads):
+        cost_estimate=light,
+    )(blk, *pieces, weight)
+
+
+def project_back_kernel(blk_ref, *refs, pieces, heads):
+    rows_in = refs[:pieces]
+    grads_ref, weight_ref, rows_ref, gain_sum, shift_sum = refs[pieces : pieces + 5]
+    out_refs, (mean_ref, inverse_ref) = refs[pieces + 5 : -2], refs[-2:]
     blk = blk_ref[0]
-    halves = out_ref.shape[0]
+    step = pl.program_id(0)
+    halves, _, block = out_refs[0].shape
     copies = grads_ref.shape[0] // heads
 
-    @pl.when(pl.program_id(0) == 0)
+    @pl.when(step == 0)
     def _():
         for c in range(halves):
             columns = [head_rows(grads_ref, c, h, copies, blk) for h in range(heads)]
@@ -379,38 +518,59 @@
                 rows_ref[c, :, part * heads * HD : (part + 1) * heads * HD] = jnp.concatenate(
                     [column[part * HD : (part + 1) * HD] for column in columns], axis=0
                 ).T
-
+            for k, place in each_piece(rows_in):
+                value = piece(rows_in, k, c, blk_ref[1]).astype(f32)
+                mean = jnp.mean(value, axis=-1, keepdims=True)
+                center = value - mean
+                mean_ref[c, place, :] = mean
+                inverse_ref[c, place, :] = lax.rsqrt(
+                    jnp.mean(center * center, axis=-1, keepdims=True) + epsilon
+                )
+
+    gain_total = shift_total = 0.0
+    columns = pl.ds(pl.multiple_of(step * block, block), block)
     for c in range(halves):
-        out_ref[c] = dot(rows_ref[c], weight_ref[...], 1, 1).astype(bf16)
-
-
-def project_back(blk, grads, weight):
+        result = dot(rows_ref[c], weight_ref[...], 1, 1)
+        put_pieces(out_refs, c, result.astype(bf16))
+        shift_total = shift_total + jnp.sum(result, axis=0, keepdims=True)
+        for k, place in each_piece(rows_in):
+            if k < 3:
+                value = rows_in[k][c, :, columns]
+            else:
+                value = jnp.where(
+                    blk_ref[1] == 1, rows_in[3][c, :, columns], rows_in[4][c, :, columns]
+                )
+            normed = (value.astype(f32) - mean_ref[c, place, :]) * inverse_ref[c, place, :]
+            gain_total = gain_total + jnp.sum(result[place] * normed, axis=0, keepdims=True)
+    gain_sum[...] = gain_total
+    shift_sum[...] = shift_total
+
+
+def project_back(blk, pieces, grads, weight, cuts):
     devices, halves, _, ch = grads.shape
     width, total = weight.shape
     block = min(512, width)
-    return pl.pallas_call(
-        functools.partial(project_back_kernel, heads=total // (3 * HD)),
+    part = ch // cuts
+    line = pl.BlockSpec((1, block), lambda step: (0, step))
+    rows, gain, shift, *out = pl.pallas_call(
+        functools.partial(project_back_kernel, pieces=len(pieces), heads=total // (3 * HD)),
         grid=(width // block,),
-        in_specs=[
-            smem,
-            whole(grads.shape),
-            pl.BlockSpec((block, total), lambda step: (step, 0)),
-        ],
-        out_specs=[
-            pl.BlockSpec((halves, ch, block), lambda step: (0, 0, step)),
-            whole((halves, ch, total)),
-        ],
+        in_specs=[smem]
+        + [whole(member.shape) for member in pieces]
+        + [whole(grads.shape), pl.BlockSpec((block, total), lambda step: (step, 0))],
+        out_specs=[whole((halves, ch, total)), line, line]
+        + [pl.BlockSpec((halves, part, block), lambda step: (0, 0, step))] * cuts,
         out_shape=[
-            jax.ShapeDtypeStruct((halves, ch, width), bf16),
             jax.ShapeDtypeStruct((halves, ch, total), bf16),
-        ],
-        compiler_params=compiler_params(32),
-        cost_estimate=pl.CostEstimate(
-            flops=2 * halves * ch * width * total,
-            bytes_accessed=2 * (grads.size + weight.size + halves * ch * (width + total)),
-            transcendentals=0,
-        ),
-    )(blk, grads, weight)
+            jax.ShapeDtypeStruct((1, width), f32),
+            jax.ShapeDtypeStruct((1, width), f32),
+        ]
+        + [jax.ShapeDtypeStruct((halves, part, width), bf16)] * cuts,
+        scratch_shapes=[pltpu.VMEM((halves, ch, 1), f32)] * 2,
+        compiler_params=compiler_params(40),
+        cost_estimate=light,
+    )(blk, *pieces, grads, weight)
+    return out, rows, gain, shift
 
 
 def attend_kernel(
@@ -471,9 +631,6 @@
         return unused
 
     lax.fori_loop(0, mine, query_tile, 0)
-
-
-vmem = pl.BlockSpec(memory_space=pltpu.VMEM)
 
 
 def attend(place, tiles, along, down, qkv):
@@ -494,11 +651,7 @@
             pltpu.VMEM((n, HD, 2 * ch), bf16),
         ],
         compiler_params=compiler_params(40),
-        cost_estimate=pl.CostEstimate(
-            flops=blocks * blocks * ch * ch * HD * 8,
-            bytes_accessed=blocks * ch * HD * 12,
-            transcendentals=blocks * blocks * ch * ch // 2,
-        ),
+        cost_estimate=heavy,
     )(place, tiles, along, down, qkv)
 
 
@@ -635,12 +788,222 @@
             pltpu.VMEM((n, 2 * ch, HD), f32),
         ],
         compiler_params=compiler_params(48),
-        cost_estimate=pl.CostEstimate(
-            flops=blocks * blocks * ch * ch * HD * 20,
-            bytes_accessed=blocks * ch * HD * 24,
-            transcendentals=blocks * blocks * ch * ch // 2,
+        cost_estimate=heavy,
+    )(place, tiles, along, down, qkv, grad, exact, lse, cosine, sine)
+
+
+def feed_kernel(order_ref, *refs, pieces):
+    rows_in, grads_in = refs[:pieces], refs[pieces]
+    gate_hbm, up_hbm, down_hbm = refs[pieces + 1 : pieces + 4]
+    hidden_ref, grad_gate_ref, grad_up_ref, rows_ref, grads_ref = refs[pieces + 4 : pieces + 9]
+    out_refs, (gate_w, up_w, down_w, sems) = refs[pieces + 9 : -4], refs[-4:]
+    pairs = ((gate_hbm, gate_w), (up_hbm, up_w), (down_hbm, down_w))
+    copies = [
+        pltpu.make_async_copy(source, target, sems.at[k])
+        for k, (source, target) in enumerate(pairs)
+    ]
+    for copy in copies:
+        copy.start()
+    halves, ch, _ = rows_ref.shape
+    count = order_ref.shape[0] - 1
+    step = ch // count
+    for c in range(halves):
+        for k, place in each_piece(rows_in):
+            rows_ref[c, place, :] = piece(rows_in, k, c, order_ref[0])
+        for k in range(count):
+            start = pl.multiple_of(order_ref[1 + k] * step, step)
+            grads_ref[c, k * step : (k + 1) * step, :] = grads_in[0, c, pl.ds(start, step), :]
+    for c in range(halves):
+        if c == 0:
+            copies[0].wait()
+        gate = dot(rows_ref[c], gate_w[...], 1, 0)
+        if c == 0:
+            copies[1].wait()
+        up_value = dot(rows_ref[c], up_w[...], 1, 0)
+        sigmoid_gate = jax.nn.sigmoid(gate)
+        silu_gate = gate * sigmoid_gate
+        hidden_ref[c] = (silu_gate * up_value).astype(bf16)
+        if c == 0:
+            copies[2].wait()
+        grad_hidden = dot(grads_ref[c], down_w[...], 1, 1)
+        grad_up = (grad_hidden * silu_gate).astype(bf16)
+        grad_gate = (
+            grad_hidden * up_value * sigmoid_gate * (1.0 + gate * (1.0 - sigmoid_gate))
+        ).astype(bf16)
+        grad_up_ref[c] = grad_up
+        grad_gate_ref[c] = grad_gate
+        summand = dot(grad_gate, gate_w[...], 1, 1) + dot(grad_up, up_w[...], 1, 1)
+        put_pieces(out_refs, c, summand.astype(bf16))
+
+
+def feed(order, rows, grads, sequence, gate_weight, up_weight, down_weight, cuts):
+    _, halves, ch, width = grads.shape
+    hidden = gate_weight.shape[1]
+    inner = jax.ShapeDtypeStruct((halves, ch, hidden), bf16)
+    outer = jax.ShapeDtypeStruct((halves, ch, width), bf16)
+    cut = jax.ShapeDtypeStruct((halves, ch // cuts, width), bf16)
+    anywhere = pl.BlockSpec(memory_space=pl.ANY)
+    weights = (gate_weight, up_weight, down_weight)
+    hidden, grad_gate, grad_up, rows, grads, *out = pl.pallas_call(
+        functools.partial(feed_kernel, pieces=len(rows)),
+        grid=(1,),
+        in_specs=[smem]
+        + [whole(member.shape) for member in rows]
+        + [pl.BlockSpec((1, halves, ch, width), lambda step: (sequence, 0, 0, 0))]
+        + [anywhere] * 3,
+        out_specs=[whole(inner.shape)] * 3 + [whole(outer.shape)] * 2 + [whole(cut.shape)] * cuts,
+        out_shape=[inner] * 3 + [outer] * 2 + [cut] * cuts,
+        scratch_shapes=[pltpu.VMEM(weight.shape, bf16) for weight in weights]
+        + [pltpu.SemaphoreType.DMA((3,))],
+        compiler_params=compiler_params(58),
+        cost_estimate=heavy,
+    )(order, *rows, grads, *weights)
+    return hidden, grad_gate, grad_up, out, rows, grads
+
+
+def weight_grad_kernel(*refs, pairs):
+    total = dot(refs[0][...], refs[1][...], 0, 0)
+    for k in range(1, pairs):
+        total = total + dot(refs[2 * k][...], refs[2 * k + 1][...], 0, 0)
+    refs[-1][...] = total.astype(bf16)
+
+
+def weight_grad(lefts, rights, cost=light):
+    lefts = [member.reshape(-1, member.shape[-1]) for member in lefts]
+    rights = [member.reshape(-1, member.shape[-1]) for member in rights]
+    rows, height = lefts[0].shape
+    width = rights[0].shape[1]
+    if height > width:
+        block = min(512, height)
+        steps = height // block
+        specs = [
+            pl.BlockSpec((rows, block), lambda step: (0, step)),
+            pl.BlockSpec((rows, width), lambda step: (0, 0)),
+        ]
+        out = pl.BlockSpec((block, width), lambda step: (step, 0))
+    else:
+        block = min(512, width)
+        steps = width // block
+        specs = [
+            pl.BlockSpec((rows, height), lambda step: (0, 0)),
+            pl.BlockSpec((rows, block), lambda step: (0, step)),
+        ]
+        out = pl.BlockSpec((height, block), lambda step: (0, step))
+    return pl.pallas_call(
+        functools.partial(weight_grad_kernel, pairs=len(lefts)),
+        grid=(steps,),
+        in_specs=specs * len(lefts),
+        out_specs=out,
+        out_shape=jax.ShapeDtypeStruct((height, width), bf16),
+        compiler_params=compiler_params(48),
+        cost_estimate=cost,
+    )(*[member for pair in zip(lefts, rights) for member in pair])
+
+
+def split_grad_kernel(at_ref, *refs, pairs, by_rows, added):
+    total = dot(refs[0][...], refs[1][...], 0, 0)
+    for k in range(1, pairs):
+        total = total + dot(refs[2 * k][...], refs[2 * k + 1][...], 0, 0)
+    keep_ref, send_ref = refs[-2:]
+    size = keep_ref.shape[1 if by_rows else 2]
+    if by_rows:
+        first, second = total[:size], total[size:]
+    else:
+        first, second = total[:, :size], total[:, size:]
+    low = at_ref[1] == 0
+    keep, send = jnp.where(low, first, second), jnp.where(low, second, first)
+    if added:
+        keep = keep + refs[2 * pairs][0].astype(f32)
+        send = send + refs[2 * pairs + 1][0].astype(f32)
+    keep_ref[0] = keep.astype(bf16)
+    send_ref[0] = send.astype(bf16)
+
+
+def split_grad(at, lefts, rights, planes, earlier=()):
+    lefts = [member.reshape(-1, member.shape[-1]) for member in lefts]
+    rights = [member.reshape(-1, member.shape[-1]) for member in rights]
+    rows, height = lefts[0].shape
+    width = rights[0].shape[1]
+    by_rows = height > width
+    if by_rows:
+        block = height // planes
+        specs = [
+            pl.BlockSpec((rows, block), lambda step, at: (0, step)),
+            pl.BlockSpec((rows, width), lambda step, at: (0, 0)),
+        ]
+        part = (block // 2, width)
+    else:
+        block = width // planes
+        specs = [
+            pl.BlockSpec((rows, height), lambda step, at: (0, 0)),
+            pl.BlockSpec((rows, block), lambda step, at: (0, step)),
+        ]
+        part = (height, block // 2)
+    out = pl.BlockSpec((1,) + part, lambda step, at: (step ^ at[0], 0, 0))
+    shape = jax.ShapeDtypeStruct((planes,) + part, bf16)
+    return pl.pallas_call(
+        functools.partial(
+            split_grad_kernel, pairs=len(lefts), by_rows=by_rows, added=len(earlier) > 0
         ),
-    )(place, tiles, along, down, qkv, grad, exact, lse, cosine, sine)
+        grid_spec=pltpu.PrefetchScalarGridSpec(
+            num_scalar_prefetch=1,
+            grid=(planes,),
+            in_specs=specs * len(lefts) + [out] * len(earlier),
+            out_specs=[out, out],
+        ),
+        out_shape=[shape, shape],
+        compiler_params=compiler_params(48),
+        cost_estimate=light,
+    )(at, *[member for pair in zip(lefts, rights) for member in pair], *earlier)
+
+
+def split_first(keep, send):
+    other = paired(send, "core", 1)
+    return [
+        (keep[k].astype(f32) + other[k].astype(f32)).astype(bf16) for k in range(keep.shape[0])
+    ]
+
+
+def split_rest(sums):
+    return sums[:1] + [paired(sums[step], "plane", step) for step in range(1, len(sums))]
+
+
+def split_whole(sums):
+    total = sums[0].astype(f32)
+    for member in sums[1:]:
+        total = total + member.astype(f32)
+    return total
+
+
+def feed_out_kernel(order_ref, *refs):
+    hidden, weight_ref, out_ref = refs[:-2], refs[-2], refs[-1]
+    halves, ch, _ = hidden[0].shape
+    count = order_ref.shape[0] - 1
+    step = ch // count
+    for s, ref in enumerate(hidden):
+        for c in range(halves):
+            result = dot(ref[c], weight_ref[...], 1, 0).astype(bf16)
+            for k in range(count):
+                start = pl.multiple_of(order_ref[1 + k] * step, step)
+                out_ref[s * halves + c, pl.ds(start, step), :] = result[k * step : (k + 1) * step]
+
+
+def feed_out(order, hidden, weight):
+    halves, ch, _ = hidden[0].shape
+    inner, width = weight.shape
+    block = min(512, width)
+    count = len(hidden) * halves
+    return pl.pallas_call(
+        feed_out_kernel,
+        grid=(width // block,),
+        in_specs=[smem]
+        + [whole(member.shape) for member in hidden]
+        + [pl.BlockSpec((inner, block), lambda step: (0, step))],
+        out_specs=pl.BlockSpec((count, ch, block), lambda step: (0, 0, step)),
+        out_shape=jax.ShapeDtypeStruct((count, ch, width), bf16),
+        compiler_params=compiler_params(40),
+        cost_estimate=light,
+    )(order, *hidden, weight)
 
 
 def local(
@@ -669,6 +1032,10 @@
     blk = lax.axis_index("plane") * 2 + lax.axis_index("core")
     head_index = lax.axis_index("head")
     blk_scalar = blk.astype(jnp.int32).reshape(1)
+    ends = ends_chain().reshape(1)
+    cuts = head_size if in_chain() else 1
+    where = jnp.concatenate([blk_scalar, ends])
+    order = jnp.concatenate([ends, head_order()])
     ch = part_rows * head_size
     blocks = halves * devices
     heads = query_bias.shape[0]
@@ -700,13 +1067,16 @@
     if copies == 1:
         tiles = jnp.arange(tile_count, dtype=jnp.int32)
 
+    core = lax.axis_index("core").astype(jnp.int32)
+    at = jnp.stack([lax.axis_index("plane").astype(jnp.int32), core])
+
     full_qkv = blk_gather(jnp.concatenate([query_weight, key_weight, value_weight], axis=1))
     full_out = blk_gather(out_weight, 1)
 
     def split_small(small):
-        small = small_gather(in_head_order(small[0], 0), BLK).astype(f32)
+        small = small_gather(in_head_order(gather_whole(small)[0], 0), BLK).astype(f32)
         gain_one, shift_one, gain_two, shift_two = [
-            small[:, k * part : (k + 1) * part].reshape(-1) for k in range(4)
+            small[:, k * part : (k + 1) * part].reshape(1, -1) for k in range(4)
         ]
         biases = lax.dynamic_index_in_dim(
             small[:, 4 * part :].reshape(devices, head_size, -1), head_index, 1, keepdims=False
@@ -725,58 +1095,20 @@
     each = range(seqs)
     inputs = [layer_input[s, 0] for s in each]
     grad_own = [out_grad[s, 0] for s in each]
-    rows_in = [member.astype(f32) for member in inputs]
-
-    def norm_one(whole_rows):
-        return normalize(whole_rows.astype(f32), gain_one, shift_one).astype(bf16)
-
-    def norm_one_sums(whole_rows, summand):
-        value = whole_rows.astype(f32)
-        upstream = summand.astype(f32)
-        center = value - jnp.mean(value, axis=-1, keepdims=True)
-        inverse = lax.rsqrt(jnp.mean(center * center, axis=-1, keepdims=True) + epsilon)
-        return jnp.sum(upstream * (center * inverse), axis=(0, 1)), jnp.sum(upstream, axis=(0, 1))
-
-    def queries_of(rows):
-        return project_in(blk_scalar, rows, full_qkv, bias, cos_own, sin_own, devices)
+
+    def queries_of(pieces):
+        return project_in(
+            where, pieces, gain_one, shift_one, full_qkv, bias, cos_own, sin_own, devices
+        )
+
+    def move_first(value, rows):
+        return exchange_first(value.reshape(devices, halves, rows, ch))
 
     def move(value, rows):
-        return exchange(value.reshape(devices, halves, rows, ch))
-
-    def norm_two(value):
-        return normalize(value, gain_two, shift_two).astype(bf16)
+        return exchange_rest(move_first(value, rows))
 
     def flat(member):
         return member.reshape(-1, member.shape[-1])
-
-    def feed_first(rows, grad):
-        gate = dot(flat(rows), full_gate, 1, 0)
-        up_value = dot(flat(rows), full_up, 1, 0)
-        sigmoid_gate = jax.nn.sigmoid(gate)
-        silu_gate = gate * sigmoid_gate
-        hidden = (silu_gate * up_value).astype(bf16)
-        grad_hidden = dot(flat(grad), full_down, 1, 1)
-        grad_up = (grad_hidden * silu_gate).astype(bf16)
-        grad_gate = (
-            grad_hidden * up_value * sigmoid_gate * (1.0 + gate * (1.0 - sigmoid_gate))
-        ).astype(bf16)
-        return hidden, grad_gate, grad_up
-
-    def feed_back(grad_gate, grad_up):
-        summand = dot(grad_gate, full_gate, 1, 1) + dot(grad_up, full_up, 1, 1)
-        return summand.astype(bf16).reshape(halves, ch, width)
-
-    def feed_out(hidden):
-        return dot(hidden, full_down, 1, 0).astype(bf16).reshape(halves, ch, width)
-
-    def back_two(s, parts, middle):
-        back, gain_grad, shift_grad = norm_back(middle, gain_two, scatter_whole(parts))
-        grad = grad_own[s].astype(f32) + back
-        return grad, grad.astype(bf16), (gain_grad, shift_grad)
-
-    def back_one(s, parts, grad_middle):
-        back, _, _ = norm_back(rows_in[s], gain_one, scatter_whole(parts))
-        return grad_middle + back
 
     def attend_of(qkv):
         return attend(place, tiles, along, down, qkv.reshape(blocks, 3 * HD, ch))
@@ -787,134 +1119,133 @@
         qkv = qkv.reshape(blocks, 3 * HD, ch)
         return attend_back(place, tiles, along, down, qkv, grad, exact, lse, cos_all, sin_all)
 
-    def weight_grad(lefts, rights):
-        total = dot(flat(lefts[0]), flat(rights[0]), 0, 0)
-        for left, right in zip(lefts[1:], rights[1:]):
-            total = total + dot(flat(left), flat(right), 0, 0)
-        return total.astype(bf16)
-
     stage = lax.optimization_barrier
     in_a, in_b = inputs
-    small = small[None, None]
-    got, got_small = gather_first(in_a), gather_first(small)
-    in_a, small, got, got_small, in_b = stage((in_a, small, got, got_small, in_b))
-    parts, small = gather_rest(in_a, got), gather_rest(small, got_small)
-    parts, small, in_b = stage((parts, small, in_b))
+    grad_own_a, grad_own_b = grad_own
+    small = gather_direct(small[None, None])
+    got = gather_first(in_a)
+    in_a, got, in_b, small = stage((in_a, got, in_b, small))
+    parts = gather_rest(in_a, got)
+    parts, in_b, cos_own, sin_own, (gain_one, shift_one, gain_two, shift_two, bias) = stage(
+        (parts, in_b, cos_own, sin_own, split_small(small))
+    )
+    x_a = gather_pieces(parts)
     got = gather_first(in_b)
-    x_a = gather_whole(parts)
-    gain_one, shift_one, gain_two, shift_two, bias = split_small(gather_whole(small))
-    one_a = norm_one(x_a)
-    qkv_a = queries_of(one_a)
-    got, in_b, x_a, one_a, qkv_a, own_grads = stage((got, in_b, x_a, one_a, qkv_a, out_grad))
-    grads = lax.all_gather(own_grads[:, 0], "head", axis=2, tiled=True)
+    qkv_a, one_a = queries_of(x_a)
+    got, in_b, x_a, one_a, qkv_a = stage((got, in_b, x_a, one_a, qkv_a))
     parts = gather_rest(in_b, got)
     qkv_a = move(qkv_a, 3 * HD)
-    parts, qkv_a, late = stage((parts, qkv_a, (gate_weight, up_weight, down_weight)))
+    parts, own_grads = stage((parts, out_grad))
+    grads = lax.all_gather(own_grads[:, 0], "head", axis=2, tiled=True)
+    x_b = gather_pieces(parts)
+    made, one_b = queries_of(x_b)
+    qkv_a, x_b, one_b, made, late = stage(
+        (qkv_a, x_b, one_b, made, (gate_weight, up_weight, down_weight))
+    )
     full_gate, full_up, full_down = blk_gather(late[0]), blk_gather(late[1]), blk_gather(late[2], 1)
-    x_b = gather_whole(parts)
-    one_b = norm_one(x_b)
-    qkv_b = move(queries_of(one_b), 3 * HD)
+    made = move_first(made, 3 * HD)
+    made, qkv_a = stage((made, qkv_a))
+    qkv_b = exchange_rest(made)
     att_a = attend_of(qkv_a)
-    x_b, one_b, qkv_b, att_a = stage((x_b, one_b, qkv_b, att_a))
+    qkv_b, att_a = stage((qkv_b, att_a))
     att = move(att_a[0], HD)
     att, qkv_b = stage((att, qkv_b))
-    partial, out_a = project_out(blk_scalar, att, full_out)
+    partial, out_a = project_out(blk_scalar, att, full_out, cuts)
     sums = scatter_first(partial)
     att_b = attend_of(qkv_b)
     sums, att_b, out_a = stage((sums, att_b, out_a))
     sums = scatter_rest(sums)
     att = move(att_b[0], HD)
-    partial, out_b = project_out(blk_scalar, att, full_out)
+    partial, out_b = project_out(blk_scalar, att, full_out, cuts)
     sums, partial, out_b = stage((sums, partial, out_b))
-    middle_a = rows_in[0] + scatter_whole(sums)
-    normed = norm_two(middle_a)
+    middle_a, normed = middle_of(scatter_pieces(sums), in_a, gain_two, shift_two)
     got = gather_first(normed)
     sums = scatter_first(partial)
-    got, sums, normed, middle_a, grads = stage((got, sums, normed, middle_a, grads))
+    got, sums, normed, middle_a = stage((got, sums, normed, middle_a))
     parts = gather_rest(normed, got)
     sums = scatter_rest(sums)
-    grads = in_head_order(grads, 2)
-    parts, sums, (grad_a, grad_b) = stage((parts, sums, (grads[0], grads[1])))
-    middle_b = rows_in[1] + scatter_whole(sums)
-    normed = norm_two(middle_b)
+    parts, sums = stage((parts, sums))
+    middle_b, normed = middle_of(scatter_pieces(sums), in_b, gain_two, shift_two)
     got = gather_first(normed)
-    two_a = gather_whole(parts)
-    hid_a, gate_a, up_a = feed_first(two_a, grad_a)
-    got, normed, middle_b, two_a, hid_a, gate_a, up_a = stage(
-        (got, normed, middle_b, two_a, hid_a, gate_a, up_a)
-    )
+    feeding = feed(
+        order, gather_pieces(parts), grads, 0, full_gate, full_up, full_down, cuts
+    )
+    got, normed, middle_b, feeding = stage((got, normed, middle_b, feeding))
+    hid_a, gate_a, up_a, partial, two_a, og_a = feeding
+    sums = scatter_first(partial)
     parts = gather_rest(normed, got)
-    partial = feed_back(gate_a, up_a)
-    parts, partial, hid_a, gate_a, up_a = stage((parts, partial, hid_a, gate_a, up_a))
-    sums = scatter_first(partial)
-    two_b = gather_whole(parts)
-    hid_b, gate_b, up_b = feed_first(two_b, grad_b)
-    sums, two_b, hid_b, gate_b, up_b = stage((sums, two_b, hid_b, gate_b, up_b))
+    parts, sums = stage((parts, sums))
     sums = scatter_rest(sums)
-    partial = feed_back(gate_b, up_b)
-    sums, partial, hid_a, hid_b, gate_b, up_b, two_b = stage(
-        (sums, partial, hid_a, hid_b, gate_b, up_b, two_b)
-    )
-    mid_grad_a, branch_a, norm_grads_two_a = back_two(0, sums, middle_a)
+    feeding = feed(
+        order, gather_pieces(parts), grads, 1, full_gate, full_up, full_down, cuts
+    )
+    sums, feeding, hid_a = stage((sums, feeding, hid_a))
+    hid_b, gate_b, up_b, partial, two_b, og_b = feeding
+    mid_grad_a, branch_a, gain_two_a, shift_two_a = back_two(
+        scatter_pieces(sums), middle_a, grad_own_a, gain_two
+    )
     got = gather_first(branch_a)
     sums = scatter_first(partial)
-    down_grad = weight_grad((hid_a, hid_b), (grad_a, grad_b))
-    feeds = jnp.concatenate([feed_out(hid_a), feed_out(hid_b)])
-    got, sums, down_grad, feeds, branch_a, mid_grad_a, gate_a, up_a = stage(
-        (got, sums, down_grad, feeds, branch_a, mid_grad_a, gate_a, up_a)
+    down_grad = weight_grad((hid_a, hid_b), (og_a, og_b))
+    got, sums, down_grad, branch_a, mid_grad_a, gate_a, up_a, hid_a = stage(
+        (got, sums, down_grad, branch_a, mid_grad_a, gate_a, up_a, hid_a)
     )
     down_grad = blk_scatter(down_grad, 1)
     parts = gather_rest(branch_a, got)
     sums = scatter_rest(sums)
     gate_grad = weight_grad((two_a, two_b), (gate_a, gate_b))
+    gate_grad, up_a = stage((gate_grad, up_a))
     up_grad = weight_grad((two_a, two_b), (up_a, up_b))
-    parts, sums, gate_grad, up_grad, feeds = stage((parts, sums, gate_grad, up_grad, feeds))
+    up_grad, hid_a = stage((up_grad, hid_a))
+    feeds = feed_out(order, (hid_a, hid_b), full_down)
+    parts, sums, gate_grad, feeds, up_grad = stage((parts, sums, gate_grad, feeds, up_grad))
     gate_grad = blk_scatter(gate_grad)
+    mid_grad_b, branch_b, gain_two_b, shift_two_b = back_two(
+        scatter_pieces(sums), middle_b, grad_own_b, gain_two
+    )
+    branch_b, parts, mid_grad_b = stage((branch_b, parts, mid_grad_b))
+    got = gather_direct(branch_b)
+    att_grad_a, whole_a = project_grad(where, gather_pieces(parts), full_out, devices, ch)
+    att_grad_a = move(att_grad_a, HD)
+    branch_b, mid_grad_b, whole_a, att_grad_a, feeds, up_grad = stage(
+        (branch_b, mid_grad_b, whole_a, att_grad_a, feeds, up_grad)
+    )
+    feeds = lax.psum_scatter(feeds, "head", scatter_dimension=1, tiled=True)
+    made_a, bias_sums_a = attend_back_of(qkv_a, att_a, att_grad_a)
+    got, made_a, whole_a, up_grad = stage((got, made_a, whole_a, up_grad))
+    att_grad_b, whole_b = project_grad(where, gather_pieces(got), full_out, devices, ch)
+    att_grad_b = move_first(att_grad_b, HD)
+    moved = move_first(made_a, 3 * HD)
+    att_grad_b, moved, whole_b = stage((att_grad_b, moved, whole_b))
+    att_grad_b = exchange_rest(att_grad_b)
+    out_weight_grad = weight_grad((out_a, out_b), (whole_a, whole_b))
+    moved, att_grad_b, up_grad, out_weight_grad = stage(
+        (moved, att_grad_b, up_grad, out_weight_grad)
+    )
+    moved = exchange_rest(moved)
+    made_b, bias_sums_b = attend_back_of(qkv_b, att_b, att_grad_b)
+    moved, made_b, out_weight_grad, up_grad = stage((moved, made_b, out_weight_grad, up_grad))
     up_grad = blk_scatter(up_grad)
-    mid_grad_b, branch_b, norm_grads_two_b = back_two(1, sums, middle_b)
-    got = gather_first(branch_b)
-    whole_a = gather_whole(parts)
-    att_grad_a = move(project_grad(blk_scalar, whole_a, full_out, devices), HD)
-    got, branch_b, mid_grad_b, whole_a, att_grad_a, feeds = stage(
-        (got, branch_b, mid_grad_b, whole_a, att_grad_a, feeds)
-    )
-    parts = gather_rest(branch_b, got)
-    feeds = scatter_first(feeds)
-    made_a, bias_sums_a = attend_back_of(qkv_a, att_a, att_grad_a)
-    parts, feeds, made_a, whole_a = stage((parts, feeds, made_a, whole_a))
-    whole_b = gather_whole(parts)
-    att_grad_b = move(project_grad(blk_scalar, whole_b, full_out, devices), HD)
-    out_weight_grad = weight_grad((out_a, out_b), (whole_a, whole_b))
-    feeds, made_a, att_grad_b, out_weight_grad, down_grad = stage(
-        (feeds, made_a, att_grad_b, out_weight_grad, down_grad)
-    )
     out_weight_grad = blk_scatter(out_weight_grad, 1)
-    feeds = scatter_rest(feeds)
-    moved = move(made_a, 3 * HD)
-    made_b, bias_sums_b = attend_back_of(qkv_b, att_b, att_grad_b)
-    feeds, moved, made_b = stage((feeds, moved, made_b))
-    partial_a, qkv_rows_a = project_back(blk_scalar, moved, full_qkv)
-    sums = scatter_first(partial_a)
-    moved = move(made_b, 3 * HD)
-    feeds = scatter_whole(feeds)
-    layer_output = (middle_a + feeds[:halves], middle_b + feeds[halves:])
-    sums, moved, partial_a, qkv_rows_a, layer_output, gate_grad = stage(
-        (sums, moved, partial_a, qkv_rows_a, layer_output, gate_grad)
-    )
-    partial_b, qkv_rows_b = project_back(blk_scalar, moved, full_qkv)
-    sums_b = scatter_first(partial_b)
-    sums = scatter_rest(sums)
-    qkv_grad = weight_grad((one_a, one_b), (qkv_rows_a, qkv_rows_b))
-    norm_grads_one_a = norm_one_sums(x_a, partial_a)
-    sums, sums_b, partial_b, qkv_grad, norm_grads_one_a = stage(
-        (sums, sums_b, partial_b, qkv_grad, norm_grads_one_a)
-    )
-    qkv_grad = blk_scatter(qkv_grad)
+    moved_b = move_first(made_b, 3 * HD)
+    moved, moved_b, down_grad, gate_grad = stage((moved, moved_b, down_grad, gate_grad))
+    down_grad, gate_grad = down_grad.astype(f32), gate_grad.astype(f32)
+    moved_b = exchange_rest(moved_b)
+    partial, qkv_rows_a, gain_one_a, shift_one_a = project_back(where, x_a, moved, full_qkv, cuts)
+    sums_a = scatter_first(partial)
+    moved_b, sums_a, down_grad, gate_grad, feeds = stage(
+        (moved_b, sums_a, down_grad, gate_grad, feeds)
+    )
+    partial, qkv_rows_b, gain_one_b, shift_one_b = project_back(where, x_b, moved_b, full_qkv, cuts)
+    partial, qkv_rows_b, sums_a = stage((partial, qkv_rows_b, sums_a))
+    sums_a = scatter_rest(sums_a)
+    sums_b = scatter_first(partial)
+    qkv_split = split_grad(at, (one_a, one_b), (qkv_rows_a, qkv_rows_b), planes)
+    sums_a, sums_b, qkv_split = stage((sums_a, sums_b, qkv_split))
     sums_b = scatter_rest(sums_b)
-    norm_grads_one_b = norm_one_sums(x_b, partial_b)
-    input_grad = (back_one(0, sums, mid_grad_a), back_one(1, sums_b, mid_grad_b))
-    norm_one_grads = (norm_grads_one_a, norm_grads_one_b)
-    norm_two_grads = (norm_grads_two_a, norm_grads_two_b)
+
+    norm_one_grads = ((gain_one_a, shift_one_a), (gain_one_b, shift_one_b))
+    norm_two_grads = ((gain_two_a, shift_two_a), (gain_two_b, shift_two_b))
     bias_sums = (bias_sums_a, bias_sums_b)
 
     def over_all(grads, k):
@@ -950,13 +1281,27 @@
         ],
         axis=1,
     )
-    smalls = small_scatter(smalls)
+    smalls = small_scatter(smalls.reshape(devices, head_size, -1), BLK)
+    qkv_split = split_first(*qkv_split)
+    qkv_split = split_rest(qkv_split)
+    input_grad_a = back_one(scatter_pieces(sums_a), in_a, mid_grad_a, gain_one)
+    feeds = feeds.astype(f32)
+    layer_output = jnp.stack([middle_a + feeds[:halves], middle_b + feeds[halves:]])[:, None]
+    sums_b, smalls, input_grad_a, qkv_split, layer_output, out_weight_grad = stage(
+        (sums_b, smalls, input_grad_a, qkv_split, layer_output, out_weight_grad)
+    )
+    up_grad = up_grad.astype(f32)
+    smalls = small_scatter(smalls, ALL[2:])
+    qkv_grad = split_whole(qkv_split)
+    out_weight_grad = out_weight_grad.astype(f32)
+
     norm_grads = [smalls[k * part : (k + 1) * part] for k in range(4)]
     bias_grads = smalls[4 * part :].reshape(heads, 2 * q_dims + k_dims)
-    stacked = lambda members: jnp.stack(members)[:, None]
+    input_grad_b = back_one(scatter_pieces(sums_b), in_b, mid_grad_b, gain_one)
+    input_grad = jnp.stack([input_grad_a, input_grad_b])[:, None]
     return (
-        stacked(layer_output),
-        stacked(input_grad),
+        layer_output,
+        input_grad,
         norm_grads[0],
         norm_grads[1],
         qkv_grad[:, :local_width],

time: 820 us -> 813 us (level)
  Pallas kernels: 138 us -> 272 us
  matrix products: 127 us -> 0 us
  other arithmetic: 97.2 us -> 31.8 us
  starting transfers between devices: 132 us -> 164 us
  local copies, waits for them, and re-layouts: 47.8 us -> 72.6 us
    pallas_call x6 -> x20, Pallas kernels: 21.1 us -> 155 us  [the longest x2 48.1 us: feed(): pl.pallas_call(functools.partial(feed_kernel, pieces=len(rows)), grid=(1,...]
    dot_general x22 -> x0, matrix products: 127 us -> none  [dot(): lax.dot_general(left, right, (((left_axis,), (right_axis,)), ((), ())), p...]
    unnamed x246 -> x268, local copies, waits for them, and re-layouts: 19.1 us -> 53.4 us
    reduce_sum x22 -> x0, other arithmetic: 33.4 us -> none  [the longest x3 6.31 us: normalize(): center = value - jnp.mean(value, axis=-1, keepdims=True)]
    reduce_scatter x5, waiting for transfers between devices: 5.02 us -> 35.2 us  [the longest x4 35.2 us: blk_scatter(): return lax.psum_scatter(value, BLK, scatter_dimension=axis, tiled=True)]
    ppermute x7 -> x6, starting transfers between devices: 13.8 us -> 41.4 us  [scatter_rest(): lax.ppermute(passed, 'head', TWO)]
    ppermute x40 -> x44, waiting for transfers between devices: 67.3 us -> 41.7 us  [paired(): lax.ppermute(value, axis, [(source, source ^ step) for source in range(co...]
    ppermute x7 -> x6, waiting for transfers between devices: 73.5 us -> 49.6 us  [scatter_rest(): lax.ppermute(passed, 'head', TWO)]
  transfers between devices with their start and end apart: 107 -> 105, of which waited for: 43 -> 36; matrix products, arithmetic and copies ran while one was open for 30% -> 6% of each run, Pallas kernels for 17% -> 34%
where the time goes in v3:
time: 813 us; the launch traced here: 803 us
  Pallas kernels  272 us (33%)
  waiting for transfers between devices  239 us (29%)
  starting transfers between devices  164 us (20%)
  local copies, waits for them, and re-layouts  72.6 us (9%)
  other arithmetic  31.8 us (4%)
  between operations  24.1 us (3%)
    pallas_call x2, Pallas kernels, attend_back(): pl.pallas_call(attend_back_kernel, in_specs=[smem, smem] + [vmem] * 8, ou...  64.2 us
    unnamed x268, local copies, waits for them, and re-layouts  53.4 us
    ppermute x6, waiting for transfers between devices, scatter_rest(): lax.ppermute(passed, 'head', TWO)  49.6 us
    pallas_call x2, Pallas kernels, attend(): pl.pallas_call(attend_kernel, in_specs=[smem, smem] + [vmem] * 3, out_spe...  48.6 us
    pallas_call x2, Pallas kernels, feed(): pl.pallas_call(functools.partial(feed_kernel, pieces=len(rows)), grid=(1,...  48.1 us
    ppermute x10, waiting for transfers between devices, gather_first(): return (lax.ppermute(value, 'head', TWO), lax.ppermute(value, 'head', ONE))  42.3 us
    ppermute x44, starting transfers between devices, paired(): lax.ppermute(value, axis, [(source, source ^ step) for source in range(co...  42.1 us
    ppermute x44, waiting for transfers between devices, paired(): lax.ppermute(value, axis, [(source, source ^ step) for source in range(co...  41.7 us
  transfers between devices with their start and end apart: 105, of which 36 were waited for; matrix products, arithmetic and copies ran while one was open for 6% of the time, Pallas kernels for 34%

profile of v3, /device:TPU:0, one launch (start us, length us, event | category | flops | bytes accessed | tf_op | source)
XLA Modules:
  0.0 802.7 jit_solution(18059747782686806850)
XLA Ops:
  48.7 11.3 %collective-permute-done.5.refs_3_ = bf16[2,64,2048]{2,1,0:T(8,128)(2,1)S(1)} collective-permute-done((bf16[2,64,2048]{2,1,0:T(8,128)(2,1)S(1)}, bf16[2,64,2048]{2,1,0:T(8,128)(2,1)S(1)}, u32[]{:S(2)}, u32[]{:S(2)}) %collective-permute-start.5) | collective-permute-done | bytes 524320 | tf_op jit(solution)/shard_map/ppermute | solution.py:128
  74.7 11.0 %collective-permute-done.10.refs_2_ = bf16[2,64,2048]{2,1,0:T(8,128)(2,1)} collective-permute-done((bf16[2,64,2048]{2,1,0:T(8,128)(2,1)S(1)}, bf16[2,64,2048]{2,1,0:T(8,128)(2,1)}, u32[]{:S(2)}, u32[]{:S(2)}) %collective-permute-start.10) | collective-permute-done | bytes 524320 | tf_op jit(solution)/shard_map/ppermute | solution.py:117
  87.7 12.5 %collective-permute-done.16.refs_3_ = bf16[2,64,2048]{2,1,0:T(8,128)(2,1)S(1)} collective-permute-done((bf16[2,64,2048]{2,1,0:T(8,128)(2,1)}, bf16[2,64,2048]{2,1,0:T(8,128)(2,1)S(1)}, u32[]{:S(2)}, u32[]{:S(2)}) %collective-permute-start.16) | collective-permute-done | bytes 524320 | tf_op jit(solution)/shard_map/ppermute | solution.py:128
  108.2 9.5 %shard_map.289 = (bf16[8,2,192,256]{3,2,1,0:T(8,128)(2,1)S(1)}, bf16[2,256,2048]{2,1,0:T(8,128)(2,1)}) custom-call(s32[2]{0:T(128)S(1)} %pad_add_fusion.1.blk_ref, bf16[2,64,2048]{2,1,0:T(8,128)(2,1)S(1)} %get-tuple-element.357.refs_0_.refs_4_, bf16[2,64,2048]{2,1,0:T(8,128)(2,1)} %collective-permute-done.11.refs_1_, ...), custom_call_target="tpu_custom_call" | custom-call | flops 1000 | bytes 1000 | tf_op jit(solution)/shard_map/pallas_call | solution.py:299
  136.2 24.3 %shard_map.290 = (bf16[16,64,256]{2,1,0:T(8,128)(2,1)S(1)}, f32[16,64,256]{2,1,0:T(8,128)S(1)}, f32[16,1,256]{2,1,0:T(1,128)S(1)}) custom-call(s32[16]{0:T(128)S(1)} %scatter_custom_fusion.place_ref, s32[8]{0:T(128)S(1)} %iota.54.tiles_ref, s32[1,512]{1,0:T(1,128)S(1)} %bitcast.331, s32[512,1]{1,0:T(8,128)S(1)} %bitcast.326, bf16[16,192,256]{2,1,0:T(8,128)(2,1)S(1)} %bitcast.302), custom_call_target="tpu_custom_call" | custom-call | flops 30000001024 | bytes 1000 | tf_op jit(solution)/shard_map/pallas_call | solution.py:639
  182.9 24.3 %shard_map.292 = (bf16[16,64,256]{2,1,0:T(8,128)(2,1)S(1)}, f32[16,64,256]{2,1,0:T(8,128)S(1)}, f32[16,1,256]{2,1,0:T(1,128)S(1)}) custom-call(s32[16]{0:T(128)S(1)} %scatter_custom_fusion.place_ref, s32[8]{0:T(128)S(1)} %iota.56.tiles_ref, s32[1,512]{1,0:T(1,128)S(1)} %bitcast.332, s32[512,1]{1,0:T(8,128)S(1)} %bitcast.327, bf16[16,192,256]{2,1,0:T(8,128)(2,1)S(1)} %bitcast.300), custom_call_target="tpu_custom_call" | custom-call | flops 30000001024 | bytes 1000 | tf_op jit(solution)/shard_map/pallas_call | solution.py:639
  249.5 16.3 %collective-permute-done.34.refs_2_ = bf16[2,64,2048]{2,1,0:T(8,128)(2,1)S(1)} collective-permute-done((bf16[2,64,2048]{2,1,0:T(8,128)(2,1)S(1)}, bf16[2,64,2048]{2,1,0:T(8,128)(2,1)S(1)}, u32[]{:S(2)}, u32[]{:S(2)}) %collective-permute-start.34) | collective-permute-done | bytes 524320 | tf_op jit(solution)/shard_map/ppermute | solution.py:117
  290.2 23.4 %collective-permute-done.40.refs_1_ = bf16[2,64,2048]{2,1,0:T(8,128)(2,1)S(1)} collective-permute-done((bf16[2,64,2048]{2,1,0:T(8,128)(2,1)S(1)}, bf16[2,64,2048]{2,1,0:T(8,128)(2,1)S(1)}, u32[]{:S(2)}, u32[]{:S(2)}) %collective-permute-start.40) | collective-permute-done | bytes 524320 | tf_op jit(solution)/shard_map/ppermute | solution.py:177
  322.7 24.0 %shard_map.296 = (bf16[2,256,1408]{2,1,0:T(8,128)(2,1)}, bf16[2,256,1408]{2,1,0:T(8,128)(2,1)}, bf16[2,256,1408]{2,1,0:T(8,128)(2,1)}, bf16[2,256,2048]{2,1,0:T(...) custom-call(s32[5]{0:T(128)} %pad_add_fusion.2.order_ref, ...), custom_call_target="tpu_custom_call" | custom-call | flops 30000001024 | bytes 1000 | tf_op jit(solution)/shard_map/pallas_call | solution.py:847
  352.8 9.2 %collective-permute-done.46 = bf16[2,64,2048]{2,1,0:T(8,128)(2,1)S(1)} collective-permute-done((bf16[2,64,2048]{2,1,0:T(8,128)(2,1)}, bf16[2,64,2048]{2,1,0:T(8,128)(2,1)S(1)}, u32[]{:S(2)}, u32[]{:S(2)}) %collective-permute-start.46) | collective-permute-done | bytes 524320 | tf_op jit(solution)/shard_map/ppermute | solution.py:162
  366.9 15.8 %collective-permute-start.48 = (bf16[2,64,2048]{2,1,0:T(8,128)(2,1)}, bf16[2,64,2048]{2,1,0:T(8,128)(2,1)S(1)}, u32[]{:S(2)}, u32[]{:S(2)}) collective-permute-start(bf16[2,64,2048]{2,1,0:T(8,128)(2,1)} %add_convert_fusion.7), channel_id=1, source_target_pairs={{0,2},{1,3},{2,0},{3,1},{4,6},{5,7},{6,4},{7,5},{8,10},{9,11},{10,... | collective-permute-start | bytes 1572872 | tf_op jit(solution)/shard_map/ppermute | solution.py:177
  382.7 24.2 %shard_map.297 = (bf16[2,256,1408]{2,1,0:T(8,128)(2,1)}, bf16[2,256,1408]{2,1,0:T(8,128)(2,1)}, bf16[2,256,1408]{2,1,0:T(8,128)(2,1)}, bf16[2,256,2048]{2,1,0:T(...) custom-call(s32[5]{0:T(128)} %pad_add_fusion.2.order_ref, ...), custom_call_target="tpu_custom_call" | custom-call | flops 30000001024 | bytes 1000 | tf_op jit(solution)/shard_map/pallas_call | solution.py:847
  424.4 9.3 %shard_map.299 = bf16[1408,2048]{1,0:T(8,128)(2,1)} custom-call(bf16[512,1408]{1,0:T(8,128)(2,1)S(1)} %bitcast.290, bf16[512,2048]{1,0:T(8,128)(2,1)S(1)} %bitcast.295, bf16[512,1408]{1,0:T(8,128)(2,1)S(1)} %bitcast.291, bf16[512,2048]{1,0:T(8,128)(2,1)} %bitcast.338), custom_call_target="tpu_custom_call" | custom-call | flops 1000 | bytes 1000 | tf_op jit(solution)/shard_map/pallas_call | solution.py:892
  435.8 10.2 %collective-permute-done.50.refs_2_ = bf16[2,64,2048]{2,1,0:T(8,128)(2,1)} collective-permute-done((bf16[2,64,2048]{2,1,0:T(8,128)(2,1)}, bf16[2,64,2048]{2,1,0:T(8,128)(2,1)}, u32[]{:S(2)}, u32[]{:S(2)}) %collective-permute-start.50) | collective-permute-done | bytes 524320 | tf_op jit(solution)/shard_map/ppermute | solution.py:117
  448.9 13.1 %collective-permute-start.56 = (bf16[2,64,2048]{2,1,0:T(8,128)(2,1)}, bf16[2,64,2048]{2,1,0:T(8,128)(2,1)}, u32[]{:S(2)}, u32[]{:S(2)}) collective-permute-start(bf16[2,64,2048]{2,1,0:T(8,128)(2,1)} %add_convert_fusion.6), channel_id=1, source_target_pairs={{0,2},{1,3},{2,0},{3,1},{4,6},{5,7},{6,4},{7,5},{8,10},{9,11},{10,... | collective-permute-start | bytes 1572872 | tf_op jit(solution)/shard_map/ppermute | solution.py:177
  467.1 9.8 %shard_map.300 = bf16[2048,1408]{1,0:T(8,128)(2,1)} custom-call(bf16[512,2048]{1,0:T(8,128)(2,1)S(1)} %bitcast.286, bf16[512,1408]{1,0:T(8,128)(2,1)S(1)} %bitcast.312, bf16[512,2048]{1,0:T(8,128)(2,1)} %bitcast.335, bf16[512,1408]{1,0:T(8,128)(2,1)S(1)} %bitcast.314), custom_call_target="tpu_custom_call" | custom-call | flops 1000 | bytes 1000 | tf_op jit(solution)/shard_map/pallas_call | solution.py:892
  481.6 9.7 %shard_map.301 = bf16[2048,1408]{1,0:T(8,128)(2,1)} custom-call(bf16[512,2048]{1,0:T(8,128)(2,1)S(1)} %bitcast.287, bf16[512,1408]{1,0:T(8,128)(2,1)S(1)} %bitcast.311, bf16[512,2048]{1,0:T(8,128)(2,1)} %bitcast.336, bf16[512,1408]{1,0:T(8,128)(2,1)S(1)} %bitcast.313), custom_call_target="tpu_custom_call" | custom-call | flops 1000 | bytes 1000 | tf_op jit(solution)/shard_map/pallas_call | solution.py:892
  496.8 8.5 %shard_map.302 = bf16[4,256,2048]{2,1,0:T(8,128)(2,1)S(1)} custom-call(s32[5]{0:T(128)S(1)} %copy-done.91, bf16[2,256,1408]{2,1,0:T(8,128)(2,1)S(1)} %copy-done.10, bf16[2,256,1408]{2,1,0:T(8,128)(2,1)S(1)} %copy-done.12, bf16[1408,2048]{1,0:T(8,128)(2,1)S(1)} %copy-done.13), custom_call_target="tpu_custom_call" | custom-call | flops 1000 | bytes 1000 | tf_op jit(solution)/shard_map/pallas_call | solution.py:996
  536.4 32.1 %shard_map.305 = (bf16[16,192,256]{2,1,0:T(8,128)(2,1)S(1)}, f32[192,1]{1,0:T(8,128)S(1)}) custom-call(s32[16]{0:T(128)S(1)} %scatter_custom_fusion.place_ref, s32[8]{0:T(128)S(1)} %iota.57.tiles_ref, s32[1,512]{1,0:T(1,128)S(1)} %bitcast.333, s32[512,1]{1,0:T(8,128)S(1)} %bitcast.328, bf16[16,192,256]{2,1,0:T(8,128)(2,1)S(1)} %bitcast.303, ...), custom_call_target="tpu_custom_call" | custom-call | flops 30000001024 | bytes 1000 | tf_op jit(solution)/shard_map/pallas_call | solution.py:768
  592.3 32.1 %shard_map.308 = (bf16[16,192,256]{2,1,0:T(8,128)(2,1)S(1)}, f32[192,1]{1,0:T(8,128)S(1)}) custom-call(s32[16]{0:T(128)S(1)} %scatter_custom_fusion.place_ref, s32[8]{0:T(128)S(1)} %iota.58.tiles_ref, s32[1,512]{1,0:T(1,128)S(1)} %bitcast.334, s32[512,1]{1,0:T(8,128)S(1)} %bitcast.329, bf16[16,192,256]{2,1,0:T(8,128)(2,1)S(1)} %bitcast.301, ...), custom_call_target="tpu_custom_call" | custom-call | flops 30000001024 | bytes 1000 | tf_op jit(solution)/shard_map/pallas_call | solution.py:768
  645.1 9.4 %collective-permute-start.77 = (bf16[2,64,2048]{2,1,0:T(8,128)(2,1)}, bf16[2,64,2048]{2,1,0:T(8,128)(2,1)S(1)}, u32[]{:S(2)}, u32[]{:S(2)}) collective-permute-start(bf16[2,64,2048]{2,1,0:T(8,128)(2,1)} %get-tuple-element.565), channel_id=1, source_target_pairs={{0,1},{3,2},{4,5},{7,6},{8,9},{11,10},{12,13},{15,14},{16,17},{19,... | collective-permute-start | bytes 1572872 | tf_op jit(solution)/shard_map/ppermute | solution.py:162
  687.9 10.4 %shard_map.311 = (bf16[4,256,1536]{2,1,0:T(8,128)(2,1)}, bf16[4,256,1536]{2,1,0:T(8,128)(2,1)}) custom-call(s32[2]{0:T(128)S(1)} %pad_add_fusion.3.at_ref, bf16[512,2048]{1,0:T(8,128)(2,1)S(1)} %bitcast.299, bf16[512,1536]{1,0:T(8,128)(2,1)S(1)} %bitcast.309, bf16[512,2048]{1,0:T(8,128)(2,1)} %bitcast.340, bf16[512,1536]{1,0:T(8,128)(2,1)S(1)} %bitcast.310), custom_call_target="tpu_custom_call" | custom-call | flops 1000 | bytes 1000 | tf_op jit(solution)/shard_map/pallas_call | solution.py:944
  699.3 20.1 %collective-permute-done.79.refs_1_ = bf16[2,64,2048]{2,1,0:T(8,128)(2,1)S(1)} collective-permute-done((bf16[2,64,2048]{2,1,0:T(8,128)(2,1)S(1)}, bf16[2,64,2048]{2,1,0:T(8,128)(2,1)S(1)}, u32[]{:S(2)}, u32[]{:S(2)}) %collective-permute-start.79) | collective-permute-done | bytes 524320 | tf_op jit(solution)/shard_map/ppermute | solution.py:177
  747.4 35.2 %reduce-scatter.12.cloned.1.call-done = bf16[512,256]{1,0:T(8,128)(2,1)} async-done(((bf16[512,2048]{1,0:T(8,128)(2,1)}), bf16[512,256]{1,0:T(8,128)(2,1)}) %reduce-scatter.12.cloned.1.call-update) | async-done | bytes 262160 | tf_op jit(solution)/shard_map/reduce_scatter | solution.py:194
  (681 shorter events, 372.8 us)
Async XLA Ops:
  7.2 57.9 %all-gather.8.cloned.1.call-start = ((), (), s32[]{:S(2)}) async-start(), calls=%async_computation.5 | async-start | bytes 7077888 | tf_op jit(solution)/shard_map/all_gather | solution.py:190
  9.4 163.2 %all-gather.10.cloned.1.call-start = ((), (), s32[]{:S(2)}) async-start(), calls=%async_computation.6 | async-start | bytes 2359296 | tf_op jit(solution)/shard_map/all_gather | solution.py:190
  20.2 298.8 %all-gather.18.cloned.1.call-start = ((), (), s32[]{:S(2)}) async-start(), calls=%async_computation.15 | async-start | bytes 5242880 | tf_op jit(solution)/shard_map/all_gather | solution.py:1139
  100.3 218.7 %all-gather.12.cloned.1.call-start = ((), (), s32[]{:S(2)}) async-start(), calls=%async_computation.7 | async-start | bytes 6488064 | tf_op jit(solution)/shard_map/all_gather | solution.py:190
  125.1 193.9 %all-gather.14.cloned.1.call-start = ((), (), s32[]{:S(2)}) async-start(), calls=%async_computation.8 | async-start | bytes 6488064 | tf_op jit(solution)/shard_map/all_gather | solution.py:190
  125.7 197.0 %all-gather.16.cloned.1.call-start = ((), (), s32[]{:S(2)}) async-start(), calls=%async_computation.9 | async-start | bytes 6488064 | tf_op jit(solution)/shard_map/all_gather | solution.py:190
  130.2 499.6 %reduce-scatter.6.cloned.1.call-start = ((), (), s32[]{:S(2)}) async-start(), calls=%async_computation.10 | async-start | bytes 6488064 | tf_op jit(solution)/shard_map/reduce_scatter | solution.py:194
  273.0 40.6 %collective-permute-start.40 = (bf16[2,64,2048]{2,1,0:T(8,128)(2,1)S(1)}, bf16[2,64,2048]{2,1,0:T(8,128)(2,1)S(1)}, u32[]{:S(2)}, u32[]{:S(2)}) collective-permute-start(bf16[2,64,2048]{2,1,0:T(8,128)(2,1)S(1)} %add_convert_fusion.8), channel_id=1, source_target_pairs={{0,2},{1,3},{2,0},{3,1},{4,6},{5,7},{6,4},{7,5},{8,10},{9,11},{10,... | collective-permute-start | bytes 1572872 | tf_op jit(solution)/shard_map/ppermute | solution.py:177
  446.1 183.7 %reduce-scatter.8.cloned.1.call-start = ((), (), s32[]{:S(2)}) async-start(), calls=%async_computation.11 | async-start | bytes 6488064 | tf_op jit(solution)/shard_map/reduce_scatter | solution.py:194
  446.1 61.2 %collective-permute-start.54 = (bf16[2,64,2048]{2,1,0:T(8,128)(2,1)}, bf16[2,64,2048]{2,1,0:T(8,128)(2,1)}, u32[]{:S(2)}, u32[]{:S(2)}) collective-permute-start(bf16[2,64,2048]{2,1,0:T(8,128)(2,1)} %collective-permute-done.50.refs_2_), channel_id=1, source_target_pairs={{1,0},{2,3},{5,4},{6,7},{9,8},{10,11},{13,12},{14,15},{17,16},{18,... | collective-permute-start | bytes 1572872 | tf_op jit(solution)/shard_map/ppermute | solution.py:128
  447.4 59.9 %collective-permute-start.55 = (bf16[2,64,2048]{2,1,0:T(8,128)(2,1)}, bf16[2,64,2048]{2,1,0:T(8,128)(2,1)}, u32[]{:S(2)}, u32[]{:S(2)}) collective-permute-start(bf16[2,64,2048]{2,1,0:T(8,128)(2,1)} %get-tuple-element.510.refs_0_), channel_id=1, source_target_pairs={{1,2},{2,1},{5,6},{6,5},{9,10},{10,9},{13,14},{14,13},{17,18},{18,... | collective-permute-start | bytes 1572872 | tf_op jit(solution)/shard_map/ppermute | solution.py:129
  448.9 58.4 %collective-permute-start.56 = (bf16[2,64,2048]{2,1,0:T(8,128)(2,1)}, bf16[2,64,2048]{2,1,0:T(8,128)(2,1)}, u32[]{:S(2)}, u32[]{:S(2)}) collective-permute-start(bf16[2,64,2048]{2,1,0:T(8,128)(2,1)} %add_convert_fusion.6), channel_id=1, source_target_pairs={{0,2},{1,3},{2,0},{3,1},{4,6},{5,7},{6,4},{7,5},{8,10},{9,11},{10,... | collective-permute-start | bytes 1572872 | tf_op jit(solution)/shard_map/ppermute | solution.py:177
  462.0 45.3 %collective-permute-start.57 = (bf16[2,64,2048]{2,1,0:T(8,128)(2,1)}, bf16[2,64,2048]{2,1,0:T(8,128)(2,1)}, u32[]{:S(2)}, u32[]{:S(2)}) collective-permute-start(bf16[2,64,2048]{2,1,0:T(8,128)(2,1)} %get-tuple-element.483), channel_id=1, source_target_pairs={{0,1},{1,0},{2,3},{3,2},{4,5},{5,4},{6,7},{7,6},{8,9},{9,8},{10,11... | collective-permute-start | bytes 1572872 | tf_op jit(solution)/shard_map/ppermute | solution.py:177
  507.4 158.9 %reduce-scatter.10.cloned.1.call-start = ((), (), s32[]{:S(2)}) async-start(), calls=%async_computation.12 | async-start | bytes 5242880 | tf_op jit(solution)/shard_map/reduce_scatter | solution.py:1213
  525.6 42.9 %collective-permute-start.58 = (bf16[2,64,2048]{2,1,0:T(8,128)(2,1)}, bf16[2,64,2048]{2,1,0:T(8,128)(2,1)}, u32[]{:S(2)}, u32[]{:S(2)}) collective-permute-start(bf16[2,64,2048]{2,1,0:T(8,128)(2,1)} %get-tuple-element.525.refs_0_), channel_id=1, source_target_pairs={{0,1},{1,0},{2,3},{3,2},{4,5},{5,4},{6,7},{7,6},{8,9},{9,8},{10,11... | collective-permute-start | bytes 1572872 | tf_op jit(solution)/shard_map/ppermute | solution.py:138
  527.6 40.9 %collective-permute-start.59 = (bf16[2,64,2048]{2,1,0:T(8,128)(2,1)}, bf16[2,64,2048]{2,1,0:T(8,128)(2,1)}, u32[]{:S(2)}, u32[]{:S(2)}) collective-permute-start(bf16[2,64,2048]{2,1,0:T(8,128)(2,1)} %get-tuple-element.525.refs_0_), channel_id=1, source_target_pairs={{0,2},{1,3},{2,0},{3,1},{4,6},{5,7},{6,4},{7,5},{8,10},{9,11},{10,... | collective-permute-start | bytes 1572872 | tf_op jit(solution)/shard_map/ppermute | solution.py:136
  528.4 40.1 %collective-permute-start.60 = (bf16[2,64,2048]{2,1,0:T(8,128)(2,1)}, bf16[2,64,2048]{2,1,0:T(8,128)(2,1)}, u32[]{:S(2)}, u32[]{:S(2)}) collective-permute-start(bf16[2,64,2048]{2,1,0:T(8,128)(2,1)} %get-tuple-element.525.refs_0_), channel_id=1, source_target_pairs={{0,3},{1,2},{2,1},{3,0},{4,7},{5,6},{6,5},{7,4},{8,11},{9,10},{10,... | collective-permute-start | bytes 1572872 | tf_op jit(solution)/shard_map/ppermute | solution.py:137
  531.0 214.1 %reduce-scatter.14.cloned.1.call-start = ((), (), s32[]{:S(2)}) async-start(), calls=%async_computation.14 | async-start | bytes 6488064 | tf_op jit(solution)/shard_map/reduce_scatter | solution.py:194
  625.6 156.9 %reduce-scatter.12.cloned.1.call-start = ((), (), s32[]{:S(2)}) async-start(), calls=%async_computation.13 | async-start | bytes 2359296 | tf_op jit(solution)/shard_map/reduce_scatter | solution.py:194
  730.1 52.5 %collective-permute-start.83 = (bf16[2,64,2048]{2,1,0:T(8,128)(2,1)}, bf16[2,64,2048]{2,1,0:T(8,128)(2,1)}, u32[]{:S(2)}, u32[]{:S(2)}) collective-permute-start(bf16[2,64,2048]{2,1,0:T(8,128)(2,1)} %add_convert_fusion.4), channel_id=1, source_target_pairs={{0,2},{1,3},{2,0},{3,1},{4,6},{5,7},{6,4},{7,5},{8,10},{9,11},{10,... | collective-permute-start | bytes 1572872 | tf_op jit(solution)/shard_map/ppermute | solution.py:177
  730.1 52.5 %collective-permute-start.84 = (bf16[2,64,2048]{2,1,0:T(8,128)(2,1)}, bf16[2,64,2048]{2,1,0:T(8,128)(2,1)}, u32[]{:S(2)}, u32[]{:S(2)}) collective-permute-start(bf16[2,64,2048]{2,1,0:T(8,128)(2,1)} %get-tuple-element.595), channel_id=1, source_target_pairs={{0,1},{1,0},{2,3},{3,2},{4,5},{5,4},{6,7},{7,6},{8,9},{9,8},{10,11... | collective-permute-start | bytes 1572872 | tf_op jit(solution)/shard_map/ppermute | solution.py:177
  736.8 45.7 %collective-permute-start.89 = (bf16[256,1536]{1,0:T(8,128)(2,1)}, bf16[256,1536]{1,0:T(8,128)(2,1)}, u32[]{:S(2)}, u32[]{:S(2)}) collective-permute-start(bf16[256,1536]{1,0:T(8,128)(2,1)} %get-tuple-element.686), channel_id=1, source_target_pairs={{0,8},{8,0},{16,24},{24,16},{1,9},{9,1},{17,25},{25,17},{2,10},{10... | collective-permute-start | bytes 2359304 | tf_op jit(solution)/shard_map/ppermute | solution.py:34
  738.4 44.2 %collective-permute-start.90 = (bf16[256,1536]{1,0:T(8,128)(2,1)}, bf16[256,1536]{1,0:T(8,128)(2,1)}, u32[]{:S(2)}, u32[]{:S(2)}) collective-permute-start(bf16[256,1536]{1,0:T(8,128)(2,1)} %get-tuple-element.685), channel_id=1, source_target_pairs={{0,16},{8,24},{16,0},{24,8},{1,17},{9,25},{17,1},{25,9},{2,18},{10... | collective-permute-start | bytes 2359304 | tf_op jit(solution)/shard_map/ppermute | solution.py:34
  740.3 42.3 %collective-permute-start.91 = (bf16[256,1536]{1,0:T(8,128)(2,1)}, bf16[256,1536]{1,0:T(8,128)(2,1)}, u32[]{:S(2)}, u32[]{:S(2)}) collective-permute-start(bf16[256,1536]{1,0:T(8,128)(2,1)} %get-tuple-element.684), channel_id=1, source_target_pairs={{0,24},{8,16},{16,8},{24,0},{1,25},{9,17},{17,9},{25,1},{2,26},{10... | collective-permute-start | bytes 2359304 | tf_op jit(solution)/shard_map/ppermute | solution.py:34
  (211 other events, 2612.7 us)
Sparse Core Ops, SparseCore 0:
  10.5 48.5 all-gather.7
  61.0 28.1 all-gather.9
  100.4 81.7 all-gather.17
  184.0 47.4 all-gather.11
  233.2 43.3 all-gather.13
  278.3 44.3 all-gather.15
  446.2 66.6 reduce-scatter.5
  516.7 59.0 reduce-scatter.7
  578.1 76.7 reduce-scatter.9
  658.5 59.6 reduce-scatter.13
  721.7 60.8 reduce-scatter.11
